TPU v7x, 32 devices: a whole 2x2x4 slice. The times are simulated.
32 devices in a mesh: wide: 8 (over z, y), narrow: 4 (over x, core).
Axes of the slice: x: 2, y: 2, z: 4, core: 2. Of those that a mesh axis runs over, the one named last changes fastest.
Arguments:
- quantized_inputs: bfloat16 [16384, 3072], P(('wide', 'narrow')), may hold values from -6 to 6
- x_full: bfloat16 [16384, 3072], P(('wide', 'narrow')), may hold values from -6 to 6
Outputs:
- gram_out: float32 [8, 4, 512, 16384], P(None, 'narrow', None, 'wide')
- cross_gram_result: float32 [8, 4, 512, 16384], P(None, 'narrow', None, 'wide')
All inputs are finite; a program needn't handle non-finite values.
Results may differ from a plain program's by a relative error of at most 0.003.
Values may be sent and summed in bfloat16 or wider, within the bound.
No kernel may reach another device: no remote copies, remote signals or barrier semaphores. Data moves between devices by JAX's collectives and lax.ppermute only.
A program may use at most 256 MiB of HBM per device.

v0:
```python
import jax
import jax.numpy as jnp
from jax import lax
from jax.sharding import PartitionSpec as P


def fetch_left(stacked_parts):
    return lax.all_gather(stacked_parts, "wide", axis=1, tiled=True)


def load_right_operand(quantized_inputs):
    return lax.all_gather(quantized_inputs, "narrow", axis=0, tiled=True)


def per_device(quantized_inputs, x_full):
    token_count = quantized_inputs.shape[1]
    owned_rows = quantized_inputs.shape[0]
    difference = (x_full.astype(jnp.float32) - quantized_inputs.astype(jnp.float32)).astype(
        jnp.bfloat16
    )
    stacked_parts = jnp.stack([quantized_inputs, difference])
    left_operand_block = fetch_left(stacked_parts)
    reduced_sum = jnp.einsum(
        "yia,ea->yie",
        left_operand_block,
        load_right_operand(quantized_inputs),
        preferred_element_type=jnp.float32,
    )
    tile_pairs = reduced_sum / token_count
    wide_count = lax.axis_size("wide")
    gram_out = tile_pairs[0].reshape(wide_count, 1, owned_rows, tile_pairs.shape[2])
    cross_gram_result = tile_pairs[1].reshape(wide_count, 1, owned_rows, tile_pairs.shape[2])
    return (gram_out, cross_gram_result)


def solution(mesh):
    return jax.shard_map(
        per_device,
        mesh=mesh,
        in_specs=(P(("wide", "narrow"), None), P(("wide", "narrow"), None)),
        out_specs=(P(None, "narrow", None, "wide"), P(None, "narrow", None, "wide")),
        check_vma=False,
    )
```

profile of v0, /device:TPU:0, one launch (start us, length us, event | category | flops | bytes accessed | tf_op | source)
XLA Modules:
  0.0 1213.0 jit_solution(622001512019671239)
XLA Ops:
  7.2 0.0 copy-start
  7.2 0.0 all-gather.5.cloned.1.call-start
  7.2 0.7 all-gather.5.cloned.1.call-update
  7.9 0.0 all-gather.3.cloned.1.call-start
  8.0 4.1 fusion.1
  12.1 0.0 copy-done
  12.1 3.2 pad_maximum_fusion
  15.3 0.0 all-gather.3.cloned.1.call-update
  15.4 79.0 %all-gather.5.cloned.1.call-done = bf16[2048,3072]{1,0:T(8,128)(2,1)} async-done(((bf16[512,3072]{1,0:T(8,128)(2,1)}), bf16[2048,3072]{1,0:T(8,128)(2,1)}) %all-gather.5.cloned.1.call-update) | async-done | bytes 12582928 | tf_op jit(solution)/shard_map/all_gather | solution.py:12
  94.4 954.5 %all-gather.3.cloned.1.call-done = bf16[2,4096,3072]{2,1,0:T(8,128)(2,1)} async-done(((bf16[2,512,3072]{2,1,0:T(8,128)(2,1)}), bf16[2,4096,3072]{2,1,0:T(8,128)(2,1)}) %all-gather.3.cloned.1.call-update) | async-done | bytes 50331664 | tf_op jit(solution)/shard_map/all_gather | solution.py:8
  1048.9 115.2 %broadcast_multiply_fusion = f32[2,4096,2048]{2,1,0:T(8,128)} fusion(bf16[2,4096,3072]{2,1,0:T(8,128)(2,1)} %all-gather.3.cloned.1.call-done, bf16[2048,3072]{1,0:T(8,128)(2,1)} %all-gather.5.cloned.1.call-done), kind=kOutput, calls=%fused_computation | convolution fusion | flops 103095992320 | bytes 130023424 | tf_op jit(solution)/shard_map/yia,ea->yie/dot_general | solution.py:23
  1164.1 42.1 %fusion.2 = (f32[1,4096,2048]{2,1,0:T(8,128)}, f32[1,4096,2048]{2,1,0:T(8,128)}) fusion(f32[2,4096,2048]{2,1,0:T(8,128)} %broadcast_multiply_fusion), kind=kLoop, calls=%fused_computation.5 | loop fusion | bytes 134217728 | tf_op jit(solution)/shard_map/slice | solution.py:32
Async XLA Ops:
  7.2 4.9 copy-start
  7.2 87.2 %all-gather.5.cloned.1.call-start = ((), (), s32[]{:S(2)}) async-start(), calls=%async_computation.1 | async-start | bytes 15728640 | tf_op jit(solution)/shard_map/all_gather | solution.py:12
  7.9 1041.0 %all-gather.3.cloned.1.call-start = ((), (), s32[]{:S(2)}) async-start(), calls=%async_computation | async-start | bytes 56623104 | tf_op jit(solution)/shard_map/all_gather | solution.py:8
Sparse Core Ops, SparseCore 0:
  9.6 84.7 all-gather.4
  96.5 952.3 all-gather.2
where the time goes:
time: 1210 us
  waiting for transfers between devices  1030 us (85%)
  matrix products  115 us (10%)
  local copies, waits for them, and re-layouts  42.1 us (3%)
  between operations  14.1 us (1%)
    all_gather x1, waiting for transfers between devices, fetch_left(): return lax.all_gather(stacked_parts, 'wide', axis=1, tiled=True)  954 us
    dot_general x1, matrix products, per_device(): jnp.einsum('yia,ea->yie', left_operand_block, load_right_operand(quantize...  115 us
    all_gather x1, waiting for transfers between devices, load_right_operand(): return lax.all_gather(quantized_inputs, 'narrow', axis=0, tiled=True)  79 us
    slice x1, local copies, waits for them, and re-layouts, per_device(): tile_pairs[1].reshape(wide_count, 1, owned_rows, tile_pairs.shape[2])  42.1 us
  transfers between devices with their start and end apart: 2, of which 2 were waited for; matrix products, arithmetic and copies ran while one was open for 1% of the time, Pallas kernels for 0%

commit v1 on v0

v1 whole, which is shorter than its diff:
```python
import jax
import jax.numpy as jnp
from jax import lax
from jax.sharding import PartitionSpec as P


def ring_order(count):
    return [i for i in range(0, count, 2)] + [i for i in reversed(range(1, count, 2))]


def per_device(quantized_inputs, x_full):
    token_count = quantized_inputs.shape[1]
    owned_rows = quantized_inputs.shape[0]
    wide_count = lax.axis_size("wide")
    order = ring_order(wide_count)
    forward = [(order[i], order[(i + 1) % wide_count]) for i in range(wide_count)]
    backward = [(b, a) for a, b in forward]
    place = [0] * wide_count
    for i, w in enumerate(order):
        place[w] = i
    me = jnp.asarray(place, jnp.int32)[lax.axis_index("wide")]
    order_table = jnp.asarray(order, jnp.int32)

    difference = (x_full.astype(jnp.float32) - quantized_inputs.astype(jnp.float32)).astype(
        jnp.bfloat16
    )
    right = lax.all_gather(quantized_inputs, "narrow", axis=0, tiled=True)
    columns = right.shape[0]

    far, near = wide_count // 2, (wide_count - 1) // 2
    quantized_at = {0: quantized_inputs}
    difference_at = {0: difference}
    fq, fd, bq, bd = quantized_inputs, difference, quantized_inputs, difference
    for step in range(1, far + 1):
        fq = lax.ppermute(fq, "wide", forward)
        quantized_at[step] = fq
        bd = lax.ppermute(bd, "wide", backward)
        difference_at[wide_count - step] = bd
        if step <= near:
            bq = lax.ppermute(bq, "wide", backward)
            quantized_at[wide_count - step] = bq
            fd = lax.ppermute(fd, "wide", forward)
            difference_at[step] = fd

    gram_out = jnp.zeros((wide_count, 1, owned_rows, columns), jnp.float32)
    cross_gram_result = jnp.zeros((wide_count, 1, owned_rows, columns), jnp.float32)

    def statistic(left):
        product = jnp.einsum("ia,ea->ie", left, right, preferred_element_type=jnp.float32)
        return (product / token_count)[None, None]

    offsets = [0]
    for step in range(1, far + 1):
        offsets += [step] if wide_count - step == step else [step, wide_count - step]
    for offset in offsets:
        owner = order_table[(me - offset + wide_count) % wide_count]
        gram_out = lax.dynamic_update_slice(
            gram_out, statistic(quantized_at[offset]), (owner, 0, 0, 0)
        )
        cross_gram_result = lax.dynamic_update_slice(
            cross_gram_result, statistic(difference_at[offset]), (owner, 0, 0, 0)
        )
    return (gram_out, cross_gram_result)


def solution(mesh):
    return jax.shard_map(
        per_device,
        mesh=mesh,
        in_specs=(P(("wide", "narrow"), None), P(("wide", "narrow"), None)),
        out_specs=(P(None, "narrow", None, "wide"), P(None, "narrow", None, "wide")),
        check_vma=False,
    )
```

time: 1210 us -> 550 us (0.45)
  waiting for transfers between devices: 1030 us -> 307 us
  matrix products: 115 us -> 156 us
  between operations: 14.1 us -> 35 us
  starting transfers between devices: 0.08 us -> 15.8 us
  local copies, waits for them, and re-layouts: 42.1 us -> 29.6 us
    all_gather x2 -> x1, waiting for transfers between devices: 1030 us -> 0.01 us  [per_device(): right = lax.all_gather(quantized_inputs, 'narrow', axis=0, tiled=True)]
    ppermute x0 -> x14, waiting for transfers between devices: none -> 307 us  [the longest x4 194 us: per_device(): bd = lax.ppermute(bd, 'wide', backward)]
    slice x1 -> x0, local copies, waits for them, and re-layouts: 42.1 us -> none  [per_device(): tile_pairs[1].reshape(wide_count, 1, owned_rows, tile_pairs.shape[2])]
    dot_general x1 -> x16, matrix products: 115 us -> 156 us  [statistic(): jnp.einsum('ia,ea->ie', left, right, preferred_element_type=jnp.float32)]
    another operation x0 -> x2, local copies, waits for them, and re-layouts: none -> 27.1 us
    ppermute x0 -> x14, starting transfers between devices: none -> 15.8 us  [the longest x4 9.02 us: per_device(): bd = lax.ppermute(bd, 'wide', backward)]
  transfers between devices with their start and end apart: 2 -> 15, of which waited for: 2 -> 5; matrix products, arithmetic and copies ran while one was open for 1% -> 32% of each run, Pallas kernels for 0% -> 0%
where the time goes in v1:
time: 550 us; the launch traced here: 547 us
  waiting for transfers between devices  307 us (56%)
  matrix products  156 us (28%)
  between operations  35 us (6%)
  local copies, waits for them, and re-layouts  29.6 us (5%)
  starting transfers between devices  15.8 us (3%)
    ppermute x4, waiting for transfers between devices, per_device(): bd = lax.ppermute(bd, 'wide', backward)  194 us
    dot_general x16, matrix products, statistic(): jnp.einsum('ia,ea->ie', left, right, preferred_element_type=jnp.float32)  156 us
    ppermute x3, waiting for transfers between devices, per_device(): fd = lax.ppermute(fd, 'wide', forward)  113 us
    another operation x2, local copies, waits for them, and re-layouts  27.1 us
  transfers between devices with their start and end apart: 15, of which 5 were waited for; matrix products, arithmetic and copies ran while one was open for 32% of the time, Pallas kernels for 0%

profile of v1, /device:TPU:0, one launch (start us, length us, event | category | flops | bytes accessed | tf_op | source)
XLA Modules:
  0.0 546.6 jit_solution(4564395568211351658)
XLA Ops:
  7.2 0.0 copy-start
  7.2 0.0 all-gather.2.cloned.1.call-start
  7.2 0.7 all-gather.2.cloned.1.call-update
  7.9 1.1 copy-done
  9.1 0.0 copy-start.9
  9.1 3.0 subtract_convert_fusion
  12.1 0.0 copy-start.1
  12.1 3.0 collective-permute-start.8
  15.1 0.1 collective-permute-start
  15.3 2.0 collective-permute-start.7
  17.2 0.1 collective-permute-start.1
  17.3 66.8 %collective-permute-done.8 = bf16[512,3072]{1,0:T(8,128)(2,1)S(1)} collective-permute-done((bf16[512,3072]{1,0:T(8,128)(2,1)S(1)}, bf16[512,3072]{1,0:T(8,128)(2,1)S(1)}, u32[]{:S(2)}, u32[]{:S(2)}) %collective-permute-start.8) | collective-permute-done | bytes 3145760 | tf_op jit(solution)/shard_map/ppermute | solution.py:37
  84.1 2.0 collective-permute-start.10
  86.1 0.0 collective-permute-done
  86.2 0.1 collective-permute-start.2
  86.3 67.4 %collective-permute-done.7 = bf16[512,3072]{1,0:T(8,128)(2,1)} collective-permute-done((bf16[512,3072]{1,0:T(8,128)(2,1)S(1)}, bf16[512,3072]{1,0:T(8,128)(2,1)}, u32[]{:S(2)}, u32[]{:S(2)}) %collective-permute-start.7) | collective-permute-done | bytes 3145760 | tf_op jit(solution)/shard_map/ppermute | solution.py:42
  153.7 0.1 collective-permute-start.9
  153.8 0.0 collective-permute-done.1
  153.8 0.0 copy-done.1
  153.8 1.9 collective-permute-start.3
  155.7 0.0 copy-done.5
  155.7 63.3 %collective-permute-done.10 = bf16[512,3072]{1,0:T(8,128)(2,1)} collective-permute-done((bf16[512,3072]{1,0:T(8,128)(2,1)S(1)}, bf16[512,3072]{1,0:T(8,128)(2,1)}, u32[]{:S(2)}, u32[]{:S(2)}) %collective-permute-start.10) | collective-permute-done | bytes 3145760 | tf_op jit(solution)/shard_map/ppermute | solution.py:37
  219.1 0.0 copy-done.7
  219.1 2.0 collective-permute-start.12
  221.1 0.0 collective-permute-done.2
  221.1 0.1 collective-permute-start.4
  221.2 0.0 copy-done.9
  221.2 0.6 dynamic_slice.27
  227.1 0.0 copy-done.3
  227.1 0.7 fusion
  243.1 45.4 %collective-permute-done.9 = bf16[512,3072]{1,0:T(8,128)(2,1)} collective-permute-done((bf16[512,3072]{1,0:T(8,128)(2,1)}, bf16[512,3072]{1,0:T(8,128)(2,1)}, u32[]{:S(2)}, u32[]{:S(2)}) %collective-permute-start.9) | collective-permute-done | bytes 3145760 | tf_op jit(solution)/shard_map/ppermute | solution.py:42
  288.5 0.1 collective-permute-start.11
  288.6 0.0 collective-permute-done.3
  288.6 1.9 collective-permute-start.5
  290.5 63.3 %collective-permute-done.12 = bf16[512,3072]{1,0:T(8,128)(2,1)} collective-permute-done((bf16[512,3072]{1,0:T(8,128)(2,1)}, bf16[512,3072]{1,0:T(8,128)(2,1)}, u32[]{:S(2)}, u32[]{:S(2)}) %collective-permute-start.12) | collective-permute-done | bytes 3145760 | tf_op jit(solution)/shard_map/ppermute | solution.py:37
  353.9 2.0 collective-permute-start.13
  355.9 0.0 collective-permute-done.4
  355.9 0.4 collective-permute-start.6
  356.3 15.6 %broadcast.30.clone.1 = f32[8,1,512,2048]{3,2,1,0:T(8,128)} broadcast(f32[]{:T(128)} %constant.94.clone.1), dimensions={} | broadcast | bytes 33554436 | tf_op jit(solution)/shard_map/broadcast.3
  371.9 0.0 copy-done.2
  371.9 0.0 copy-done.4
  371.9 8.3 %bitcast_dynamic-update-slice_fusion.7 = f32[8,1,512,2048]{3,2,1,0:T(8,128)} fusion(f32[8,1,512,2048]{3,2,1,0:T(8,128)} %broadcast.30.clone.1, s32[]{:T(128)S(6)} %select_n.97, bf16[512,3072]{1,0:T(8,128)(2,1)S(1)} %copy-done.2, bf16[2048,3072]{1,0:T(8,128)(2,1)S(1)} %copy-done.4), kind=kOutput, calls=%fused_computation.8 | convolution fusion | flops 6443499520 | bytes 19922948 | tf_op jit(solution)/shard_map/ia,ea->ie/dot_general | solution.py:49
  380.2 11.5 %broadcast.30.clone = f32[8,1,512,2048]{3,2,1,0:T(8,128)} broadcast(f32[]{:T(128)} %constant.94.clone.1), dimensions={} | broadcast | bytes 33554436 | tf_op jit(solution)/shard_map/broadcast.3
  391.7 8.6 %bitcast_dynamic-update-slice_fusion.15 = f32[8,1,512,2048]{3,2,1,0:T(8,128)} fusion(f32[8,1,512,2048]{3,2,1,0:T(8,128)} %broadcast.30.clone, s32[]{:T(128)S(6)} %select_n.97, bf16[512,3072]{1,0:T(8,128)(2,1)S(1)} %copy-done, bf16[2048,3072]{1,0:T(8,128)(2,1)S(1)} %copy-done.4), kind=kOutput, calls=%fused_computation.16 | convolution fusion | flops 6443499520 | bytes 19922948 | tf_op jit(solution)/shard_map/ia,ea->ie/dot_general | solution.py:49
  400.3 10.2 %bitcast_dynamic-update-slice_fusion.6 = f32[8,1,512,2048]{3,2,1,0:T(8,128)} fusion(f32[8,1,512,2048]{3,2,1,0:T(8,128)} %bitcast_dynamic-update-slice_fusion.7, s32[]{:T(128)S(6)} %select_n.100, bf16[512,3072]{1,0:T(8,128)(2,1)} %collective-permute-done.7, bf16[2048,3072]{1,0:T(8,128)(2,1)S(1)} %copy-done.4), kind=kOutput, calls=%fused_computation.7 | convolution fusion | flops 6443499520 | bytes 19922948 | tf_op jit(solution)/shard_map/ia,ea->ie/dot_general | solution.py:49
  410.5 0.0 copy-done.8
  410.5 8.9 %bitcast_dynamic-update-slice_fusion.14 = f32[8,1,512,2048]{3,2,1,0:T(8,128)} fusion(f32[8,1,512,2048]{3,2,1,0:T(8,128)} %bitcast_dynamic-update-slice_fusion.15, s32[]{:T(128)S(6)} %select_n.100, bf16[512,3072]{1,0:T(8,128)(2,1)S(1)} %copy-done.8, bf16[2048,3072]{1,0:T(8,128)(2,1)S(1)} %copy-done.4), kind=kOutput, calls=%fused_computation.15 | convolution fusion | flops 6443499520 | bytes 19922948 | tf_op jit(solution)/shard_map/ia,ea->ie/dot_general | solution.py:49
  419.4 0.0 copy-done.6
  419.4 8.6 %bitcast_dynamic-update-slice_fusion.5 = f32[8,1,512,2048]{3,2,1,0:T(8,128)} fusion(f32[8,1,512,2048]{3,2,1,0:T(8,128)} %bitcast_dynamic-update-slice_fusion.6, s32[]{:T(128)S(6)} %select_n.103, bf16[512,3072]{1,0:T(8,128)(2,1)S(1)} %copy-done.6, bf16[2048,3072]{1,0:T(8,128)(2,1)S(1)} %copy-done.4), kind=kOutput, calls=%fused_computation.6 | convolution fusion | flops 6443499520 | bytes 19922948 | tf_op jit(solution)/shard_map/ia,ea->ie/dot_general | solution.py:49
  428.0 10.1 %bitcast_dynamic-update-slice_fusion.13 = f32[8,1,512,2048]{3,2,1,0:T(8,128)} fusion(f32[8,1,512,2048]{3,2,1,0:T(8,128)} %bitcast_dynamic-update-slice_fusion.14, s32[]{:T(128)S(6)} %select_n.103, bf16[512,3072]{1,0:T(8,128)(2,1)} %collective-permute-done.1, bf16[2048,3072]{1,0:T(8,128)(2,1)S(1)} %copy-done.4), kind=kOutput, calls=%fused_computation.14 | convolution fusion | flops 6443499520 | bytes 19922948 | tf_op jit(solution)/shard_map/ia,ea->ie/dot_general | solution.py:49
  438.0 10.2 %bitcast_dynamic-update-slice_fusion.4 = f32[8,1,512,2048]{3,2,1,0:T(8,128)} fusion(f32[8,1,512,2048]{3,2,1,0:T(8,128)} %bitcast_dynamic-update-slice_fusion.5, s32[]{:T(128)S(6)} %select_n.106, bf16[512,3072]{1,0:T(8,128)(2,1)} %collective-permute-done.9, bf16[2048,3072]{1,0:T(8,128)(2,1)S(1)} %copy-done.4), kind=kOutput, calls=%fused_computation.5 | convolution fusion | flops 6443499520 | bytes 19922948 | tf_op jit(solution)/shard_map/ia,ea->ie/dot_general | solution.py:49
  448.3 10.1 %bitcast_dynamic-update-slice_fusion.12 = f32[8,1,512,2048]{3,2,1,0:T(8,128)} fusion(f32[8,1,512,2048]{3,2,1,0:T(8,128)} %bitcast_dynamic-update-slice_fusion.13, s32[]{:T(128)S(6)} %select_n.106, bf16[512,3072]{1,0:T(8,128)(2,1)} %collective-permute-done.2, bf16[2048,3072]{1,0:T(8,128)(2,1)S(1)} %copy-done.4), kind=kOutput, calls=%fused_computation.13 | convolution fusion | flops 6443499520 | bytes 19922948 | tf_op jit(solution)/shard_map/ia,ea->ie/dot_general | solution.py:49
  458.3 10.1 %bitcast_dynamic-update-slice_fusion.3 = f32[8,1,512,2048]{3,2,1,0:T(8,128)} fusion(f32[8,1,512,2048]{3,2,1,0:T(8,128)} %bitcast_dynamic-update-slice_fusion.4, s32[]{:T(128)S(6)} %select_n.109, bf16[512,3072]{1,0:T(8,128)(2,1)} %collective-permute-done.10, bf16[2048,3072]{1,0:T(8,128)(2,1)S(1)} %copy-done.4), kind=kOutput, calls=%fused_computation.4 | convolution fusion | flops 6443499520 | bytes 19922948 | tf_op jit(solution)/shard_map/ia,ea->ie/dot_general | solution.py:49
  468.4 10.2 %bitcast_dynamic-update-slice_fusion.11 = f32[8,1,512,2048]{3,2,1,0:T(8,128)} fusion(f32[8,1,512,2048]{3,2,1,0:T(8,128)} %bitcast_dynamic-update-slice_fusion.12, s32[]{:T(128)S(6)} %select_n.109, bf16[512,3072]{1,0:T(8,128)(2,1)} %collective-permute-done.3, bf16[2048,3072]{1,0:T(8,128)(2,1)S(1)} %copy-done.4), kind=kOutput, calls=%fused_computation.12 | convolution fusion | flops 6443499520 | bytes 19922948 | tf_op jit(solution)/shard_map/ia,ea->ie/dot_general | solution.py:49
  478.6 10.1 %bitcast_dynamic-update-slice_fusion.10 = f32[8,1,512,2048]{3,2,1,0:T(8,128)} fusion(f32[8,1,512,2048]{3,2,1,0:T(8,128)} %bitcast_dynamic-update-slice_fusion.11, s32[]{:T(128)S(6)} %select_n.112, bf16[512,3072]{1,0:T(8,128)(2,1)} %collective-permute-done.4, bf16[2048,3072]{1,0:T(8,128)(2,1)S(1)} %copy-done.4), kind=kOutput, calls=%fused_computation.11 | convolution fusion | flops 6443499520 | bytes 19922948 | tf_op jit(solution)/shard_map/ia,ea->ie/dot_general | solution.py:49
  488.7 0.0 collective-permute-done.11
  488.7 10.1 %bitcast_dynamic-update-slice_fusion.2 = f32[8,1,512,2048]{3,2,1,0:T(8,128)} fusion(f32[8,1,512,2048]{3,2,1,0:T(8,128)} %bitcast_dynamic-update-slice_fusion.3, s32[]{:T(128)S(6)} %select_n.112, bf16[512,3072]{1,0:T(8,128)(2,1)} %collective-permute-done.11, bf16[2048,3072]{1,0:T(8,128)(2,1)S(1)} %copy-done.4), kind=kOutput, calls=%fused_computation.3 | convolution fusion | flops 6443499520 | bytes 19922948 | tf_op jit(solution)/shard_map/ia,ea->ie/dot_general | solution.py:49
  498.7 10.3 %bitcast_dynamic-update-slice_fusion.1 = f32[8,1,512,2048]{3,2,1,0:T(8,128)} fusion(f32[8,1,512,2048]{3,2,1,0:T(8,128)} %bitcast_dynamic-update-slice_fusion.2, s32[]{:T(128)S(6)} %select_n.115, bf16[512,3072]{1,0:T(8,128)(2,1)} %collective-permute-done.12, bf16[2048,3072]{1,0:T(8,128)(2,1)S(1)} %copy-done.4), kind=kOutput, calls=%fused_computation.2 | convolution fusion | flops 6443499520 | bytes 19922948 | tf_op jit(solution)/shard_map/ia,ea->ie/dot_general | solution.py:49
  509.0 0.0 collective-permute-done.5
  509.0 10.1 %bitcast_dynamic-update-slice_fusion.9 = f32[8,1,512,2048]{3,2,1,0:T(8,128)} fusion(f32[8,1,512,2048]{3,2,1,0:T(8,128)} %bitcast_dynamic-update-slice_fusion.10, s32[]{:T(128)S(6)} %select_n.115, bf16[512,3072]{1,0:T(8,128)(2,1)} %collective-permute-done.5, bf16[2048,3072]{1,0:T(8,128)(2,1)S(1)} %copy-done.4), kind=kOutput, calls=%fused_computation.10 | convolution fusion | flops 6443499520 | bytes 19922948 | tf_op jit(solution)/shard_map/ia,ea->ie/dot_general | solution.py:49
  519.1 0.0 collective-permute-done.13
  519.1 10.1 %bitcast_dynamic-update-slice_fusion = f32[8,1,512,2048]{3,2,1,0:T(8,128)} fusion(f32[8,1,512,2048]{3,2,1,0:T(8,128)} %bitcast_dynamic-update-slice_fusion.1, s32[]{:T(128)S(6)} %select_n.118, bf16[512,3072]{1,0:T(8,128)(2,1)} %collective-permute-done.13, bf16[2048,3072]{1,0:T(8,128)(2,1)S(1)} %copy-done.4), kind=kOutput, calls=%fused_computation.1 | convolution fusion | flops 6443499520 | bytes 19922948 | tf_op jit(solution)/shard_map/ia,ea->ie/dot_general | solution.py:49
  529.2 0.0 collective-permute-done.6
  529.2 10.3 %bitcast_dynamic-update-slice_fusion.8 = f32[8,1,512,2048]{3,2,1,0:T(8,128)} fusion(f32[8,1,512,2048]{3,2,1,0:T(8,128)} %bitcast_dynamic-update-slice_fusion.9, s32[]{:T(128)S(6)} %select_n.118, bf16[512,3072]{1,0:T(8,128)(2,1)} %collective-permute-done.6, bf16[2048,3072]{1,0:T(8,128)(2,1)S(1)} %copy-done.4), kind=kOutput, calls=%fused_computation.9 | convolution fusion | flops 6443499520 | bytes 19922948 | tf_op jit(solution)/shard_map/ia,ea->ie/dot_general | solution.py:49
  (8 shorter events, 0.0 us)
Async XLA Ops:
  7.2 1.9 copy-start
  7.2 349.1 %all-gather.2.cloned.1.call-start = ((), (), s32[]{:S(2)}) async-start(), calls=%async_computation | async-start | bytes 15728640 | tf_op jit(solution)/shard_map/all_gather | solution.py:27
  9.1 212.1 %copy-start.9 = (s32[8]{0:T(128)S(1)}, s32[8]{0:T(128)}, u32[]{:S(2)}) copy-start(s32[8]{0:T(128)} %constant.109.clone) | copy-start | bytes 100
  9.1 218.0 %copy-start.3 = (s32[8]{0:T(128)S(1)}, s32[8]{0:T(128)}, u32[]{:S(2)}) copy-start(s32[8]{0:T(128)} %constant.110.clone) | copy-start | bytes 100
  12.1 141.7 %copy-start.1 = (bf16[512,3072]{1,0:T(8,128)(2,1)}, bf16[512,3072]{1,0:T(8,128)(2,1)S(1)}, u32[]{:S(2)}) copy-start(bf16[512,3072]{1,0:T(8,128)(2,1)S(1)} %subtract_convert_fusion) | copy-start | bytes 9437188
  12.1 72.0 %collective-permute-start.8 = (bf16[512,3072]{1,0:T(8,128)(2,1)S(1)}, bf16[512,3072]{1,0:T(8,128)(2,1)S(1)}, u32[]{:S(2)}, u32[]{:S(2)}) collective-permute-start(bf16[512,3072]{1,0:T(8,128)(2,1)S(1)} %subtract_convert_fusion), channel_id=1, source_target_pairs={{8,0},{16,8},{24,16},{28,24},{20,28},{12,20},{4,12},{0,4},{9,1},{1... | collective-permute-start | bytes 9437192 | tf_op jit(solution)/shard_map/ppermute | solution.py:37
  15.1 71.0 %collective-permute-start = (bf16[512,3072]{1,0:T(8,128)(2,1)S(1)}, bf16[512,3072]{1,0:T(8,128)(2,1)S(1)}, u32[]{:S(2)}, u32[]{:S(2)}) collective-permute-start(bf16[512,3072]{1,0:T(8,128)(2,1)S(1)} %copy-done), channel_id=1, source_target_pairs={{0,8},{8,16},{16,24},{24,28},{28,20},{20,12},{12,4},{4,0},{1,9},{9... | collective-permute-start | bytes 9437192 | tf_op jit(solution)/shard_map/ppermute | solution.py:35
  15.3 138.4 %collective-permute-start.7 = (bf16[512,3072]{1,0:T(8,128)(2,1)S(1)}, bf16[512,3072]{1,0:T(8,128)(2,1)}, u32[]{:S(2)}, u32[]{:S(2)}) collective-permute-start(bf16[512,3072]{1,0:T(8,128)(2,1)S(1)} %subtract_convert_fusion), channel_id=1, source_target_pairs={{0,8},{8,16},{16,24},{24,28},{28,20},{20,12},{12,4},{4,0},{1,9},{9... | collective-permute-start | bytes 9437192 | tf_op jit(solution)/shard_map/ppermute | solution.py:42
  17.2 136.5 %collective-permute-start.1 = (bf16[512,3072]{1,0:T(8,128)(2,1)S(1)}, bf16[512,3072]{1,0:T(8,128)(2,1)}, u32[]{:S(2)}, u32[]{:S(2)}) collective-permute-start(bf16[512,3072]{1,0:T(8,128)(2,1)S(1)} %copy-done), channel_id=1, source_target_pairs={{8,0},{16,8},{24,16},{28,24},{20,28},{12,20},{4,12},{0,4},{9,1},{1... | collective-permute-start | bytes 9437192 | tf_op jit(solution)/shard_map/ppermute | solution.py:40
  84.1 71.6 %copy-start.5 = (bf16[512,3072]{1,0:T(8,128)(2,1)}, bf16[512,3072]{1,0:T(8,128)(2,1)S(1)}, u32[]{:S(2)}) copy-start(bf16[512,3072]{1,0:T(8,128)(2,1)S(1)} %collective-permute-done.8) | copy-start | bytes 9437188
  84.1 134.9 %collective-permute-start.10 = (bf16[512,3072]{1,0:T(8,128)(2,1)S(1)}, bf16[512,3072]{1,0:T(8,128)(2,1)}, u32[]{:S(2)}, u32[]{:S(2)}) collective-permute-start(bf16[512,3072]{1,0:T(8,128)(2,1)S(1)} %collective-permute-done.8), channel_id=1, source_target_pairs={{8,0},{16,8},{24,16},{28,24},{20,28},{12,20},{4,12},{0,4},{9,1},{1... | collective-permute-start | bytes 9437192 | tf_op jit(solution)/shard_map/ppermute | solution.py:37
  86.2 132.9 %copy-start.7 = (bf16[512,3072]{1,0:T(8,128)(2,1)}, bf16[512,3072]{1,0:T(8,128)(2,1)S(1)}, u32[]{:S(2)}) copy-start(bf16[512,3072]{1,0:T(8,128)(2,1)S(1)} %collective-permute-done) | copy-start | bytes 9437188
  86.2 134.9 %collective-permute-start.2 = (bf16[512,3072]{1,0:T(8,128)(2,1)S(1)}, bf16[512,3072]{1,0:T(8,128)(2,1)}, u32[]{:S(2)}, u32[]{:S(2)}) collective-permute-start(bf16[512,3072]{1,0:T(8,128)(2,1)S(1)} %collective-permute-done), channel_id=1, source_target_pairs={{0,8},{8,16},{16,24},{24,28},{28,20},{20,12},{12,4},{4,0},{1,9},{9... | collective-permute-start | bytes 9437192 | tf_op jit(solution)/shard_map/ppermute | solution.py:35
  153.7 134.8 %collective-permute-start.9 = (bf16[512,3072]{1,0:T(8,128)(2,1)}, bf16[512,3072]{1,0:T(8,128)(2,1)}, u32[]{:S(2)}, u32[]{:S(2)}) collective-permute-start(bf16[512,3072]{1,0:T(8,128)(2,1)} %collective-permute-done.7), channel_id=1, source_target_pairs={{0,8},{8,16},{16,24},{24,28},{28,20},{20,12},{12,4},{4,0},{1,9},{9... | collective-permute-start | bytes 9437192 | tf_op jit(solution)/shard_map/ppermute | solution.py:42
  153.8 134.8 %collective-permute-start.3 = (bf16[512,3072]{1,0:T(8,128)(2,1)}, bf16[512,3072]{1,0:T(8,128)(2,1)}, u32[]{:S(2)}, u32[]{:S(2)}) collective-permute-start(bf16[512,3072]{1,0:T(8,128)(2,1)} %collective-permute-done.1), channel_id=1, source_target_pairs={{8,0},{16,8},{24,16},{28,24},{20,28},{12,20},{4,12},{0,4},{9,1},{1... | collective-permute-start | bytes 9437192 | tf_op jit(solution)/shard_map/ppermute | solution.py:40
  219.1 134.8 %collective-permute-start.12 = (bf16[512,3072]{1,0:T(8,128)(2,1)}, bf16[512,3072]{1,0:T(8,128)(2,1)}, u32[]{:S(2)}, u32[]{:S(2)}) collective-permute-start(bf16[512,3072]{1,0:T(8,128)(2,1)} %collective-permute-done.10), channel_id=1, source_target_pairs={{8,0},{16,8},{24,16},{28,24},{20,28},{12,20},{4,12},{0,4},{9,1},{1... | collective-permute-start | bytes 9437192 | tf_op jit(solution)/shard_map/ppermute | solution.py:37
  221.1 134.8 %collective-permute-start.4 = (bf16[512,3072]{1,0:T(8,128)(2,1)}, bf16[512,3072]{1,0:T(8,128)(2,1)}, u32[]{:S(2)}, u32[]{:S(2)}) collective-permute-start(bf16[512,3072]{1,0:T(8,128)(2,1)} %collective-permute-done.2), channel_id=1, source_target_pairs={{0,8},{8,16},{16,24},{24,28},{28,20},{20,12},{12,4},{4,0},{1,9},{9... | collective-permute-start | bytes 9437192 | tf_op jit(solution)/shard_map/ppermute | solution.py:35
  288.5 200.2 %collective-permute-start.11 = (bf16[512,3072]{1,0:T(8,128)(2,1)}, bf16[512,3072]{1,0:T(8,128)(2,1)}, u32[]{:S(2)}, u32[]{:S(2)}) collective-permute-start(bf16[512,3072]{1,0:T(8,128)(2,1)} %collective-permute-done.9), channel_id=1, source_target_pairs={{0,8},{8,16},{16,24},{24,28},{28,20},{20,12},{12,4},{4,0},{1,9},{9... | collective-permute-start | bytes 9437192 | tf_op jit(solution)/shard_map/ppermute | solution.py:42
  288.6 220.4 %collective-permute-start.5 = (bf16[512,3072]{1,0:T(8,128)(2,1)}, bf16[512,3072]{1,0:T(8,128)(2,1)}, u32[]{:S(2)}, u32[]{:S(2)}) collective-permute-start(bf16[512,3072]{1,0:T(8,128)(2,1)} %collective-permute-done.3), channel_id=1, source_target_pairs={{8,0},{16,8},{24,16},{28,24},{20,28},{12,20},{4,12},{0,4},{9,1},{1... | collective-permute-start | bytes 9437192 | tf_op jit(solution)/shard_map/ppermute | solution.py:40
  353.9 165.2 %collective-permute-start.13 = (bf16[512,3072]{1,0:T(8,128)(2,1)}, bf16[512,3072]{1,0:T(8,128)(2,1)}, u32[]{:S(2)}, u32[]{:S(2)}) collective-permute-start(bf16[512,3072]{1,0:T(8,128)(2,1)} %collective-permute-done.12), channel_id=1, source_target_pairs={{8,0},{16,8},{24,16},{28,24},{20,28},{12,20},{4,12},{0,4},{9,1},{1... | collective-permute-start | bytes 9437192 | tf_op jit(solution)/shard_map/ppermute | solution.py:37
  355.9 173.2 %collective-permute-start.6 = (bf16[512,3072]{1,0:T(8,128)(2,1)}, bf16[512,3072]{1,0:T(8,128)(2,1)}, u32[]{:S(2)}, u32[]{:S(2)}) collective-permute-start(bf16[512,3072]{1,0:T(8,128)(2,1)} %collective-permute-done.4), channel_id=1, source_target_pairs={{0,8},{8,16},{16,24},{24,28},{28,20},{20,12},{12,4},{4,0},{1,9},{9... | collective-permute-start | bytes 9437192 | tf_op jit(solution)/shard_map/ppermute | solution.py:35
  356.3 15.6 %copy-start.2 = (bf16[512,3072]{1,0:T(8,128)(2,1)S(1)}, bf16[512,3072]{1,0:T(8,128)(2,1)}, u32[]{:S(2)}) copy-start(bf16[512,3072]{1,0:T(8,128)(2,1)} %copy-done.1) | copy-start | bytes 9437188
  356.3 15.6 %copy-start.4 = (bf16[2048,3072]{1,0:T(8,128)(2,1)S(1)}, bf16[2048,3072]{1,0:T(8,128)(2,1)}, u32[]{:S(2)}) copy-start(bf16[2048,3072]{1,0:T(8,128)(2,1)} %all-gather.2.cloned.1.call-done) | copy-start | bytes 37748740
  400.3 10.2 %copy-start.8 = (bf16[512,3072]{1,0:T(8,128)(2,1)S(1)}, bf16[512,3072]{1,0:T(8,128)(2,1)}, u32[]{:S(2)}) copy-start(bf16[512,3072]{1,0:T(8,128)(2,1)} %copy-done.7) | copy-start | bytes 9437188
  410.5 8.9 %copy-start.6 = (bf16[512,3072]{1,0:T(8,128)(2,1)S(1)}, bf16[512,3072]{1,0:T(8,128)(2,1)}, u32[]{:S(2)}) copy-start(bf16[512,3072]{1,0:T(8,128)(2,1)} %copy-done.5) | copy-start | bytes 9437188
Sparse Core Ops, SparseCore 0:
  9.6 84.7 all-gather.1

commit v2 on v0

v2 whole, which is shorter than its diff:
```python
import functools

import jax
import jax.numpy as jnp
from jax import lax
from jax.experimental import pallas as pl
from jax.experimental.pallas import tpu as pltpu
from jax.sharding import PartitionSpec as P

TILE = 512


def product_kernel(scale, place_ref, left_ref, right_ref, *refs):
    total = lax.dot_general(
        left_ref[...],
        right_ref[...],
        (((1,), (1,)), ((), ())),
        preferred_element_type=jnp.float32,
    )
    result_ref = refs[-1]
    result_ref[...] = (total * scale).astype(result_ref.dtype).reshape(result_ref.shape)


def product(left, right, owner=None, out=None, out_shape=None):
    rows, tokens = left.shape
    columns = right.shape[0]
    tile = min(TILE, columns)
    if owner is None:
        owner = 0
        out_spec = pl.BlockSpec((rows, tile), lambda j, at: (0, j))
        shape = jax.ShapeDtypeStruct((rows, columns), jnp.bfloat16)
    else:
        out_spec = pl.BlockSpec((1, 1, rows, tile), lambda j, at: (at[0], 0, 0, j))
        shape = jax.ShapeDtypeStruct(out_shape, jnp.float32)
    in_specs = [
        pl.BlockSpec((rows, tokens), lambda j, at: (0, 0)),
        pl.BlockSpec((tile, tokens), lambda j, at: (j, 0)),
    ]
    operands = [jnp.asarray(owner, jnp.int32).reshape(1), left, right]
    aliases = {}
    if out is not None:
        aliases = {len(operands): 0}
        in_specs.append(pl.BlockSpec(memory_space=pl.ANY))
        operands.append(out)
    return pl.pallas_call(
        functools.partial(product_kernel, 1.0 / tokens),
        out_shape=shape,
        grid_spec=pltpu.PrefetchScalarGridSpec(
            num_scalar_prefetch=1,
            grid=(columns // tile,),
            in_specs=in_specs,
            out_specs=out_spec,
        ),
        input_output_aliases=aliases,
        compiler_params=pltpu.CompilerParams(vmem_limit_bytes=32 * 1024 * 1024),
        cost_estimate=pl.CostEstimate(
            flops=2 * rows * columns * tokens,
            bytes_accessed=2 * (rows + columns) * tokens + 4 * rows * columns,
            transcendentals=0,
        ),
    )(*operands)


def ring_order(count):
    return [i for i in range(0, count, 2)] + [i for i in reversed(range(1, count, 2))]


def per_device(quantized_inputs, x_full):
    owned_rows = quantized_inputs.shape[0]
    wide_count = lax.axis_size("wide")
    columns = owned_rows * lax.axis_size("narrow")
    order = ring_order(wide_count)
    forward = [(order[i], order[(i + 1) % wide_count]) for i in range(wide_count)]
    pairs = (forward, [(b, a) for a, b in forward])
    place = [order.index(w) for w in range(wide_count)]
    me = jnp.asarray(place, jnp.int32)[lax.axis_index("wide")]

    def owner_of(way, distance):
        offset = distance if way == 1 else -distance
        return jnp.asarray(order, jnp.int32)[(me + offset + wide_count) % wide_count]

    out_shape = (wide_count, 1, owned_rows, columns)
    outs = [None, None]
    now = []

    def tie(value):
        held = [i for i in range(2) if outs[i] is not None]
        done = lax.optimization_barrier((value, *[outs[i] for i in held], *now))
        for place_of, i in enumerate(held):
            outs[i] = done[1 + place_of]
        return done[0]

    def put(which, owner, block):
        outs[which] = product(tie(block), right_own, owner, outs[which], out_shape)

    def put_arrived(which, owner, block):
        outs[which] = lax.dynamic_update_slice(
            outs[which], tie(block).astype(jnp.float32)[None, None], (owner, 0, 0, 0)
        )

    def gather(block):
        return lax.all_gather(block, "narrow", axis=0, tiled=True)

    q = quantized_inputs
    d = (x_full.astype(jnp.float32) - q.astype(jnp.float32)).astype(jnp.bfloat16)
    right_own = gather(q)

    far, near = wide_count // 2, (wide_count - 1) // 2
    reach = {(0, 0): far, (0, 1): near, (1, 0): near, (1, 1): far}
    raw = {chain: max(hops - 1, min(hops, 1)) for chain, hops in reach.items()}
    at = {(which, way): [(q, d)[which]] for which in range(2) for way in range(2)}

    def start(which, step):
        for way in range(2):
            chain = (which, way)
            if step <= raw[chain]:
                block = at[chain][step - 1]
                block = block if step == 1 else tie(block)
                at[chain].append(lax.ppermute(block, "wide", pairs[way]))

    def arrivals(which, step):
        return [at[which, way][step] for way in range(2) if step <= raw[which, way]]

    start(0, 1)
    start(1, 1)
    right_next = [None, None]
    results = []
    for step in range(1, far + 1):
        if arrivals(0, step):
            now[:] = arrivals(0, step)
            start(0, step + 1)
            if step == 1:
                for way in range(2):
                    if raw[0, 1 - way] >= 1:
                        right_next[way] = gather(tie(at[0, 1 - way][1]))
        if arrivals(1, step):
            now[:] = arrivals(1, step)
            start(1, step + 1)
        sent = []
        for which in (1, 0):
            for way in range(2):
                if step == raw[which, way] < reach[which, way]:
                    result = product(tie(at[which, way][step]), right_next[way])
                    sent.append(result)
                    results.append(
                        (which, owner_of(way, step + 1), lax.ppermute(result, "wide", pairs[way]))
                    )
        now += sent
        if step == 1:
            put(0, lax.axis_index("wide"), q)
            put(1, lax.axis_index("wide"), d)
        for which in range(2):
            for way in range(2):
                if step <= raw[which, way]:
                    put(which, owner_of(way, step), at[which, way][step])
    now[:] = []
    for result in results:
        put_arrived(*result)
    return tuple(outs)


def solution(mesh):
    return jax.shard_map(
        per_device,
        mesh=mesh,
        in_specs=(P(("wide", "narrow"), None), P(("wide", "narrow"), None)),
        out_specs=(P(None, "narrow", None, "wide"), P(None, "narrow", None, "wide")),
        check_vma=False,
    )
```

time: 1210 us -> 463 us (0.38)
  waiting for transfers between devices: 1030 us -> 206 us
  Pallas kernels: 0 us -> 163 us
  matrix products: 115 us -> 0 us
  starting transfers between devices: 0.08 us -> 16 us
  between operations: 14.1 us -> 26.9 us
  other arithmetic: 7.36 us -> 19.6 us
    all_gather x2 -> x3, waiting for transfers between devices: 1030 us -> 0.01 us  [gather(): return lax.all_gather(block, 'narrow', axis=0, tiled=True)]
    ppermute x0 -> x14, waiting for transfers between devices: none -> 204 us  [the longest x10 187 us: start(): at[chain].append(lax.ppermute(block, 'wide', pairs[way]))]
    pallas_call x0 -> x16, Pallas kernels: none -> 163 us  [product(): pl.pallas_call(functools.partial(product_kernel, 1.0 / tokens), out_shape...]
    dot_general x1 -> x0, matrix products: 115 us -> none  [per_device(): jnp.einsum('yia,ea->yie', left_operand_block, load_right_operand(quantize...]
    slice x1 -> x0, local copies, waits for them, and re-layouts: 42.1 us -> none  [per_device(): tile_pairs[1].reshape(wide_count, 1, owned_rows, tile_pairs.shape[2])]
    unnamed x2 -> x30, local copies, waits for them, and re-layouts: 0.01 us -> 29.3 us
    ppermute x0 -> x14, starting transfers between devices: none -> 15.9 us  [the longest x10 11.2 us: start(): at[chain].append(lax.ppermute(block, 'wide', pairs[way]))]
    dynamic_update_slice x0 -> x4, other arithmetic: none -> 14.9 us  [put_arrived(): lax.dynamic_update_slice(outs[which], tie(block).astype(jnp.float32)[None...]
  transfers between devices with their start and end apart: 2 -> 17, of which waited for: 2 -> 6; matrix products, arithmetic and copies ran while one was open for 1% -> 4% of each run, Pallas kernels for 0% -> 35%
where the time goes in v2:
time: 463 us; the launch traced here: 462 us
  waiting for transfers between devices  206 us (44%)
  Pallas kernels  163 us (35%)
  local copies, waits for them, and re-layouts  30.6 us (7%)
  between operations  26.9 us (6%)
  other arithmetic  19.6 us (4%)
  starting transfers between devices  16 us (3%)
    ppermute x10, waiting for transfers between devices, start(): at[chain].append(lax.ppermute(block, 'wide', pairs[way]))  187 us
    pallas_call x16, Pallas kernels, product(): pl.pallas_call(functools.partial(product_kernel, 1.0 / tokens), out_shape...  163 us
    unnamed x30, local copies, waits for them, and re-layouts  29.3 us
    ppermute x4, waiting for transfers between devices, per_device(): lax.ppermute(result, 'wide', pairs[way])  17.5 us
    dynamic_update_slice x4, other arithmetic, put_arrived(): lax.dynamic_update_slice(outs[which], tie(block).astype(jnp.float32)[None...  14.9 us
    ppermute x10, starting transfers between devices, start(): at[chain].append(lax.ppermute(block, 'wide', pairs[way]))  11.2 us
  transfers between devices with their start and end apart: 17, of which 6 were waited for; matrix products, arithmetic and copies ran while one was open for 4% of the time, Pallas kernels for 35%

profile of v2, /device:TPU:0, one launch (start us, length us, event | category | flops | bytes accessed | tf_op | source)
XLA Modules:
  0.0 461.7 jit_solution(4234979795572071262)
XLA Ops:
  7.2 0.0 all-gather.4.cloned.1.call-start
  7.2 0.7 all-gather.4.cloned.1.call-update
  7.9 0.0 all-gather.6.cloned.1.call-start
  8.0 3.1 collective-permute-start.3
  11.0 0.0 collective-permute-start.4
  11.0 68.4 %collective-permute-done.3.left_ref = bf16[512,3072]{1,0:T(8,128)(2,1)} collective-permute-done((bf16[512,3072]{1,0:T(8,128)(2,1)}, bf16[512,3072]{1,0:T(8,128)(2,1)}, u32[]{:S(2)}, u32[]{:S(2)}) %collective-permute-start.3) | collective-permute-done | bytes 3145760 | tf_op jit(solution)/shard_map/ppermute | solution.py:119
  79.4 1.5 collective-permute-done.4.left_ref
  80.9 0.0 all-gather.6.cloned.1.call-update
  80.9 0.0 all-gather.8.cloned.1.call-start
  81.0 0.7 all-gather.8.cloned.1.call-update
  81.7 0.0 copy-start.11
  81.7 0.0 copy-start.10
  81.7 4.7 %subtract_convert_fusion.left_ref = bf16[512,3072]{1,0:T(8,128)(2,1)} fusion(bf16[512,3072]{1,0:T(8,128)(2,1)S(1)} %copy-done.3, bf16[512,3072]{1,0:T(8,128)(2,1)} %param.18), kind=kLoop, calls=%fused_computation | loop fusion | flops 6291456 | bytes 9437184 | tf_op jit(solution)/shard_map/convert_element_type | solution.py:105
  86.4 0.3 collective-permute-start
  86.7 1.7 collective-permute-start.1
  88.4 0.6 dynamic_slice.45
  94.3 0.7 fusion
  102.7 0.4 collective-permute-start.6
  103.1 1.7 collective-permute-start.5
  104.8 52.9 %collective-permute-done.left_ref = bf16[512,3072]{1,0:T(8,128)(2,1)} collective-permute-done((bf16[512,3072]{1,0:T(8,128)(2,1)}, bf16[512,3072]{1,0:T(8,128)(2,1)}, u32[]{:S(2)}, u32[]{:S(2)}) %collective-permute-start) | collective-permute-done | bytes 3145760 | tf_op jit(solution)/shard_map/ppermute | solution.py:119
  157.7 0.3 collective-permute-done.1.left_ref
  158.0 1.7 collective-permute-start.7
  159.7 0.3 collective-permute-start.2
  160.1 4.7 %copy-done = bf16[2048,3072]{1,0:T(8,128)(2,1)S(1)} copy-done((bf16[2048,3072]{1,0:T(8,128)(2,1)S(1)}, bf16[2048,3072]{1,0:T(8,128)(2,1)}, u32[]{:S(2)}) %copy-start) | copy-done | bytes 12582936
  164.7 8.3 %shard_map.176.refs_0_ = f32[8,1,512,2048]{3,2,1,0:T(8,128)} custom-call(s32[1]{0:T(128)} %bitcast.2.place_ref, bf16[512,3072]{1,0:T(8,128)(2,1)S(1)} %copy-done.3, bf16[2048,3072]{1,0:T(8,128)(2,1)S(1)} %copy-done), custom_call_target="tpu_custom_call" | custom-call | flops 6442450944 | bytes 19922944 | tf_op jit(solution)/shard_map/pallas_call | solution.py:45
  173.0 10.2 %shard_map.177.refs_0_ = f32[8,1,512,2048]{3,2,1,0:T(8,128)} custom-call(s32[1]{0:T(128)} %bitcast.2.place_ref, bf16[512,3072]{1,0:T(8,128)(2,1)} %subtract_convert_fusion.left_ref, bf16[2048,3072]{1,0:T(8,128)(2,1)S(1)} %copy-done.1), custom_call_target="tpu_custom_call" | custom-call | flops 6442450944 | bytes 19922944 | tf_op jit(solution)/shard_map/pallas_call | solution.py:45
  183.2 11.0 %shard_map.178.refs_0_ = f32[8,1,512,2048]{3,2,1,0:T(8,128)} custom-call(s32[1]{0:T(128)} %get-tuple-element.132.place_ref, bf16[512,3072]{1,0:T(8,128)(2,1)} %collective-permute-done.3.left_ref, bf16[2048,3072]{1,0:T(8,128)(2,1)S(1)} %copy-done.1, f32[8,1,512,2048]{3,2,1,0:T(8,128)} %shard_map.176.refs_0_), custom_call_target="tpu_custom_call", output_to_operand_aliasing={{}: (3, {})} | custom-call | flops 6442450944 | bytes 19922944 | tf_op jit(solution)/shard_map/pallas_call | solution.py:45
  194.2 11.1 %shard_map.179.refs_0_ = f32[8,1,512,2048]{3,2,1,0:T(8,128)} custom-call(s32[1]{0:T(128)} %get-tuple-element.133.place_ref, bf16[512,3072]{1,0:T(8,128)(2,1)} %collective-permute-done.4.left_ref, bf16[2048,3072]{1,0:T(8,128)(2,1)S(1)} %copy-done.1, f32[8,1,512,2048]{3,2,1,0:T(8,128)} %shard_map.178.refs_0_), custom_call_target="tpu_custom_call", output_to_operand_aliasing={{}: (3, {})} | custom-call | flops 6442450944 | bytes 19922944 | tf_op jit(solution)/shard_map/pallas_call | solution.py:45
  205.3 10.8 %shard_map.180.refs_0_ = f32[8,1,512,2048]{3,2,1,0:T(8,128)} custom-call(s32[1]{0:T(128)} %get-tuple-element.132.place_ref, bf16[512,3072]{1,0:T(8,128)(2,1)} %collective-permute-done.1.left_ref, bf16[2048,3072]{1,0:T(8,128)(2,1)S(1)} %copy-done.1, f32[8,1,512,2048]{3,2,1,0:T(8,128)} %shard_map.177.refs_0_), custom_call_target="tpu_custom_call", output_to_operand_aliasing={{}: (3, {})} | custom-call | flops 6442450944 | bytes 19922944 | tf_op jit(solution)/shard_map/pallas_call | solution.py:45
  216.1 10.9 %shard_map.181.refs_0_ = f32[8,1,512,2048]{3,2,1,0:T(8,128)} custom-call(s32[1]{0:T(128)} %get-tuple-element.133.place_ref, bf16[512,3072]{1,0:T(8,128)(2,1)} %collective-permute-done.left_ref, bf16[2048,3072]{1,0:T(8,128)(2,1)S(1)} %copy-done.1, f32[8,1,512,2048]{3,2,1,0:T(8,128)} %shard_map.180.refs_0_), custom_call_target="tpu_custom_call", output_to_operand_aliasing={{}: (3, {})} | custom-call | flops 6442450944 | bytes 19922944 | tf_op jit(solution)/shard_map/pallas_call | solution.py:45
  227.0 0.0 collective-permute-done.6.left_ref
  227.0 0.0 collective-permute-done.5.left_ref
  227.0 63.5 %collective-permute-done.7.left_ref = bf16[512,3072]{1,0:T(8,128)(2,1)} collective-permute-done((bf16[512,3072]{1,0:T(8,128)(2,1)}, bf16[512,3072]{1,0:T(8,128)(2,1)}, u32[]{:S(2)}, u32[]{:S(2)}) %collective-permute-start.7) | collective-permute-done | bytes 3145760 | tf_op jit(solution)/shard_map/ppermute | solution.py:119
  290.5 0.0 collective-permute-done.2.left_ref
  290.5 1.5 collective-permute-start.8
  292.0 0.5 collective-permute-start.11
  292.5 4.6 copy-done.6
  297.1 10.0 %shard_map.182 = bf16[512,2048]{1,0:T(8,128)(2,1)} custom-call(s32[1]{0:T(128)} %constant.84.clone.1.place_ref, bf16[512,3072]{1,0:T(8,128)(2,1)} %collective-permute-done.7.left_ref, bf16[2048,3072]{1,0:T(8,128)(2,1)S(1)} %copy-done.6), custom_call_target="tpu_custom_call" | custom-call | flops 6442450944 | bytes 19922944 | tf_op jit(solution)/shard_map/pallas_call | solution.py:45
  307.2 1.4 collective-permute-start.10
  308.6 4.6 copy-done.8
  313.1 10.1 %shard_map.183 = bf16[512,2048]{1,0:T(8,128)(2,1)} custom-call(s32[1]{0:T(128)} %constant.84.clone.1.place_ref, bf16[512,3072]{1,0:T(8,128)(2,1)} %collective-permute-done.6.left_ref, bf16[2048,3072]{1,0:T(8,128)(2,1)S(1)} %copy-done.8), custom_call_target="tpu_custom_call" | custom-call | flops 6442450944 | bytes 19922944 | tf_op jit(solution)/shard_map/pallas_call | solution.py:45
  323.2 0.6 collective-permute-start.12
  323.9 4.6 copy-done.2
  328.4 10.9 %shard_map.184.refs_0_ = f32[8,1,512,2048]{3,2,1,0:T(8,128)} custom-call(s32[1]{0:T(128)} %get-tuple-element.129.place_ref, bf16[512,3072]{1,0:T(8,128)(2,1)} %collective-permute-done.5.left_ref, bf16[2048,3072]{1,0:T(8,128)(2,1)S(1)} %copy-done.2, f32[8,1,512,2048]{3,2,1,0:T(8,128)} %shard_map.179.refs_0_), custom_call_target="tpu_custom_call", output_to_operand_aliasing={{}: (3, {})} | custom-call | flops 6442450944 | bytes 19922944 | tf_op jit(solution)/shard_map/pallas_call | solution.py:45
  339.3 10.8 %shard_map.185.refs_0_ = f32[8,1,512,2048]{3,2,1,0:T(8,128)} custom-call(s32[1]{0:T(128)} %get-tuple-element.130.place_ref, bf16[512,3072]{1,0:T(8,128)(2,1)} %collective-permute-done.6.left_ref, bf16[2048,3072]{1,0:T(8,128)(2,1)S(1)} %copy-done.2, f32[8,1,512,2048]{3,2,1,0:T(8,128)} %shard_map.184.refs_0_), custom_call_target="tpu_custom_call", output_to_operand_aliasing={{}: (3, {})} | custom-call | flops 6442450944 | bytes 19922944 | tf_op jit(solution)/shard_map/pallas_call | solution.py:45
  350.1 10.9 %shard_map.186.refs_0_ = f32[8,1,512,2048]{3,2,1,0:T(8,128)} custom-call(s32[1]{0:T(128)} %get-tuple-element.129.place_ref, bf16[512,3072]{1,0:T(8,128)(2,1)} %collective-permute-done.7.left_ref, bf16[2048,3072]{1,0:T(8,128)(2,1)S(1)} %copy-done.2, f32[8,1,512,2048]{3,2,1,0:T(8,128)} %shard_map.181.refs_0_), custom_call_target="tpu_custom_call", output_to_operand_aliasing={{}: (3, {})} | custom-call | flops 6442450944 | bytes 19922944 | tf_op jit(solution)/shard_map/pallas_call | solution.py:45
  361.0 10.8 %shard_map.187.refs_0_ = f32[8,1,512,2048]{3,2,1,0:T(8,128)} custom-call(s32[1]{0:T(128)} %get-tuple-element.130.place_ref, bf16[512,3072]{1,0:T(8,128)(2,1)} %collective-permute-done.2.left_ref, bf16[2048,3072]{1,0:T(8,128)(2,1)S(1)} %copy-done.2, f32[8,1,512,2048]{3,2,1,0:T(8,128)} %shard_map.186.refs_0_), custom_call_target="tpu_custom_call", output_to_operand_aliasing={{}: (3, {})} | custom-call | flops 6442450944 | bytes 19922944 | tf_op jit(solution)/shard_map/pallas_call | solution.py:45
  371.8 0.0 collective-permute-done.8.left_ref
  371.8 4.6 copy-done.9
  376.4 8.2 %shard_map.188 = bf16[512,2048]{1,0:T(8,128)(2,1)} custom-call(s32[1]{0:T(128)} %constant.84.clone.1.place_ref, bf16[512,3072]{1,0:T(8,128)(2,1)S(1)} %collective-permute-done.8.left_ref, bf16[2048,3072]{1,0:T(8,128)(2,1)S(1)} %copy-done.9), custom_call_target="tpu_custom_call" | custom-call | flops 6442450944 | bytes 19922944 | tf_op jit(solution)/shard_map/pallas_call | solution.py:45
  384.5 1.7 copy-done.4
  386.3 0.0 collective-permute-done.11.left_ref
  386.3 1.5 collective-permute-start.9
  387.8 4.6 copy-done.7
  392.4 9.3 %shard_map.189 = bf16[512,2048]{1,0:T(8,128)(2,1)S(1)} custom-call(s32[1]{0:T(128)} %constant.84.clone.1.place_ref, bf16[512,3072]{1,0:T(8,128)(2,1)} %collective-permute-done.11.left_ref, bf16[2048,3072]{1,0:T(8,128)(2,1)S(1)} %copy-done.7), custom_call_target="tpu_custom_call" | custom-call | flops 6442450944 | bytes 19922944 | tf_op jit(solution)/shard_map/pallas_call | solution.py:45
  401.7 1.1 collective-permute-start.13
  402.9 10.9 %shard_map.190 = f32[8,1,512,2048]{3,2,1,0:T(8,128)} custom-call(s32[1]{0:T(128)} %get-tuple-element.135.place_ref, bf16[512,3072]{1,0:T(8,128)(2,1)} %collective-permute-done.11.left_ref, bf16[2048,3072]{1,0:T(8,128)(2,1)S(1)} %bitcast.26, f32[8,1,512,2048]{3,2,1,0:T(8,128)} %shard_map.185.refs_0_), custom_call_target="tpu_custom_call", output_to_operand_aliasing={{}: (3, {})} | custom-call | flops 6442450944 | bytes 19922944 | tf_op jit(solution)/shard_map/pallas_call | solution.py:45
  413.7 9.0 %shard_map.191 = f32[8,1,512,2048]{3,2,1,0:T(8,128)} custom-call(s32[1]{0:T(128)} %get-tuple-element.131.place_ref, bf16[512,3072]{1,0:T(8,128)(2,1)S(1)} %copy-done.5, bf16[2048,3072]{1,0:T(8,128)(2,1)S(1)} %bitcast.26, f32[8,1,512,2048]{3,2,1,0:T(8,128)} %shard_map.187.refs_0_), custom_call_target="tpu_custom_call", output_to_operand_aliasing={{}: (3, {})} | custom-call | flops 6442450944 | bytes 19922944 | tf_op jit(solution)/shard_map/pallas_call | solution.py:45
  422.7 0.0 collective-permute-done.10
  422.7 4.1 convert_dynamic-update-slice_fusion.3
  426.8 4.1 convert_dynamic-update-slice_fusion.2
  430.9 17.5 %collective-permute-done.9 = bf16[512,2048]{1,0:T(8,128)(2,1)} collective-permute-done((bf16[512,2048]{1,0:T(8,128)(2,1)}, bf16[512,2048]{1,0:T(8,128)(2,1)}, u32[]{:S(2)}, u32[]{:S(2)}) %collective-permute-start.9) | collective-permute-done | bytes 2097184 | tf_op jit(solution)/shard_map/ppermute | solution.py:146
  448.5 4.1 convert_dynamic-update-slice_fusion.1
  452.6 2.5 convert_dynamic-update-slice_fusion
  (27 shorter events, 0.0 us)
Async XLA Ops:
  7.2 74.5 %copy-start.3 = (bf16[512,3072]{1,0:T(8,128)(2,1)S(1)}, bf16[512,3072]{1,0:T(8,128)(2,1)}, u32[]{:S(2)}) copy-start(bf16[512,3072]{1,0:T(8,128)(2,1)} %left_ref) | copy-start | bytes 9437188
  7.2 152.9 %all-gather.4.cloned.1.call-start = ((), (), s32[]{:S(2)}) async-start(), calls=%async_computation | async-start | bytes 15728640 | tf_op jit(solution)/shard_map/all_gather | solution.py:102
  7.9 284.6 %all-gather.6.cloned.1.call-start = ((), (), s32[]{:S(2)}) async-start(), calls=%async_computation.1 | async-start | bytes 15728640 | tf_op jit(solution)/shard_map/all_gather | solution.py:102
  8.0 71.4 %collective-permute-start.3 = (bf16[512,3072]{1,0:T(8,128)(2,1)}, bf16[512,3072]{1,0:T(8,128)(2,1)}, u32[]{:S(2)}, u32[]{:S(2)}) collective-permute-start(bf16[512,3072]{1,0:T(8,128)(2,1)} %left_ref), channel_id=1, source_target_pairs={{0,8},{8,16},{16,24},{24,28},{28,20},{20,12},{12,4},{4,0},{1,9},{9... | collective-permute-start | bytes 9437192 | tf_op jit(solution)/shard_map/ppermute | solution.py:119
  11.0 69.9 %collective-permute-start.4 = (bf16[512,3072]{1,0:T(8,128)(2,1)}, bf16[512,3072]{1,0:T(8,128)(2,1)}, u32[]{:S(2)}, u32[]{:S(2)}) collective-permute-start(bf16[512,3072]{1,0:T(8,128)(2,1)} %left_ref), channel_id=1, source_target_pairs={{8,0},{16,8},{24,16},{28,24},{20,28},{12,20},{4,12},{0,4},{9,1},{1... | collective-permute-start | bytes 9437192 | tf_op jit(solution)/shard_map/ppermute | solution.py:119
  80.9 227.6 %all-gather.8.cloned.1.call-start = ((), (), s32[]{:S(2)}) async-start(), calls=%async_computation.2 | async-start | bytes 15728640 | tf_op jit(solution)/shard_map/all_gather | solution.py:102
  81.7 6.7 %copy-start.11 = (s32[8]{0:T(128)S(1)}, s32[8]{0:T(128)}, u32[]{:S(2)}) copy-start(s32[8]{0:T(128)} %constant.98.clone) | copy-start | bytes 100
  81.7 12.6 %copy-start.10 = (s32[8]{0:T(128)S(1)}, s32[8]{0:T(128)}, u32[]{:S(2)}) copy-start(s32[8]{0:T(128)} %constant.99.clone) | copy-start | bytes 100
  86.4 71.4 %collective-permute-start = (bf16[512,3072]{1,0:T(8,128)(2,1)}, bf16[512,3072]{1,0:T(8,128)(2,1)}, u32[]{:S(2)}, u32[]{:S(2)}) collective-permute-start(bf16[512,3072]{1,0:T(8,128)(2,1)} %subtract_convert_fusion.left_ref), channel_id=1, source_target_pairs={{8,0},{16,8},{24,16},{28,24},{20,28},{12,20},{4,12},{0,4},{9,1},{1... | collective-permute-start | bytes 9437192 | tf_op jit(solution)/shard_map/ppermute | solution.py:119
  86.7 71.4 %collective-permute-start.1 = (bf16[512,3072]{1,0:T(8,128)(2,1)}, bf16[512,3072]{1,0:T(8,128)(2,1)}, u32[]{:S(2)}, u32[]{:S(2)}) collective-permute-start(bf16[512,3072]{1,0:T(8,128)(2,1)} %subtract_convert_fusion.left_ref), channel_id=1, source_target_pairs={{0,8},{8,16},{16,24},{24,28},{28,20},{20,12},{12,4},{4,0},{1,9},{9... | collective-permute-start | bytes 9437192 | tf_op jit(solution)/shard_map/ppermute | solution.py:119
  102.7 124.3 %collective-permute-start.6 = (bf16[512,3072]{1,0:T(8,128)(2,1)}, bf16[512,3072]{1,0:T(8,128)(2,1)}, u32[]{:S(2)}, u32[]{:S(2)}) collective-permute-start(bf16[512,3072]{1,0:T(8,128)(2,1)} %collective-permute-done.4.left_ref), channel_id=1, source_target_pairs={{8,0},{16,8},{24,16},{28,24},{20,28},{12,20},{4,12},{0,4},{9,1},{1... | collective-permute-start | bytes 9437192 | tf_op jit(solution)/shard_map/ppermute | solution.py:119
  103.1 124.0 %collective-permute-start.5 = (bf16[512,3072]{1,0:T(8,128)(2,1)}, bf16[512,3072]{1,0:T(8,128)(2,1)}, u32[]{:S(2)}, u32[]{:S(2)}) collective-permute-start(bf16[512,3072]{1,0:T(8,128)(2,1)} %collective-permute-done.3.left_ref), channel_id=1, source_target_pairs={{0,8},{8,16},{16,24},{24,28},{28,20},{20,12},{12,4},{4,0},{1,9},{9... | collective-permute-start | bytes 9437192 | tf_op jit(solution)/shard_map/ppermute | solution.py:119
  158.0 132.5 %collective-permute-start.7 = (bf16[512,3072]{1,0:T(8,128)(2,1)}, bf16[512,3072]{1,0:T(8,128)(2,1)}, u32[]{:S(2)}, u32[]{:S(2)}) collective-permute-start(bf16[512,3072]{1,0:T(8,128)(2,1)} %collective-permute-done.1.left_ref), channel_id=1, source_target_pairs={{0,8},{8,16},{16,24},{24,28},{28,20},{20,12},{12,4},{4,0},{1,9},{9... | collective-permute-start | bytes 9437192 | tf_op jit(solution)/shard_map/ppermute | solution.py:119
  159.7 130.8 %collective-permute-start.2 = (bf16[512,3072]{1,0:T(8,128)(2,1)}, bf16[512,3072]{1,0:T(8,128)(2,1)}, u32[]{:S(2)}, u32[]{:S(2)}) collective-permute-start(bf16[512,3072]{1,0:T(8,128)(2,1)} %collective-permute-done.left_ref), channel_id=1, source_target_pairs={{8,0},{16,8},{24,16},{28,24},{20,28},{12,20},{4,12},{0,4},{9,1},{1... | collective-permute-start | bytes 9437192 | tf_op jit(solution)/shard_map/ppermute | solution.py:119
  160.1 4.7 %copy-start = (bf16[2048,3072]{1,0:T(8,128)(2,1)S(1)}, bf16[2048,3072]{1,0:T(8,128)(2,1)}, u32[]{:S(2)}) copy-start(bf16[2048,3072]{1,0:T(8,128)(2,1)} %all-gather.4.cloned.1.call-done.right_ref) | copy-start | bytes 37748740
  164.7 8.3 %copy-start.1 = (bf16[2048,3072]{1,0:T(8,128)(2,1)S(1)}, bf16[2048,3072]{1,0:T(8,128)(2,1)}, u32[]{:S(2)}) copy-start(bf16[2048,3072]{1,0:T(8,128)(2,1)} %all-gather.4.cloned.1.call-done.right_ref) | copy-start | bytes 37748740
  290.5 81.3 %collective-permute-start.8 = (bf16[512,3072]{1,0:T(8,128)(2,1)}, bf16[512,3072]{1,0:T(8,128)(2,1)S(1)}, u32[]{:S(2)}, u32[]{:S(2)}) collective-permute-start(bf16[512,3072]{1,0:T(8,128)(2,1)} %collective-permute-done.2.left_ref), channel_id=1, source_target_pairs={{8,0},{16,8},{24,16},{28,24},{20,28},{12,20},{4,12},{0,4},{9,1},{1... | collective-permute-start | bytes 9437192 | tf_op jit(solution)/shard_map/ppermute | solution.py:119
  292.0 94.3 %collective-permute-start.11 = (bf16[512,3072]{1,0:T(8,128)(2,1)}, bf16[512,3072]{1,0:T(8,128)(2,1)}, u32[]{:S(2)}, u32[]{:S(2)}) collective-permute-start(bf16[512,3072]{1,0:T(8,128)(2,1)} %collective-permute-done.5.left_ref), channel_id=1, source_target_pairs={{0,8},{8,16},{16,24},{24,28},{28,20},{20,12},{12,4},{4,0},{1,9},{9... | collective-permute-start | bytes 9437192 | tf_op jit(solution)/shard_map/ppermute | solution.py:119
  292.5 4.6 copy-start.6
  307.2 115.5 %collective-permute-start.10 = (bf16[512,2048]{1,0:T(8,128)(2,1)}, bf16[512,2048]{1,0:T(8,128)(2,1)}, u32[]{:S(2)}, u32[]{:S(2)}) collective-permute-start(bf16[512,2048]{1,0:T(8,128)(2,1)} %shard_map.182), channel_id=1, source_target_pairs={{0,8},{8,16},{16,24},{24,28},{28,20},{20,12},{12,4},{4,0},{1,9},{9... | collective-permute-start | bytes 6291464 | tf_op jit(solution)/shard_map/ppermute | solution.py:146
  308.6 4.6 copy-start.8
  323.2 103.6 %collective-permute-start.12 = (bf16[512,2048]{1,0:T(8,128)(2,1)}, bf16[512,2048]{1,0:T(8,128)(2,1)}, u32[]{:S(2)}, u32[]{:S(2)}) collective-permute-start(bf16[512,2048]{1,0:T(8,128)(2,1)} %shard_map.183), channel_id=1, source_target_pairs={{8,0},{16,8},{24,16},{28,24},{20,28},{12,20},{4,12},{0,4},{9,1},{1... | collective-permute-start | bytes 6291464 | tf_op jit(solution)/shard_map/ppermute | solution.py:146
  323.8 4.6 copy-start.2
  371.8 4.6 copy-start.9
  376.4 26.5 %slice-start = ((s8[12582912]{0:T(1024)(128)(4,1)}), s8[4194304]{0:T(1024)(128)(4,1)S(1)}, s32[]{:S(2)}) async-start(s8[12582912]{0:T(1024)(128)(4,1)} %bitcast.25), calls=%async_computation.3 | async-start | bytes 8388608
  376.4 26.5 %slice-start.1 = ((s8[12582912]{0:T(1024)(128)(4,1)}), s8[4194304]{0:T(1024)(128)(4,1)S(1)}, s32[]{:S(2)}) async-start(s8[12582912]{0:T(1024)(128)(4,1)} %bitcast.25), calls=%async_computation.4 | async-start | bytes 8388608
  384.5 1.7 copy-start.4
  386.3 16.6 %slice-start.2 = ((s8[12582912]{0:T(1024)(128)(4,1)}), s8[4194304]{0:T(1024)(128)(4,1)S(1)}, s32[]{:S(2)}) async-start(s8[12582912]{0:T(1024)(128)(4,1)} %bitcast.25), calls=%async_computation.5 | async-start | bytes 8388608
  386.3 62.2 %collective-permute-start.9 = (bf16[512,2048]{1,0:T(8,128)(2,1)}, bf16[512,2048]{1,0:T(8,128)(2,1)}, u32[]{:S(2)}, u32[]{:S(2)}) collective-permute-start(bf16[512,2048]{1,0:T(8,128)(2,1)} %shard_map.188), channel_id=1, source_target_pairs={{8,0},{16,8},{24,16},{28,24},{20,28},{12,20},{4,12},{0,4},{9,1},{1... | collective-permute-start | bytes 6291464 | tf_op jit(solution)/shard_map/ppermute | solution.py:146
  387.8 4.6 copy-start.7
  401.7 12.0 %copy-start.5 = (bf16[512,3072]{1,0:T(8,128)(2,1)S(1)}, bf16[512,3072]{1,0:T(8,128)(2,1)}, u32[]{:S(2)}) copy-start(bf16[512,3072]{1,0:T(8,128)(2,1)} %copy-done.4) | copy-start | bytes 9437188
  401.7 50.9 %collective-permute-start.13 = (bf16[512,2048]{1,0:T(8,128)(2,1)S(1)}, bf16[512,2048]{1,0:T(8,128)(2,1)S(1)}, u32[]{:S(2)}, u32[]{:S(2)}) collective-permute-start(bf16[512,2048]{1,0:T(8,128)(2,1)S(1)} %shard_map.189), channel_id=1, source_target_pairs={{0,8},{8,16},{16,24},{24,28},{28,20},{20,12},{12,4},{4,0},{1,9},{9... | collective-permute-start | bytes 6291464 | tf_op jit(solution)/shard_map/ppermute | solution.py:146
Sparse Core Ops, SparseCore 0:
  9.6 84.7 all-gather.3
  96.0 82.0 all-gather.5
  179.7 82.0 all-gather.7

commit v3 on v2

--- a/solution.py
+++ b/solution.py
@@ -8,6 +8,7 @@
 from jax.sharding import PartitionSpec as P
 
 TILE = 512
+LAST_PIECES = 2
 
 
 def product_kernel(scale, place_ref, left_ref, right_ref, *refs):
@@ -21,8 +22,8 @@
     result_ref[...] = (total * scale).astype(result_ref.dtype).reshape(result_ref.shape)
 
 
-def product(left, right, owner=None, out=None, out_shape=None):
-    rows, tokens = left.shape
+def product(left, right, owner=None, out=None, out_shape=None, piece=0, pieces=1):
+    rows, tokens = left.shape[0] // pieces, left.shape[1]
     columns = right.shape[0]
     tile = min(TILE, columns)
     if owner is None:
@@ -33,7 +34,7 @@
         out_spec = pl.BlockSpec((1, 1, rows, tile), lambda j, at: (at[0], 0, 0, j))
         shape = jax.ShapeDtypeStruct(out_shape, jnp.float32)
     in_specs = [
-        pl.BlockSpec((rows, tokens), lambda j, at: (0, 0)),
+        pl.BlockSpec((rows, tokens), lambda j, at: (piece, 0)),
         pl.BlockSpec((tile, tokens), lambda j, at: (j, 0)),
     ]
     operands = [jnp.asarray(owner, jnp.int32).reshape(1), left, right]
@@ -53,11 +54,7 @@
         ),
         input_output_aliases=aliases,
         compiler_params=pltpu.CompilerParams(vmem_limit_bytes=32 * 1024 * 1024),
-        cost_estimate=pl.CostEstimate(
-            flops=2 * rows * columns * tokens,
-            bytes_accessed=2 * (rows + columns) * tokens + 4 * rows * columns,
-            transcendentals=0,
-        ),
+        cost_estimate=pl.CostEstimate(flops=0, bytes_accessed=0, transcendentals=0),
     )(*operands)
 
 
@@ -83,9 +80,9 @@
     outs = [None, None]
     now = []
 
-    def tie(value):
+    def tie(value, *others):
         held = [i for i in range(2) if outs[i] is not None]
-        done = lax.optimization_barrier((value, *[outs[i] for i in held], *now))
+        done = lax.optimization_barrier((value, *[outs[i] for i in held], *now, *others))
         for place_of, i in enumerate(held):
             outs[i] = done[1 + place_of]
         return done[0]
@@ -93,13 +90,13 @@
     def put(which, owner, block):
         outs[which] = product(tie(block), right_own, owner, outs[which], out_shape)
 
-    def put_arrived(which, owner, block):
+    def put_arrived(which, owner, block, first_row):
         outs[which] = lax.dynamic_update_slice(
-            outs[which], tie(block).astype(jnp.float32)[None, None], (owner, 0, 0, 0)
+            outs[which], block.astype(jnp.float32)[None, None], (owner, 0, first_row, 0)
         )
 
-    def gather(block):
-        return lax.all_gather(block, "narrow", axis=0, tiled=True)
+    def gather(block, *others):
+        return lax.all_gather(tie(block, *others), "narrow", axis=0, tiled=True)
 
     q = quantized_inputs
     d = (x_full.astype(jnp.float32) - q.astype(jnp.float32)).astype(jnp.bfloat16)
@@ -126,35 +123,41 @@
     right_next = [None, None]
     results = []
     for step in range(1, far + 1):
-        if arrivals(0, step):
-            now[:] = arrivals(0, step)
-            start(0, step + 1)
-            if step == 1:
+        for which in range(2):
+            if not arrivals(which, step):
+                continue
+            now[:] = arrivals(which, step)
+            start(which, step + 1)
+            if step == 1 and which == 0:
                 for way in range(2):
                     if raw[0, 1 - way] >= 1:
-                        right_next[way] = gather(tie(at[0, 1 - way][1]))
-        if arrivals(1, step):
-            now[:] = arrivals(1, step)
-            start(1, step + 1)
-        sent = []
-        for which in (1, 0):
-            for way in range(2):
-                if step == raw[which, way] < reach[which, way]:
-                    result = product(tie(at[which, way][step]), right_next[way])
-                    sent.append(result)
-                    results.append(
-                        (which, owner_of(way, step + 1), lax.ppermute(result, "wide", pairs[way]))
-                    )
-        now += sent
-        if step == 1:
-            put(0, lax.axis_index("wide"), q)
-            put(1, lax.axis_index("wide"), d)
-        for which in range(2):
-            for way in range(2):
-                if step <= raw[which, way]:
-                    put(which, owner_of(way, step), at[which, way][step])
-    now[:] = []
-    for result in results:
+                        right_next[way] = gather(at[0, 1 - way][1], d)
+            together = step in (1, far - 1)
+            if which == 0 and together:
+                continue
+            if which == 1:
+                for sent, way in ((1, 0), (0, 1), (1, 1), (0, 0)):
+                    if step == raw[sent, way] < reach[sent, way]:
+                        pieces = LAST_PIECES if step == far - 1 else 1
+                        for i in range(pieces):
+                            result = product(
+                                tie(at[sent, way][step]), right_next[way], piece=i, pieces=pieces
+                            )
+                            now.append(result)
+                            results.append((
+                                sent,
+                                owner_of(way, step + 1),
+                                lax.ppermute(result, "wide", pairs[way]),
+                                i * owned_rows // pieces,
+                            ))
+            if step == 1:
+                put(0, lax.axis_index("wide"), q)
+                put(1, lax.axis_index("wide"), d)
+            for own in range(2) if together else (which,):
+                for way in range(2):
+                    if step <= raw[own, way]:
+                        put(own, owner_of(way, step), at[own, way][step])
+    for result in sorted(results, key=lambda result: result[3]):
         put_arrived(*result)
     return tuple(outs)
 

time: 463 us -> 459 us (level)
  waiting for transfers between devices: 206 us -> 199 us
  local copies, waits for them, and re-layouts: 30.6 us -> 24.2 us
    ppermute x10, waiting for transfers between devices: 187 us -> 172 us  [start(): at[chain].append(lax.ppermute(block, 'wide', pairs[way]))]
    ppermute x4 -> x6, waiting for transfers between devices: 17.5 us -> 25.2 us  [per_device(): lax.ppermute(result, 'wide', pairs[way])]
    unnamed x30 -> x32, local copies, waits for them, and re-layouts: 29.3 us -> 22.9 us
    pallas_call x16 -> x18, Pallas kernels: 163 us -> 167 us  [product(): pl.pallas_call(functools.partial(product_kernel, 1.0 / tokens), out_shape...]
    dynamic_update_slice x4 -> x6, other arithmetic: 14.9 us -> 18.2 us  [put_arrived(): lax.dynamic_update_slice(outs[which], block.astype(jnp.float32)[None, Non...]
  transfers between devices with their start and end apart: 17 -> 19, of which waited for: 6 -> 8; matrix products, arithmetic and copies ran while one was open for 4% -> 5% of each run, Pallas kernels for 35% -> 36%
where the time goes in v3:
time: 459 us; the launch traced here: 458 us
  waiting for transfers between devices  199 us (43%)
  Pallas kernels  167 us (36%)
  between operations  26.7 us (6%)
  local copies, waits for them, and re-layouts  24.2 us (5%)
  other arithmetic  23.8 us (5%)
  starting transfers between devices  17.5 us (4%)
    ppermute x10, waiting for transfers between devices, start(): at[chain].append(lax.ppermute(block, 'wide', pairs[way]))  172 us
    pallas_call x18, Pallas kernels, product(): pl.pallas_call(functools.partial(product_kernel, 1.0 / tokens), out_shape...  167 us
    ppermute x6, waiting for transfers between devices, per_device(): lax.ppermute(result, 'wide', pairs[way])  25.2 us
    unnamed x32, local copies, waits for them, and re-layouts  22.9 us
    dynamic_update_slice x6, other arithmetic, put_arrived(): lax.dynamic_update_slice(outs[which], block.astype(jnp.float32)[None, Non...  18.2 us
    ppermute x10, starting transfers between devices, start(): at[chain].append(lax.ppermute(block, 'wide', pairs[way]))  11.2 us
  transfers between devices with their start and end apart: 19, of which 8 were waited for; matrix products, arithmetic and copies ran while one was open for 5% of the time, Pallas kernels for 36%

profile of v3, /device:TPU:0, one launch (start us, length us, event | category | flops | bytes accessed | tf_op | source)
XLA Modules:
  0.0 457.5 jit_solution(845350774924412273)
XLA Ops:
  7.2 0.0 copy-start.9
  7.2 0.0 copy-start.8
  7.2 0.0 all-gather.4.cloned.1.call-start
  7.2 0.7 all-gather.4.cloned.1.call-update
  7.9 0.0 all-gather.6.cloned.1.call-start
  8.0 3.1 collective-permute-start.4
  11.1 0.0 collective-permute-start.3
  11.1 5.6 %subtract_convert_fusion.left_ref = bf16[512,3072]{1,0:T(8,128)(2,1)} fusion(bf16[512,3072]{1,0:T(8,128)(2,1)} %left_ref, bf16[512,3072]{1,0:T(8,128)(2,1)} %param.20), kind=kLoop, calls=%fused_computation | loop fusion | flops 6291456 | bytes 9437184 | tf_op jit(solution)/shard_map/convert_element_type | solution.py:102
  16.7 62.7 %collective-permute-done.4.left_ref = bf16[512,3072]{1,0:T(8,128)(2,1)} collective-permute-done((bf16[512,3072]{1,0:T(8,128)(2,1)}, bf16[512,3072]{1,0:T(8,128)(2,1)}, u32[]{:S(2)}, u32[]{:S(2)}) %collective-permute-start.4) | collective-permute-done | bytes 3145760 | tf_op jit(solution)/shard_map/ppermute | solution.py:116
  79.4 1.5 collective-permute-done.3.left_ref
  80.9 0.0 all-gather.6.cloned.1.call-update
  81.0 0.0 all-gather.8.cloned.1.call-start
  81.0 0.7 all-gather.8.cloned.1.call-update
  81.7 0.4 collective-permute-start
  82.1 1.7 collective-permute-start.1
  83.8 0.3 collective-permute-start.5
  84.1 1.7 collective-permute-start.6
  85.8 67.3 %collective-permute-done.left_ref = bf16[512,3072]{1,0:T(8,128)(2,1)} collective-permute-done((bf16[512,3072]{1,0:T(8,128)(2,1)}, bf16[512,3072]{1,0:T(8,128)(2,1)}, u32[]{:S(2)}, u32[]{:S(2)}) %collective-permute-start) | collective-permute-done | bytes 3145760 | tf_op jit(solution)/shard_map/ppermute | solution.py:116
  153.1 0.3 collective-permute-done.1.left_ref
  153.4 1.7 collective-permute-start.7
  155.1 0.3 collective-permute-start.2
  155.4 0.6 dynamic_slice.51
  161.4 0.7 fusion
  162.1 4.6 copy-done
  166.7 8.3 %shard_map.194.refs_0_ = f32[8,1,512,2048]{3,2,1,0:T(8,128)} custom-call(s32[1]{0:T(128)} %bitcast.4.place_ref, bf16[512,3072]{1,0:T(8,128)(2,1)S(1)} %copy-done.6, bf16[2048,3072]{1,0:T(8,128)(2,1)S(1)} %copy-done), custom_call_target="tpu_custom_call" | custom-call | tf_op jit(solution)/shard_map/pallas_call | solution.py:46
  175.0 8.3 %shard_map.195.refs_0_ = f32[8,1,512,2048]{3,2,1,0:T(8,128)} custom-call(s32[1]{0:T(128)} %bitcast.4.place_ref, bf16[512,3072]{1,0:T(8,128)(2,1)S(1)} %copy-done.7, bf16[2048,3072]{1,0:T(8,128)(2,1)S(1)} %copy-done.1), custom_call_target="tpu_custom_call" | custom-call | tf_op jit(solution)/shard_map/pallas_call | solution.py:46
  183.3 11.0 %shard_map.196.refs_0_ = f32[8,1,512,2048]{3,2,1,0:T(8,128)} custom-call(s32[1]{0:T(128)} %get-tuple-element.130.place_ref, bf16[512,3072]{1,0:T(8,128)(2,1)} %collective-permute-done.4.left_ref, bf16[2048,3072]{1,0:T(8,128)(2,1)S(1)} %copy-done.1, f32[8,1,512,2048]{3,2,1,0:T(8,128)} %shard_map.194.refs_0_), custom_call_target="tpu_custom_call", output_to_operand_aliasing={{}: (3, {})} | custom-call | tf_op jit(solution)/shard_map/pallas_call | solution.py:46
  194.3 11.0 %shard_map.197.refs_0_ = f32[8,1,512,2048]{3,2,1,0:T(8,128)} custom-call(s32[1]{0:T(128)} %get-tuple-element.131.place_ref, bf16[512,3072]{1,0:T(8,128)(2,1)} %collective-permute-done.3.left_ref, bf16[2048,3072]{1,0:T(8,128)(2,1)S(1)} %copy-done.1, f32[8,1,512,2048]{3,2,1,0:T(8,128)} %shard_map.196.refs_0_), custom_call_target="tpu_custom_call", output_to_operand_aliasing={{}: (3, {})} | custom-call | tf_op jit(solution)/shard_map/pallas_call | solution.py:46
  205.3 10.8 %shard_map.198.refs_0_ = f32[8,1,512,2048]{3,2,1,0:T(8,128)} custom-call(s32[1]{0:T(128)} %get-tuple-element.130.place_ref, bf16[512,3072]{1,0:T(8,128)(2,1)} %collective-permute-done.1.left_ref, bf16[2048,3072]{1,0:T(8,128)(2,1)S(1)} %copy-done.1, f32[8,1,512,2048]{3,2,1,0:T(8,128)} %shard_map.195.refs_0_), custom_call_target="tpu_custom_call", output_to_operand_aliasing={{}: (3, {})} | custom-call | tf_op jit(solution)/shard_map/pallas_call | solution.py:46
  216.1 10.8 %shard_map.199.refs_0_ = f32[8,1,512,2048]{3,2,1,0:T(8,128)} custom-call(s32[1]{0:T(128)} %get-tuple-element.131.place_ref, bf16[512,3072]{1,0:T(8,128)(2,1)} %collective-permute-done.left_ref, bf16[2048,3072]{1,0:T(8,128)(2,1)S(1)} %copy-done.1, f32[8,1,512,2048]{3,2,1,0:T(8,128)} %shard_map.198.refs_0_), custom_call_target="tpu_custom_call", output_to_operand_aliasing={{}: (3, {})} | custom-call | tf_op jit(solution)/shard_map/pallas_call | solution.py:46
  226.9 10.9 %shard_map.200.refs_0_ = f32[8,1,512,2048]{3,2,1,0:T(8,128)} custom-call(s32[1]{0:T(128)} %get-tuple-element.132.place_ref, bf16[512,3072]{1,0:T(8,128)(2,1)} %collective-permute-done.6.left_ref, bf16[2048,3072]{1,0:T(8,128)(2,1)S(1)} %copy-done.1, f32[8,1,512,2048]{3,2,1,0:T(8,128)} %shard_map.197.refs_0_), custom_call_target="tpu_custom_call", output_to_operand_aliasing={{}: (3, {})} | custom-call | tf_op jit(solution)/shard_map/pallas_call | solution.py:46
  237.8 10.9 %shard_map.201.refs_0_ = f32[8,1,512,2048]{3,2,1,0:T(8,128)} custom-call(s32[1]{0:T(128)} %get-tuple-element.133.place_ref, bf16[512,3072]{1,0:T(8,128)(2,1)} %collective-permute-done.5.left_ref, bf16[2048,3072]{1,0:T(8,128)(2,1)S(1)} %copy-done.1, f32[8,1,512,2048]{3,2,1,0:T(8,128)} %shard_map.200.refs_0_), custom_call_target="tpu_custom_call", output_to_operand_aliasing={{}: (3, {})} | custom-call | tf_op jit(solution)/shard_map/pallas_call | solution.py:46
  248.7 37.1 %collective-permute-done.7.left_ref = bf16[512,3072]{1,0:T(8,128)(2,1)} collective-permute-done((bf16[512,3072]{1,0:T(8,128)(2,1)}, bf16[512,3072]{1,0:T(8,128)(2,1)}, u32[]{:S(2)}, u32[]{:S(2)}) %collective-permute-start.7) | collective-permute-done | bytes 3145760 | tf_op jit(solution)/shard_map/ppermute | solution.py:116
  285.9 1.5 collective-permute-start.8
  287.4 0.5 collective-permute-start.9
  287.9 4.6 copy-done.3
  292.5 10.1 %shard_map.202 = bf16[512,2048]{1,0:T(8,128)(2,1)} custom-call(s32[1]{0:T(128)} %constant.99.clone.1.place_ref, bf16[512,3072]{1,0:T(8,128)(2,1)} %collective-permute-done.7.left_ref, bf16[2048,3072]{1,0:T(8,128)(2,1)S(1)} %copy-done.3), custom_call_target="tpu_custom_call" | custom-call | tf_op jit(solution)/shard_map/pallas_call | solution.py:46
  302.6 1.4 collective-permute-start.13
  304.0 4.6 copy-done.5
  308.5 10.1 %shard_map.203 = bf16[512,2048]{1,0:T(8,128)(2,1)} custom-call(s32[1]{0:T(128)} %constant.99.clone.1.place_ref, bf16[512,3072]{1,0:T(8,128)(2,1)} %collective-permute-done.5.left_ref, bf16[2048,3072]{1,0:T(8,128)(2,1)S(1)} %copy-done.5), custom_call_target="tpu_custom_call" | custom-call | tf_op jit(solution)/shard_map/pallas_call | solution.py:46
  318.6 0.6 collective-permute-start.10
  326.7 4.6 copy-done.2
  331.3 11.5 %shard_map.204.refs_0_ = f32[8,1,512,2048]{3,2,1,0:T(8,128)} custom-call(s32[1]{0:T(128)} %get-tuple-element.132.place_ref, bf16[512,3072]{1,0:T(8,128)(2,1)} %collective-permute-done.7.left_ref, bf16[2048,3072]{1,0:T(8,128)(2,1)S(1)} %copy-done.2, f32[8,1,512,2048]{3,2,1,0:T(8,128)} %shard_map.199.refs_0_), custom_call_target="tpu_custom_call", output_to_operand_aliasing={{}: (3, {})} | custom-call | tf_op jit(solution)/shard_map/pallas_call | solution.py:46
  342.8 11.3 %shard_map.205.refs_0_ = f32[8,1,512,2048]{3,2,1,0:T(8,128)} custom-call(s32[1]{0:T(128)} %get-tuple-element.133.place_ref, bf16[512,3072]{1,0:T(8,128)(2,1)} %collective-permute-done.2.left_ref, bf16[2048,3072]{1,0:T(8,128)(2,1)S(1)} %copy-done.2, f32[8,1,512,2048]{3,2,1,0:T(8,128)} %shard_map.204.refs_0_), custom_call_target="tpu_custom_call", output_to_operand_aliasing={{}: (3, {})} | custom-call | tf_op jit(solution)/shard_map/pallas_call | solution.py:46
  354.0 3.1 collective-permute-done.8.left_ref
  357.2 4.8 %shard_map.206 = bf16[256,2048]{1,0:T(8,128)(2,1)} custom-call(s32[1]{0:T(128)} %constant.99.clone.1.place_ref, bf16[512,3072]{1,0:T(8,128)(2,1)S(1)} %collective-permute-done.8.left_ref, bf16[2048,3072]{1,0:T(8,128)(2,1)S(1)} %bitcast.34), custom_call_target="tpu_custom_call" | custom-call | tf_op jit(solution)/shard_map/pallas_call | solution.py:46
  362.0 1.5 collective-permute-start.14
  363.5 4.8 %shard_map.207 = bf16[256,2048]{1,0:T(8,128)(2,1)} custom-call(s32[1]{0:T(128)} %constant.99.clone.1.place_ref, bf16[512,3072]{1,0:T(8,128)(2,1)S(1)} %collective-permute-done.8.left_ref, bf16[2048,3072]{1,0:T(8,128)(2,1)S(1)} %bitcast.34), custom_call_target="tpu_custom_call" | custom-call | tf_op jit(solution)/shard_map/pallas_call | solution.py:46
  368.3 1.6 collective-permute-start.15
  369.9 4.6 copy-done.4
  374.5 6.4 %shard_map.208 = bf16[256,2048]{1,0:T(8,128)(2,1)} custom-call(s32[1]{0:T(128)} %constant.99.clone.1.place_ref, bf16[512,3072]{1,0:T(8,128)(2,1)} %collective-permute-done.9.left_ref, bf16[2048,3072]{1,0:T(8,128)(2,1)S(1)} %copy-done.4), custom_call_target="tpu_custom_call" | custom-call | tf_op jit(solution)/shard_map/pallas_call | solution.py:46
  380.9 0.5 collective-permute-start.11
  381.3 5.8 %shard_map.209 = bf16[256,2048]{1,0:T(8,128)(2,1)S(1)} custom-call(s32[1]{0:T(128)} %constant.99.clone.1.place_ref, bf16[512,3072]{1,0:T(8,128)(2,1)} %collective-permute-done.9.left_ref, bf16[2048,3072]{1,0:T(8,128)(2,1)S(1)} %copy-done.4), custom_call_target="tpu_custom_call" | custom-call | tf_op jit(solution)/shard_map/pallas_call | solution.py:46
  387.1 10.9 %shard_map.210 = f32[8,1,512,2048]{3,2,1,0:T(8,128)} custom-call(s32[1]{0:T(128)} %get-tuple-element.135.place_ref, bf16[512,3072]{1,0:T(8,128)(2,1)} %collective-permute-done.9.left_ref, bf16[2048,3072]{1,0:T(8,128)(2,1)S(1)} %bitcast.32, f32[8,1,512,2048]{3,2,1,0:T(8,128)} %shard_map.201.refs_0_), custom_call_target="tpu_custom_call", output_to_operand_aliasing={{}: (3, {})} | custom-call | tf_op jit(solution)/shard_map/pallas_call | solution.py:46
  398.0 9.0 %shard_map.211 = f32[8,1,512,2048]{3,2,1,0:T(8,128)} custom-call(s32[1]{0:T(128)} %get-tuple-element.134.place_ref, bf16[512,3072]{1,0:T(8,128)(2,1)S(1)} %collective-permute-done.8.left_ref, bf16[2048,3072]{1,0:T(8,128)(2,1)S(1)} %bitcast.32, f32[8,1,512,2048]{3,2,1,0:T(8,128)} %shard_map.205.refs_0_), custom_call_target="tpu_custom_call", output_to_operand_aliasing={{}: (3, {})} | custom-call | tf_op jit(solution)/shard_map/pallas_call | solution.py:46
  407.0 0.6 collective-permute-start.12
  407.6 4.1 convert_dynamic-update-slice_fusion
  411.7 4.1 convert_dynamic-update-slice_fusion.1
  415.8 8.8 %collective-permute-done.14 = bf16[256,2048]{1,0:T(8,128)(2,1)} collective-permute-done((bf16[256,2048]{1,0:T(8,128)(2,1)}, bf16[256,2048]{1,0:T(8,128)(2,1)}, u32[]{:S(2)}, u32[]{:S(2)}) %collective-permute-start.14) | collective-permute-done | bytes 1048608 | tf_op jit(solution)/shard_map/ppermute | solution.py:150
  424.7 2.8 convert_dynamic-update-slice_fusion.3
  427.5 16.4 %collective-permute-done.15 = bf16[256,2048]{1,0:T(8,128)(2,1)} collective-permute-done((bf16[256,2048]{1,0:T(8,128)(2,1)}, bf16[256,2048]{1,0:T(8,128)(2,1)}, u32[]{:S(2)}, u32[]{:S(2)}) %collective-permute-start.15) | collective-permute-done | bytes 1048608 | tf_op jit(solution)/shard_map/ppermute | solution.py:150
  443.9 2.8 convert_dynamic-update-slice_fusion.2
  446.7 2.8 convert_dynamic-update-slice_fusion.5
  449.4 1.6 convert_dynamic-update-slice_fusion.4
  (38 shorter events, 0.1 us)
Async XLA Ops:
  7.2 148.3 %copy-start.9 = (s32[8]{0:T(128)S(1)}, s32[8]{0:T(128)}, u32[]{:S(2)}) copy-start(s32[8]{0:T(128)} %constant.104.clone) | copy-start | bytes 100
  7.2 154.2 %copy-start.8 = (s32[8]{0:T(128)S(1)}, s32[8]{0:T(128)}, u32[]{:S(2)}) copy-start(s32[8]{0:T(128)} %constant.105.clone) | copy-start | bytes 100
  7.2 154.9 %copy-start.6 = (bf16[512,3072]{1,0:T(8,128)(2,1)S(1)}, bf16[512,3072]{1,0:T(8,128)(2,1)}, u32[]{:S(2)}) copy-start(bf16[512,3072]{1,0:T(8,128)(2,1)} %left_ref) | copy-start | bytes 9437188
  7.2 154.9 %all-gather.4.cloned.1.call-start = ((), (), s32[]{:S(2)}) async-start(), calls=%async_computation | async-start | bytes 15728640 | tf_op jit(solution)/shard_map/all_gather | solution.py:99
  7.9 280.0 %all-gather.6.cloned.1.call-start = ((), (), s32[]{:S(2)}) async-start(), calls=%async_computation.1 | async-start | bytes 15728640 | tf_op jit(solution)/shard_map/all_gather | solution.py:99
  8.0 71.4 %collective-permute-start.4 = (bf16[512,3072]{1,0:T(8,128)(2,1)}, bf16[512,3072]{1,0:T(8,128)(2,1)}, u32[]{:S(2)}, u32[]{:S(2)}) collective-permute-start(bf16[512,3072]{1,0:T(8,128)(2,1)} %left_ref), channel_id=1, source_target_pairs={{0,8},{8,16},{16,24},{24,28},{28,20},{20,12},{12,4},{4,0},{1,9},{9... | collective-permute-start | bytes 9437192 | tf_op jit(solution)/shard_map/ppermute | solution.py:116
  11.1 69.9 %collective-permute-start.3 = (bf16[512,3072]{1,0:T(8,128)(2,1)}, bf16[512,3072]{1,0:T(8,128)(2,1)}, u32[]{:S(2)}, u32[]{:S(2)}) collective-permute-start(bf16[512,3072]{1,0:T(8,128)(2,1)} %left_ref), channel_id=1, source_target_pairs={{8,0},{16,8},{24,16},{28,24},{20,28},{12,20},{4,12},{0,4},{9,1},{1... | collective-permute-start | bytes 9437192 | tf_op jit(solution)/shard_map/ppermute | solution.py:116
  81.0 223.0 %all-gather.8.cloned.1.call-start = ((), (), s32[]{:S(2)}) async-start(), calls=%async_computation.2 | async-start | bytes 15728640 | tf_op jit(solution)/shard_map/all_gather | solution.py:99
  81.7 71.4 %collective-permute-start = (bf16[512,3072]{1,0:T(8,128)(2,1)}, bf16[512,3072]{1,0:T(8,128)(2,1)}, u32[]{:S(2)}, u32[]{:S(2)}) collective-permute-start(bf16[512,3072]{1,0:T(8,128)(2,1)} %subtract_convert_fusion.left_ref), channel_id=1, source_target_pairs={{8,0},{16,8},{24,16},{28,24},{20,28},{12,20},{4,12},{0,4},{9,1},{1... | collective-permute-start | bytes 9437192 | tf_op jit(solution)/shard_map/ppermute | solution.py:116
  82.1 71.4 %collective-permute-start.1 = (bf16[512,3072]{1,0:T(8,128)(2,1)}, bf16[512,3072]{1,0:T(8,128)(2,1)}, u32[]{:S(2)}, u32[]{:S(2)}) collective-permute-start(bf16[512,3072]{1,0:T(8,128)(2,1)} %subtract_convert_fusion.left_ref), channel_id=1, source_target_pairs={{0,8},{8,16},{16,24},{24,28},{28,20},{20,12},{12,4},{4,0},{1,9},{9... | collective-permute-start | bytes 9437192 | tf_op jit(solution)/shard_map/ppermute | solution.py:116
  83.8 143.2 %collective-permute-start.5 = (bf16[512,3072]{1,0:T(8,128)(2,1)}, bf16[512,3072]{1,0:T(8,128)(2,1)}, u32[]{:S(2)}, u32[]{:S(2)}) collective-permute-start(bf16[512,3072]{1,0:T(8,128)(2,1)} %collective-permute-done.3.left_ref), channel_id=1, source_target_pairs={{8,0},{16,8},{24,16},{28,24},{20,28},{12,20},{4,12},{0,4},{9,1},{1... | collective-permute-start | bytes 9437192 | tf_op jit(solution)/shard_map/ppermute | solution.py:116
  84.1 142.9 %collective-permute-start.6 = (bf16[512,3072]{1,0:T(8,128)(2,1)}, bf16[512,3072]{1,0:T(8,128)(2,1)}, u32[]{:S(2)}, u32[]{:S(2)}) collective-permute-start(bf16[512,3072]{1,0:T(8,128)(2,1)} %collective-permute-done.4.left_ref), channel_id=1, source_target_pairs={{0,8},{8,16},{16,24},{24,28},{28,20},{20,12},{12,4},{4,0},{1,9},{9... | collective-permute-start | bytes 9437192 | tf_op jit(solution)/shard_map/ppermute | solution.py:116
  153.4 132.5 %collective-permute-start.7 = (bf16[512,3072]{1,0:T(8,128)(2,1)}, bf16[512,3072]{1,0:T(8,128)(2,1)}, u32[]{:S(2)}, u32[]{:S(2)}) collective-permute-start(bf16[512,3072]{1,0:T(8,128)(2,1)} %collective-permute-done.1.left_ref), channel_id=1, source_target_pairs={{0,8},{8,16},{16,24},{24,28},{28,20},{20,12},{12,4},{4,0},{1,9},{9... | collective-permute-start | bytes 9437192 | tf_op jit(solution)/shard_map/ppermute | solution.py:116
  155.1 130.8 %collective-permute-start.2 = (bf16[512,3072]{1,0:T(8,128)(2,1)}, bf16[512,3072]{1,0:T(8,128)(2,1)}, u32[]{:S(2)}, u32[]{:S(2)}) collective-permute-start(bf16[512,3072]{1,0:T(8,128)(2,1)} %collective-permute-done.left_ref), channel_id=1, source_target_pairs={{8,0},{16,8},{24,16},{28,24},{20,28},{12,20},{4,12},{0,4},{9,1},{1... | collective-permute-start | bytes 9437192 | tf_op jit(solution)/shard_map/ppermute | solution.py:116
  162.1 4.6 %copy-start = (bf16[2048,3072]{1,0:T(8,128)(2,1)S(1)}, bf16[2048,3072]{1,0:T(8,128)(2,1)}, u32[]{:S(2)}) copy-start(bf16[2048,3072]{1,0:T(8,128)(2,1)} %all-gather.4.cloned.1.call-done.right_ref) | copy-start | bytes 37748740
  166.7 8.3 %copy-start.1 = (bf16[2048,3072]{1,0:T(8,128)(2,1)S(1)}, bf16[2048,3072]{1,0:T(8,128)(2,1)}, u32[]{:S(2)}) copy-start(bf16[2048,3072]{1,0:T(8,128)(2,1)} %all-gather.4.cloned.1.call-done.right_ref) | copy-start | bytes 37748740
  166.7 8.3 %copy-start.7 = (bf16[512,3072]{1,0:T(8,128)(2,1)S(1)}, bf16[512,3072]{1,0:T(8,128)(2,1)}, u32[]{:S(2)}) copy-start(bf16[512,3072]{1,0:T(8,128)(2,1)} %subtract_convert_fusion.left_ref) | copy-start | bytes 9437188
  285.9 71.2 %collective-permute-start.8 = (bf16[512,3072]{1,0:T(8,128)(2,1)}, bf16[512,3072]{1,0:T(8,128)(2,1)S(1)}, u32[]{:S(2)}, u32[]{:S(2)}) collective-permute-start(bf16[512,3072]{1,0:T(8,128)(2,1)} %collective-permute-done.2.left_ref), channel_id=1, source_target_pairs={{8,0},{16,8},{24,16},{28,24},{20,28},{12,20},{4,12},{0,4},{9,1},{1... | collective-permute-start | bytes 9437192 | tf_op jit(solution)/shard_map/ppermute | solution.py:116
  287.4 82.5 %collective-permute-start.9 = (bf16[512,3072]{1,0:T(8,128)(2,1)}, bf16[512,3072]{1,0:T(8,128)(2,1)}, u32[]{:S(2)}, u32[]{:S(2)}) collective-permute-start(bf16[512,3072]{1,0:T(8,128)(2,1)} %collective-permute-done.6.left_ref), channel_id=1, source_target_pairs={{0,8},{8,16},{16,24},{24,28},{28,20},{20,12},{12,4},{4,0},{1,9},{9... | collective-permute-start | bytes 9437192 | tf_op jit(solution)/shard_map/ppermute | solution.py:116
  287.9 4.6 %copy-start.3 = (bf16[2048,3072]{1,0:T(8,128)(2,1)S(1)}, bf16[2048,3072]{1,0:T(8,128)(2,1)}, u32[]{:S(2)}) copy-start(bf16[2048,3072]{1,0:T(8,128)(2,1)} %all-gather.6.cloned.1.call-done.right_ref) | copy-start | bytes 37748740
  302.6 104.4 %collective-permute-start.13 = (bf16[512,2048]{1,0:T(8,128)(2,1)}, bf16[512,2048]{1,0:T(8,128)(2,1)}, u32[]{:S(2)}, u32[]{:S(2)}) collective-permute-start(bf16[512,2048]{1,0:T(8,128)(2,1)} %shard_map.202), channel_id=1, source_target_pairs={{0,8},{8,16},{16,24},{24,28},{28,20},{20,12},{12,4},{4,0},{1,9},{9... | collective-permute-start | bytes 6291464 | tf_op jit(solution)/shard_map/ppermute | solution.py:150
  304.0 4.6 %copy-start.5 = (bf16[2048,3072]{1,0:T(8,128)(2,1)S(1)}, bf16[2048,3072]{1,0:T(8,128)(2,1)}, u32[]{:S(2)}) copy-start(bf16[2048,3072]{1,0:T(8,128)(2,1)} %all-gather.8.cloned.1.call-done.right_ref) | copy-start | bytes 37748740
  318.6 93.1 %collective-permute-start.10 = (bf16[512,2048]{1,0:T(8,128)(2,1)}, bf16[512,2048]{1,0:T(8,128)(2,1)}, u32[]{:S(2)}, u32[]{:S(2)}) collective-permute-start(bf16[512,2048]{1,0:T(8,128)(2,1)} %shard_map.203), channel_id=1, source_target_pairs={{8,0},{16,8},{24,16},{28,24},{20,28},{12,20},{4,12},{0,4},{9,1},{1... | collective-permute-start | bytes 6291464 | tf_op jit(solution)/shard_map/ppermute | solution.py:150
  326.7 4.6 %copy-start.2 = (bf16[2048,3072]{1,0:T(8,128)(2,1)S(1)}, bf16[2048,3072]{1,0:T(8,128)(2,1)}, u32[]{:S(2)}) copy-start(bf16[2048,3072]{1,0:T(8,128)(2,1)} %all-gather.4.cloned.1.call-done.right_ref) | copy-start | bytes 37748740
  331.3 25.9 %slice-start.3 = ((s8[12582912]{0:T(1024)(128)(4,1)}), s8[4194304]{0:T(1024)(128)(4,1)S(1)}, s32[]{:S(2)}) async-start(s8[12582912]{0:T(1024)(128)(4,1)} %bitcast.33), calls=%async_computation.6 | async-start | bytes 8388608
  331.3 25.9 %slice-start.4 = ((s8[12582912]{0:T(1024)(128)(4,1)}), s8[4194304]{0:T(1024)(128)(4,1)S(1)}, s32[]{:S(2)}) async-start(s8[12582912]{0:T(1024)(128)(4,1)} %bitcast.33), calls=%async_computation.7 | async-start | bytes 8388608
  342.8 14.4 %slice-start.5 = ((s8[12582912]{0:T(1024)(128)(4,1)}), s8[4194304]{0:T(1024)(128)(4,1)S(1)}, s32[]{:S(2)}) async-start(s8[12582912]{0:T(1024)(128)(4,1)} %bitcast.33), calls=%async_computation.8 | async-start | bytes 8388608
  362.0 62.7 %collective-permute-start.14 = (bf16[256,2048]{1,0:T(8,128)(2,1)}, bf16[256,2048]{1,0:T(8,128)(2,1)}, u32[]{:S(2)}, u32[]{:S(2)}) collective-permute-start(bf16[256,2048]{1,0:T(8,128)(2,1)} %shard_map.206), channel_id=1, source_target_pairs={{8,0},{16,8},{24,16},{28,24},{20,28},{12,20},{4,12},{0,4},{9,1},{1... | collective-permute-start | bytes 3145736 | tf_op jit(solution)/shard_map/ppermute | solution.py:150
  368.3 75.6 %collective-permute-start.15 = (bf16[256,2048]{1,0:T(8,128)(2,1)}, bf16[256,2048]{1,0:T(8,128)(2,1)}, u32[]{:S(2)}, u32[]{:S(2)}) collective-permute-start(bf16[256,2048]{1,0:T(8,128)(2,1)} %shard_map.207), channel_id=1, source_target_pairs={{8,0},{16,8},{24,16},{28,24},{20,28},{12,20},{4,12},{0,4},{9,1},{1... | collective-permute-start | bytes 3145736 | tf_op jit(solution)/shard_map/ppermute | solution.py:150
  369.9 4.6 %copy-start.4 = (bf16[2048,3072]{1,0:T(8,128)(2,1)S(1)}, bf16[2048,3072]{1,0:T(8,128)(2,1)}, u32[]{:S(2)}) copy-start(bf16[2048,3072]{1,0:T(8,128)(2,1)} %all-gather.6.cloned.1.call-done.right_ref) | copy-start | bytes 37748740
  374.5 12.7 %slice-start = ((s8[12582912]{0:T(1024)(128)(4,1)}), s8[4194304]{0:T(1024)(128)(4,1)S(1)}, s32[]{:S(2)}) async-start(s8[12582912]{0:T(1024)(128)(4,1)} %bitcast.31), calls=%async_computation.3 | async-start | bytes 8388608
  374.5 12.7 %slice-start.1 = ((s8[12582912]{0:T(1024)(128)(4,1)}), s8[4194304]{0:T(1024)(128)(4,1)S(1)}, s32[]{:S(2)}) async-start(s8[12582912]{0:T(1024)(128)(4,1)} %bitcast.31), calls=%async_computation.4 | async-start | bytes 8388608
  380.9 6.3 %slice-start.2 = ((s8[12582912]{0:T(1024)(128)(4,1)}), s8[4194304]{0:T(1024)(128)(4,1)S(1)}, s32[]{:S(2)}) async-start(s8[12582912]{0:T(1024)(128)(4,1)} %bitcast.31), calls=%async_computation.5 | async-start | bytes 8388608
  380.9 65.8 %collective-permute-start.11 = (bf16[256,2048]{1,0:T(8,128)(2,1)}, bf16[256,2048]{1,0:T(8,128)(2,1)}, u32[]{:S(2)}, u32[]{:S(2)}) collective-permute-start(bf16[256,2048]{1,0:T(8,128)(2,1)} %shard_map.208), channel_id=1, source_target_pairs={{0,8},{8,16},{16,24},{24,28},{28,20},{20,12},{12,4},{4,0},{1,9},{9... | collective-permute-start | bytes 3145736 | tf_op jit(solution)/shard_map/ppermute | solution.py:150
  407.0 42.5 %collective-permute-start.12 = (bf16[256,2048]{1,0:T(8,128)(2,1)S(1)}, bf16[256,2048]{1,0:T(8,128)(2,1)S(1)}, u32[]{:S(2)}, u32[]{:S(2)}) collective-permute-start(bf16[256,2048]{1,0:T(8,128)(2,1)S(1)} %shard_map.209), channel_id=1, source_target_pairs={{0,8},{8,16},{16,24},{24,28},{28,20},{20,12},{12,4},{4,0},{1,9},{9... | collective-permute-start | bytes 3145736 | tf_op jit(solution)/shard_map/ppermute | solution.py:150
Sparse Core Ops, SparseCore 0:
  9.6 84.7 all-gather.3
  96.0 82.0 all-gather.5
  179.7 82.0 all-gather.7

commit v4 on v3

--- a/solution.py
+++ b/solution.py
@@ -8,7 +8,7 @@
 from jax.sharding import PartitionSpec as P
 
 TILE = 512
-LAST_PIECES = 2
+QUARTERS = 4
 
 
 def product_kernel(scale, place_ref, left_ref, right_ref, *refs):
@@ -22,8 +22,8 @@
     result_ref[...] = (total * scale).astype(result_ref.dtype).reshape(result_ref.shape)
 
 
-def product(left, right, owner=None, out=None, out_shape=None, piece=0, pieces=1):
-    rows, tokens = left.shape[0] // pieces, left.shape[1]
+def product(left, right, owner=None, out=None, out_shape=None, first_row=0, rows=None):
+    rows, tokens = rows or left.shape[0], left.shape[1]
     columns = right.shape[0]
     tile = min(TILE, columns)
     if owner is None:
@@ -34,7 +34,7 @@
         out_spec = pl.BlockSpec((1, 1, rows, tile), lambda j, at: (at[0], 0, 0, j))
         shape = jax.ShapeDtypeStruct(out_shape, jnp.float32)
     in_specs = [
-        pl.BlockSpec((rows, tokens), lambda j, at: (piece, 0)),
+        pl.BlockSpec((rows, tokens), lambda j, at: (first_row // rows, 0)),
         pl.BlockSpec((tile, tokens), lambda j, at: (j, 0)),
     ]
     operands = [jnp.asarray(owner, jnp.int32).reshape(1), left, right]
@@ -92,7 +92,7 @@
 
     def put_arrived(which, owner, block, first_row):
         outs[which] = lax.dynamic_update_slice(
-            outs[which], block.astype(jnp.float32)[None, None], (owner, 0, first_row, 0)
+            outs[which], tie(block).astype(jnp.float32)[None, None], (owner, 0, first_row, 0)
         )
 
     def gather(block, *others):
@@ -138,17 +138,22 @@
             if which == 1:
                 for sent, way in ((1, 0), (0, 1), (1, 1), (0, 0)):
                     if step == raw[sent, way] < reach[sent, way]:
-                        pieces = LAST_PIECES if step == far - 1 else 1
-                        for i in range(pieces):
+                        cut = owned_rows - owned_rows // QUARTERS if step == far - 1 else owned_rows
+                        for first_row, rows in ((0, cut), (cut, owned_rows - cut)):
+                            if rows == 0:
+                                continue
                             result = product(
-                                tie(at[sent, way][step]), right_next[way], piece=i, pieces=pieces
+                                tie(at[sent, way][step]),
+                                right_next[way],
+                                first_row=first_row,
+                                rows=rows,
                             )
                             now.append(result)
                             results.append((
                                 sent,
                                 owner_of(way, step + 1),
                                 lax.ppermute(result, "wide", pairs[way]),
-                                i * owned_rows // pieces,
+                                first_row,
                             ))
             if step == 1:
                 put(0, lax.axis_index("wide"), q)
@@ -157,6 +162,7 @@
                 for way in range(2):
                     if step <= raw[own, way]:
                         put(own, owner_of(way, step), at[own, way][step])
+    now[:] = []
     for result in sorted(results, key=lambda result: result[3]):
         put_arrived(*result)
     return tuple(outs)

time: 459 us -> 453 us (0.987)
  waiting for transfers between devices: 199 us -> 186 us
  local copies, waits for them, and re-layouts: 24.2 us -> 28.8 us
    ppermute x6, waiting for transfers between devices: 25.2 us -> 4.81 us  [per_device(): lax.ppermute(result, 'wide', pairs[way])]
    ppermute x10, waiting for transfers between devices: 172 us -> 180 us  [start(): at[chain].append(lax.ppermute(block, 'wide', pairs[way]))]
    unnamed x32 -> x34, local copies, waits for them, and re-layouts: 22.9 us -> 27.5 us
  transfers between devices with their start and end apart: 19 -> 19, of which waited for: 8 -> 8; matrix products, arithmetic and copies ran while one was open for 5% -> 5% of each run, Pallas kernels for 36% -> 38%
where the time goes in v4:
time: 453 us; the launch traced here: 452 us
  waiting for transfers between devices  186 us (41%)
  Pallas kernels  170 us (38%)
  local copies, waits for them, and re-layouts  28.8 us (6%)
  between operations  26.9 us (6%)
  other arithmetic  23 us (5%)
  starting transfers between devices  17.5 us (4%)
    ppermute x10, waiting for transfers between devices, start(): at[chain].append(lax.ppermute(block, 'wide', pairs[way]))  180 us
    pallas_call x18, Pallas kernels, product(): pl.pallas_call(functools.partial(product_kernel, 1.0 / tokens), out_shape...  170 us
    unnamed x34, local copies, waits for them, and re-layouts  27.5 us
    dynamic_update_slice x6, other arithmetic, put_arrived(): lax.dynamic_update_slice(outs[which], tie(block).astype(jnp.float32)[None...  17.3 us
    ppermute x10, starting transfers between devices, start(): at[chain].append(lax.ppermute(block, 'wide', pairs[way]))  11.2 us
  transfers between devices with their start and end apart: 19, of which 8 were waited for; matrix products, arithmetic and copies ran while one was open for 5% of the time, Pallas kernels for 38%

profile of v4, /device:TPU:0, one launch (start us, length us, event | category | flops | bytes accessed | tf_op | source)
XLA Modules:
  0.0 452.4 jit_solution(4702727728989508869)
XLA Ops:
  7.2 0.0 all-gather.4.cloned.1.call-start
  7.2 0.7 all-gather.4.cloned.1.call-update
  7.9 0.0 copy-start.10
  7.9 0.0 all-gather.6.cloned.1.call-start
  8.0 3.1 collective-permute-start.4
  11.1 0.0 collective-permute-start.3
  11.1 5.6 %subtract_convert_fusion.left_ref = bf16[512,3072]{1,0:T(8,128)(2,1)} fusion(bf16[512,3072]{1,0:T(8,128)(2,1)} %left_ref, bf16[512,3072]{1,0:T(8,128)(2,1)} %param.20), kind=kLoop, calls=%fused_computation | loop fusion | flops 6291456 | bytes 9437184 | tf_op jit(solution)/shard_map/convert_element_type | solution.py:102
  16.7 62.7 %collective-permute-done.4.left_ref = bf16[512,3072]{1,0:T(8,128)(2,1)} collective-permute-done((bf16[512,3072]{1,0:T(8,128)(2,1)}, bf16[512,3072]{1,0:T(8,128)(2,1)}, u32[]{:S(2)}, u32[]{:S(2)}) %collective-permute-start.4) | collective-permute-done | bytes 3145760 | tf_op jit(solution)/shard_map/ppermute | solution.py:116
  79.4 1.5 collective-permute-done.3.left_ref
  80.9 0.0 all-gather.6.cloned.1.call-update
  81.0 0.0 all-gather.8.cloned.1.call-start
  81.0 0.7 all-gather.8.cloned.1.call-update
  81.7 0.4 collective-permute-start
  82.1 1.7 collective-permute-start.1
  83.8 0.3 collective-permute-start.5
  84.1 1.7 collective-permute-start.6
  85.8 67.3 %collective-permute-done.left_ref = bf16[512,3072]{1,0:T(8,128)(2,1)} collective-permute-done((bf16[512,3072]{1,0:T(8,128)(2,1)}, bf16[512,3072]{1,0:T(8,128)(2,1)}, u32[]{:S(2)}, u32[]{:S(2)}) %collective-permute-start) | collective-permute-done | bytes 3145760 | tf_op jit(solution)/shard_map/ppermute | solution.py:116
  153.1 0.3 collective-permute-done.1.left_ref
  153.4 1.7 collective-permute-start.7
  155.1 0.3 collective-permute-start.2
  155.4 0.6 dynamic_slice.51
  161.4 0.7 fusion
  162.1 4.6 %copy-done = bf16[2048,3072]{1,0:T(8,128)(2,1)S(1)} copy-done((bf16[2048,3072]{1,0:T(8,128)(2,1)S(1)}, bf16[2048,3072]{1,0:T(8,128)(2,1)}, u32[]{:S(2)}) %copy-start) | copy-done | bytes 12582936
  166.7 8.3 %shard_map.194.refs_0_ = f32[8,1,512,2048]{3,2,1,0:T(8,128)} custom-call(s32[1]{0:T(128)} %bitcast.4.place_ref, bf16[512,3072]{1,0:T(8,128)(2,1)S(1)} %copy-done.7, bf16[2048,3072]{1,0:T(8,128)(2,1)S(1)} %copy-done), custom_call_target="tpu_custom_call" | custom-call | tf_op jit(solution)/shard_map/pallas_call | solution.py:46
  175.0 8.3 %shard_map.195.refs_0_ = f32[8,1,512,2048]{3,2,1,0:T(8,128)} custom-call(s32[1]{0:T(128)} %bitcast.4.place_ref, bf16[512,3072]{1,0:T(8,128)(2,1)S(1)} %copy-done.8, bf16[2048,3072]{1,0:T(8,128)(2,1)S(1)} %copy-done.1), custom_call_target="tpu_custom_call" | custom-call | tf_op jit(solution)/shard_map/pallas_call | solution.py:46
  183.3 11.0 %shard_map.196.refs_0_ = f32[8,1,512,2048]{3,2,1,0:T(8,128)} custom-call(s32[1]{0:T(128)} %get-tuple-element.155.place_ref, bf16[512,3072]{1,0:T(8,128)(2,1)} %collective-permute-done.4.left_ref, bf16[2048,3072]{1,0:T(8,128)(2,1)S(1)} %copy-done.1, f32[8,1,512,2048]{3,2,1,0:T(8,128)} %shard_map.194.refs_0_), custom_call_target="tpu_custom_call", output_to_operand_aliasing={{}: (3, {})} | custom-call | tf_op jit(solution)/shard_map/pallas_call | solution.py:46
  194.3 11.0 %shard_map.197.refs_0_ = f32[8,1,512,2048]{3,2,1,0:T(8,128)} custom-call(s32[1]{0:T(128)} %get-tuple-element.156.place_ref, bf16[512,3072]{1,0:T(8,128)(2,1)} %collective-permute-done.3.left_ref, bf16[2048,3072]{1,0:T(8,128)(2,1)S(1)} %copy-done.1, f32[8,1,512,2048]{3,2,1,0:T(8,128)} %shard_map.196.refs_0_), custom_call_target="tpu_custom_call", output_to_operand_aliasing={{}: (3, {})} | custom-call | tf_op jit(solution)/shard_map/pallas_call | solution.py:46
  205.3 10.8 %shard_map.198.refs_0_ = f32[8,1,512,2048]{3,2,1,0:T(8,128)} custom-call(s32[1]{0:T(128)} %get-tuple-element.155.place_ref, bf16[512,3072]{1,0:T(8,128)(2,1)} %collective-permute-done.1.left_ref, bf16[2048,3072]{1,0:T(8,128)(2,1)S(1)} %copy-done.1, f32[8,1,512,2048]{3,2,1,0:T(8,128)} %shard_map.195.refs_0_), custom_call_target="tpu_custom_call", output_to_operand_aliasing={{}: (3, {})} | custom-call | tf_op jit(solution)/shard_map/pallas_call | solution.py:46
  216.1 10.8 %shard_map.199.refs_0_ = f32[8,1,512,2048]{3,2,1,0:T(8,128)} custom-call(s32[1]{0:T(128)} %get-tuple-element.156.place_ref, bf16[512,3072]{1,0:T(8,128)(2,1)} %collective-permute-done.left_ref, bf16[2048,3072]{1,0:T(8,128)(2,1)S(1)} %copy-done.1, f32[8,1,512,2048]{3,2,1,0:T(8,128)} %shard_map.198.refs_0_), custom_call_target="tpu_custom_call", output_to_operand_aliasing={{}: (3, {})} | custom-call | tf_op jit(solution)/shard_map/pallas_call | solution.py:46
  226.9 10.8 %shard_map.200.refs_0_ = f32[8,1,512,2048]{3,2,1,0:T(8,128)} custom-call(s32[1]{0:T(128)} %get-tuple-element.157.place_ref, bf16[512,3072]{1,0:T(8,128)(2,1)} %collective-permute-done.6.left_ref, bf16[2048,3072]{1,0:T(8,128)(2,1)S(1)} %copy-done.1, f32[8,1,512,2048]{3,2,1,0:T(8,128)} %shard_map.197.refs_0_), custom_call_target="tpu_custom_call", output_to_operand_aliasing={{}: (3, {})} | custom-call | tf_op jit(solution)/shard_map/pallas_call | solution.py:46
  237.8 10.8 %shard_map.201.refs_0_ = f32[8,1,512,2048]{3,2,1,0:T(8,128)} custom-call(s32[1]{0:T(128)} %get-tuple-element.158.place_ref, bf16[512,3072]{1,0:T(8,128)(2,1)} %collective-permute-done.5.left_ref, bf16[2048,3072]{1,0:T(8,128)(2,1)S(1)} %copy-done.1, f32[8,1,512,2048]{3,2,1,0:T(8,128)} %shard_map.200.refs_0_), custom_call_target="tpu_custom_call", output_to_operand_aliasing={{}: (3, {})} | custom-call | tf_op jit(solution)/shard_map/pallas_call | solution.py:46
  248.6 37.3 %collective-permute-done.7.left_ref = bf16[512,3072]{1,0:T(8,128)(2,1)} collective-permute-done((bf16[512,3072]{1,0:T(8,128)(2,1)}, bf16[512,3072]{1,0:T(8,128)(2,1)}, u32[]{:S(2)}, u32[]{:S(2)}) %collective-permute-start.7) | collective-permute-done | bytes 3145760 | tf_op jit(solution)/shard_map/ppermute | solution.py:116
  285.9 1.5 collective-permute-start.8
  287.4 0.5 collective-permute-start.12
  287.9 4.6 %copy-done.3 = bf16[2048,3072]{1,0:T(8,128)(2,1)S(1)} copy-done((bf16[2048,3072]{1,0:T(8,128)(2,1)S(1)}, bf16[2048,3072]{1,0:T(8,128)(2,1)}, u32[]{:S(2)}) %copy-start.3) | copy-done | bytes 12582936
  292.5 10.1 %shard_map.202 = bf16[512,2048]{1,0:T(8,128)(2,1)} custom-call(s32[1]{0:T(128)} %constant.89.clone.1.place_ref, bf16[512,3072]{1,0:T(8,128)(2,1)} %collective-permute-done.7.left_ref, bf16[2048,3072]{1,0:T(8,128)(2,1)S(1)} %copy-done.3), custom_call_target="tpu_custom_call" | custom-call | tf_op jit(solution)/shard_map/pallas_call | solution.py:46
  302.6 1.4 collective-permute-start.11
  304.0 4.6 %copy-done.5 = bf16[2048,3072]{1,0:T(8,128)(2,1)S(1)} copy-done((bf16[2048,3072]{1,0:T(8,128)(2,1)S(1)}, bf16[2048,3072]{1,0:T(8,128)(2,1)}, u32[]{:S(2)}) %copy-start.5) | copy-done | bytes 12582936
  308.5 10.1 %shard_map.203 = bf16[512,2048]{1,0:T(8,128)(2,1)} custom-call(s32[1]{0:T(128)} %constant.89.clone.1.place_ref, bf16[512,3072]{1,0:T(8,128)(2,1)} %collective-permute-done.5.left_ref, bf16[2048,3072]{1,0:T(8,128)(2,1)S(1)} %copy-done.5), custom_call_target="tpu_custom_call" | custom-call | tf_op jit(solution)/shard_map/pallas_call | solution.py:46
  318.6 0.6 collective-permute-start.13
  319.2 4.6 %copy-done.2 = bf16[2048,3072]{1,0:T(8,128)(2,1)S(1)} copy-done((bf16[2048,3072]{1,0:T(8,128)(2,1)S(1)}, bf16[2048,3072]{1,0:T(8,128)(2,1)}, u32[]{:S(2)}) %copy-start.2) | copy-done | bytes 12582936
  323.8 11.4 %shard_map.204.refs_0_ = f32[8,1,512,2048]{3,2,1,0:T(8,128)} custom-call(s32[1]{0:T(128)} %get-tuple-element.157.place_ref, bf16[512,3072]{1,0:T(8,128)(2,1)} %collective-permute-done.7.left_ref, bf16[2048,3072]{1,0:T(8,128)(2,1)S(1)} %copy-done.2, f32[8,1,512,2048]{3,2,1,0:T(8,128)} %shard_map.199.refs_0_), custom_call_target="tpu_custom_call", output_to_operand_aliasing={{}: (3, {})} | custom-call | tf_op jit(solution)/shard_map/pallas_call | solution.py:46
  335.2 11.1 %shard_map.205.refs_0_ = f32[8,1,512,2048]{3,2,1,0:T(8,128)} custom-call(s32[1]{0:T(128)} %get-tuple-element.158.place_ref, bf16[512,3072]{1,0:T(8,128)(2,1)} %collective-permute-done.2.left_ref, bf16[2048,3072]{1,0:T(8,128)(2,1)S(1)} %copy-done.2, f32[8,1,512,2048]{3,2,1,0:T(8,128)} %shard_map.204.refs_0_), custom_call_target="tpu_custom_call", output_to_operand_aliasing={{}: (3, {})} | custom-call | tf_op jit(solution)/shard_map/pallas_call | solution.py:46
  346.4 10.8 %collective-permute-done.8.left_ref = bf16[512,3072]{1,0:T(8,128)(2,1)S(1)} collective-permute-done((bf16[512,3072]{1,0:T(8,128)(2,1)}, bf16[512,3072]{1,0:T(8,128)(2,1)S(1)}, u32[]{:S(2)}, u32[]{:S(2)}) %collective-permute-start.8) | collective-permute-done | bytes 3145760 | tf_op jit(solution)/shard_map/ppermute | solution.py:116
  357.2 6.5 %shard_map.206 = bf16[384,2048]{1,0:T(8,128)(2,1)} custom-call(s32[1]{0:T(128)} %constant.89.clone.1.place_ref, bf16[512,3072]{1,0:T(8,128)(2,1)S(1)} %collective-permute-done.8.left_ref, bf16[2048,3072]{1,0:T(8,128)(2,1)S(1)} %bitcast.34), custom_call_target="tpu_custom_call" | custom-call | tf_op jit(solution)/shard_map/pallas_call | solution.py:46
  363.7 1.5 collective-permute-start.10
  372.8 4.6 %copy-done.6 = bf16[2048,3072]{1,0:T(8,128)(2,1)S(1)} copy-done((bf16[2048,3072]{1,0:T(8,128)(2,1)S(1)}, bf16[2048,3072]{1,0:T(8,128)(2,1)}, u32[]{:S(2)}) %copy-start.6) | copy-done | bytes 12582936
  377.4 4.8 %shard_map.207 = bf16[128,2048]{1,0:T(8,128)(2,1)S(1)} custom-call(s32[1]{0:T(128)} %constant.89.clone.1.place_ref, bf16[512,3072]{1,0:T(8,128)(2,1)S(1)} %collective-permute-done.8.left_ref, bf16[2048,3072]{1,0:T(8,128)(2,1)S(1)} %copy-done.6), custom_call_target="tpu_custom_call" | custom-call | tf_op jit(solution)/shard_map/pallas_call | solution.py:46
  382.2 1.6 collective-permute-start.9
  383.8 4.6 %copy-done.4 = bf16[2048,3072]{1,0:T(8,128)(2,1)S(1)} copy-done((bf16[2048,3072]{1,0:T(8,128)(2,1)S(1)}, bf16[2048,3072]{1,0:T(8,128)(2,1)}, u32[]{:S(2)}) %copy-start.4) | copy-done | bytes 12582936
  388.4 8.3 %shard_map.208 = bf16[384,2048]{1,0:T(8,128)(2,1)} custom-call(s32[1]{0:T(128)} %constant.89.clone.1.place_ref, bf16[512,3072]{1,0:T(8,128)(2,1)} %collective-permute-done.12.left_ref, bf16[2048,3072]{1,0:T(8,128)(2,1)S(1)} %copy-done.4), custom_call_target="tpu_custom_call" | custom-call | tf_op jit(solution)/shard_map/pallas_call | solution.py:46
  396.7 0.4 collective-permute-start.14
  397.2 6.1 %shard_map.209 = bf16[128,2048]{1,0:T(8,128)(2,1)S(1)} custom-call(s32[1]{0:T(128)} %constant.89.clone.1.place_ref, bf16[512,3072]{1,0:T(8,128)(2,1)} %collective-permute-done.12.left_ref, bf16[2048,3072]{1,0:T(8,128)(2,1)S(1)} %copy-done.4), custom_call_target="tpu_custom_call" | custom-call | tf_op jit(solution)/shard_map/pallas_call | solution.py:46
  403.4 10.8 %shard_map.210 = f32[8,1,512,2048]{3,2,1,0:T(8,128)} custom-call(s32[1]{0:T(128)} %get-tuple-element.154.place_ref, bf16[512,3072]{1,0:T(8,128)(2,1)} %collective-permute-done.12.left_ref, bf16[2048,3072]{1,0:T(8,128)(2,1)S(1)} %bitcast.32, f32[8,1,512,2048]{3,2,1,0:T(8,128)} %shard_map.201.refs_0_), custom_call_target="tpu_custom_call", output_to_operand_aliasing={{}: (3, {})} | custom-call | tf_op jit(solution)/shard_map/pallas_call | solution.py:46
  414.2 9.0 %shard_map.211 = f32[8,1,512,2048]{3,2,1,0:T(8,128)} custom-call(s32[1]{0:T(128)} %get-tuple-element.159.place_ref, bf16[512,3072]{1,0:T(8,128)(2,1)S(1)} %collective-permute-done.8.left_ref, bf16[2048,3072]{1,0:T(8,128)(2,1)S(1)} %bitcast.32, f32[8,1,512,2048]{3,2,1,0:T(8,128)} %shard_map.205.refs_0_), custom_call_target="tpu_custom_call", output_to_operand_aliasing={{}: (3, {})} | custom-call | tf_op jit(solution)/shard_map/pallas_call | solution.py:46
  423.2 0.6 collective-permute-start.15
  423.8 4.1 convert_dynamic-update-slice_fusion.1
  427.9 4.1 convert_dynamic-update-slice_fusion
  432.1 3.8 collective-permute-done.10
  435.9 3.4 convert_dynamic-update-slice_fusion.3
  439.3 3.4 convert_dynamic-update-slice_fusion.2
  442.8 1.0 collective-permute-done.9
  443.8 1.1 convert_dynamic-update-slice_fusion.5
  444.8 1.1 convert_dynamic-update-slice_fusion.4
  (40 shorter events, 0.1 us)
Async XLA Ops:
  7.2 154.9 %all-gather.4.cloned.1.call-start = ((), (), s32[]{:S(2)}) async-start(), calls=%async_computation | async-start | bytes 15728640 | tf_op jit(solution)/shard_map/all_gather | solution.py:99
  7.9 147.5 %copy-start.10 = (s32[8]{0:T(128)S(1)}, s32[8]{0:T(128)}, u32[]{:S(2)}) copy-start(s32[8]{0:T(128)} %constant.104.clone) | copy-start | bytes 100
  7.9 153.5 %copy-start.9 = (s32[8]{0:T(128)S(1)}, s32[8]{0:T(128)}, u32[]{:S(2)}) copy-start(s32[8]{0:T(128)} %constant.105.clone) | copy-start | bytes 100
  7.9 154.2 %copy-start.7 = (bf16[512,3072]{1,0:T(8,128)(2,1)S(1)}, bf16[512,3072]{1,0:T(8,128)(2,1)}, u32[]{:S(2)}) copy-start(bf16[512,3072]{1,0:T(8,128)(2,1)} %left_ref) | copy-start | bytes 9437188
  7.9 280.0 %all-gather.6.cloned.1.call-start = ((), (), s32[]{:S(2)}) async-start(), calls=%async_computation.1 | async-start | bytes 15728640 | tf_op jit(solution)/shard_map/all_gather | solution.py:99
  8.0 71.4 %collective-permute-start.4 = (bf16[512,3072]{1,0:T(8,128)(2,1)}, bf16[512,3072]{1,0:T(8,128)(2,1)}, u32[]{:S(2)}, u32[]{:S(2)}) collective-permute-start(bf16[512,3072]{1,0:T(8,128)(2,1)} %left_ref), channel_id=1, source_target_pairs={{0,8},{8,16},{16,24},{24,28},{28,20},{20,12},{12,4},{4,0},{1,9},{9... | collective-permute-start | bytes 9437192 | tf_op jit(solution)/shard_map/ppermute | solution.py:116
  11.1 69.9 %collective-permute-start.3 = (bf16[512,3072]{1,0:T(8,128)(2,1)}, bf16[512,3072]{1,0:T(8,128)(2,1)}, u32[]{:S(2)}, u32[]{:S(2)}) collective-permute-start(bf16[512,3072]{1,0:T(8,128)(2,1)} %left_ref), channel_id=1, source_target_pairs={{8,0},{16,8},{24,16},{28,24},{20,28},{12,20},{4,12},{0,4},{9,1},{1... | collective-permute-start | bytes 9437192 | tf_op jit(solution)/shard_map/ppermute | solution.py:116
  81.0 223.0 %all-gather.8.cloned.1.call-start = ((), (), s32[]{:S(2)}) async-start(), calls=%async_computation.2 | async-start | bytes 15728640 | tf_op jit(solution)/shard_map/all_gather | solution.py:99
  81.7 71.4 %collective-permute-start = (bf16[512,3072]{1,0:T(8,128)(2,1)}, bf16[512,3072]{1,0:T(8,128)(2,1)}, u32[]{:S(2)}, u32[]{:S(2)}) collective-permute-start(bf16[512,3072]{1,0:T(8,128)(2,1)} %subtract_convert_fusion.left_ref), channel_id=1, source_target_pairs={{8,0},{16,8},{24,16},{28,24},{20,28},{12,20},{4,12},{0,4},{9,1},{1... | collective-permute-start | bytes 9437192 | tf_op jit(solution)/shard_map/ppermute | solution.py:116
  82.1 71.4 %collective-permute-start.1 = (bf16[512,3072]{1,0:T(8,128)(2,1)}, bf16[512,3072]{1,0:T(8,128)(2,1)}, u32[]{:S(2)}, u32[]{:S(2)}) collective-permute-start(bf16[512,3072]{1,0:T(8,128)(2,1)} %subtract_convert_fusion.left_ref), channel_id=1, source_target_pairs={{0,8},{8,16},{16,24},{24,28},{28,20},{20,12},{12,4},{4,0},{1,9},{9... | collective-permute-start | bytes 9437192 | tf_op jit(solution)/shard_map/ppermute | solution.py:116
  83.8 143.2 %collective-permute-start.5 = (bf16[512,3072]{1,0:T(8,128)(2,1)}, bf16[512,3072]{1,0:T(8,128)(2,1)}, u32[]{:S(2)}, u32[]{:S(2)}) collective-permute-start(bf16[512,3072]{1,0:T(8,128)(2,1)} %collective-permute-done.3.left_ref), channel_id=1, source_target_pairs={{8,0},{16,8},{24,16},{28,24},{20,28},{12,20},{4,12},{0,4},{9,1},{1... | collective-permute-start | bytes 9437192 | tf_op jit(solution)/shard_map/ppermute | solution.py:116
  84.1 142.8 %collective-permute-start.6 = (bf16[512,3072]{1,0:T(8,128)(2,1)}, bf16[512,3072]{1,0:T(8,128)(2,1)}, u32[]{:S(2)}, u32[]{:S(2)}) collective-permute-start(bf16[512,3072]{1,0:T(8,128)(2,1)} %collective-permute-done.4.left_ref), channel_id=1, source_target_pairs={{0,8},{8,16},{16,24},{24,28},{28,20},{20,12},{12,4},{4,0},{1,9},{9... | collective-permute-start | bytes 9437192 | tf_op jit(solution)/shard_map/ppermute | solution.py:116
  153.4 132.5 %collective-permute-start.7 = (bf16[512,3072]{1,0:T(8,128)(2,1)}, bf16[512,3072]{1,0:T(8,128)(2,1)}, u32[]{:S(2)}, u32[]{:S(2)}) collective-permute-start(bf16[512,3072]{1,0:T(8,128)(2,1)} %collective-permute-done.1.left_ref), channel_id=1, source_target_pairs={{0,8},{8,16},{16,24},{24,28},{28,20},{20,12},{12,4},{4,0},{1,9},{9... | collective-permute-start | bytes 9437192 | tf_op jit(solution)/shard_map/ppermute | solution.py:116
  155.1 130.8 %collective-permute-start.2 = (bf16[512,3072]{1,0:T(8,128)(2,1)}, bf16[512,3072]{1,0:T(8,128)(2,1)}, u32[]{:S(2)}, u32[]{:S(2)}) collective-permute-start(bf16[512,3072]{1,0:T(8,128)(2,1)} %collective-permute-done.left_ref), channel_id=1, source_target_pairs={{8,0},{16,8},{24,16},{28,24},{20,28},{12,20},{4,12},{0,4},{9,1},{1... | collective-permute-start | bytes 9437192 | tf_op jit(solution)/shard_map/ppermute | solution.py:116
  162.1 4.6 %copy-start = (bf16[2048,3072]{1,0:T(8,128)(2,1)S(1)}, bf16[2048,3072]{1,0:T(8,128)(2,1)}, u32[]{:S(2)}) copy-start(bf16[2048,3072]{1,0:T(8,128)(2,1)} %all-gather.4.cloned.1.call-done.right_ref) | copy-start | bytes 37748740
  166.7 8.3 %copy-start.1 = (bf16[2048,3072]{1,0:T(8,128)(2,1)S(1)}, bf16[2048,3072]{1,0:T(8,128)(2,1)}, u32[]{:S(2)}) copy-start(bf16[2048,3072]{1,0:T(8,128)(2,1)} %all-gather.4.cloned.1.call-done.right_ref) | copy-start | bytes 37748740
  166.7 8.3 %copy-start.8 = (bf16[512,3072]{1,0:T(8,128)(2,1)S(1)}, bf16[512,3072]{1,0:T(8,128)(2,1)}, u32[]{:S(2)}) copy-start(bf16[512,3072]{1,0:T(8,128)(2,1)} %subtract_convert_fusion.left_ref) | copy-start | bytes 9437188
  285.9 71.2 %collective-permute-start.8 = (bf16[512,3072]{1,0:T(8,128)(2,1)}, bf16[512,3072]{1,0:T(8,128)(2,1)S(1)}, u32[]{:S(2)}, u32[]{:S(2)}) collective-permute-start(bf16[512,3072]{1,0:T(8,128)(2,1)} %collective-permute-done.2.left_ref), channel_id=1, source_target_pairs={{8,0},{16,8},{24,16},{28,24},{20,28},{12,20},{4,12},{0,4},{9,1},{1... | collective-permute-start | bytes 9437192 | tf_op jit(solution)/shard_map/ppermute | solution.py:116
  287.4 96.4 %collective-permute-start.12 = (bf16[512,3072]{1,0:T(8,128)(2,1)}, bf16[512,3072]{1,0:T(8,128)(2,1)}, u32[]{:S(2)}, u32[]{:S(2)}) collective-permute-start(bf16[512,3072]{1,0:T(8,128)(2,1)} %collective-permute-done.6.left_ref), channel_id=1, source_target_pairs={{0,8},{8,16},{16,24},{24,28},{28,20},{20,12},{12,4},{4,0},{1,9},{9... | collective-permute-start | bytes 9437192 | tf_op jit(solution)/shard_map/ppermute | solution.py:116
  287.9 4.6 %copy-start.3 = (bf16[2048,3072]{1,0:T(8,128)(2,1)S(1)}, bf16[2048,3072]{1,0:T(8,128)(2,1)}, u32[]{:S(2)}) copy-start(bf16[2048,3072]{1,0:T(8,128)(2,1)} %all-gather.6.cloned.1.call-done.right_ref) | copy-start | bytes 37748740
  302.6 120.6 %collective-permute-start.11 = (bf16[512,2048]{1,0:T(8,128)(2,1)}, bf16[512,2048]{1,0:T(8,128)(2,1)}, u32[]{:S(2)}, u32[]{:S(2)}) collective-permute-start(bf16[512,2048]{1,0:T(8,128)(2,1)} %shard_map.202), channel_id=1, source_target_pairs={{0,8},{8,16},{16,24},{24,28},{28,20},{20,12},{12,4},{4,0},{1,9},{9... | collective-permute-start | bytes 6291464 | tf_op jit(solution)/shard_map/ppermute | solution.py:155
  304.0 4.6 %copy-start.5 = (bf16[2048,3072]{1,0:T(8,128)(2,1)S(1)}, bf16[2048,3072]{1,0:T(8,128)(2,1)}, u32[]{:S(2)}) copy-start(bf16[2048,3072]{1,0:T(8,128)(2,1)} %all-gather.8.cloned.1.call-done.right_ref) | copy-start | bytes 37748740
  318.6 109.3 %collective-permute-start.13 = (bf16[512,2048]{1,0:T(8,128)(2,1)}, bf16[512,2048]{1,0:T(8,128)(2,1)}, u32[]{:S(2)}, u32[]{:S(2)}) collective-permute-start(bf16[512,2048]{1,0:T(8,128)(2,1)} %shard_map.203), channel_id=1, source_target_pairs={{8,0},{16,8},{24,16},{28,24},{20,28},{12,20},{4,12},{0,4},{9,1},{1... | collective-permute-start | bytes 6291464 | tf_op jit(solution)/shard_map/ppermute | solution.py:155
  319.2 4.6 %copy-start.2 = (bf16[2048,3072]{1,0:T(8,128)(2,1)S(1)}, bf16[2048,3072]{1,0:T(8,128)(2,1)}, u32[]{:S(2)}) copy-start(bf16[2048,3072]{1,0:T(8,128)(2,1)} %all-gather.4.cloned.1.call-done.right_ref) | copy-start | bytes 37748740
  323.8 33.3 %slice-start.3 = ((s8[12582912]{0:T(1024)(128)(4,1)}), s8[4194304]{0:T(1024)(128)(4,1)S(1)}, s32[]{:S(2)}) async-start(s8[12582912]{0:T(1024)(128)(4,1)} %bitcast.33), calls=%async_computation.6 | async-start | bytes 8388608
  323.8 33.3 %slice-start.4 = ((s8[12582912]{0:T(1024)(128)(4,1)}), s8[4194304]{0:T(1024)(128)(4,1)S(1)}, s32[]{:S(2)}) async-start(s8[12582912]{0:T(1024)(128)(4,1)} %bitcast.33), calls=%async_computation.7 | async-start | bytes 8388608
  335.2 21.9 %slice-start.5 = ((s8[12582912]{0:T(1024)(128)(4,1)}), s8[4194304]{0:T(1024)(128)(4,1)S(1)}, s32[]{:S(2)}) async-start(s8[12582912]{0:T(1024)(128)(4,1)} %bitcast.33), calls=%async_computation.8 | async-start | bytes 8388608
  363.7 72.2 %collective-permute-start.10 = (bf16[384,2048]{1,0:T(8,128)(2,1)}, bf16[384,2048]{1,0:T(8,128)(2,1)}, u32[]{:S(2)}, u32[]{:S(2)}) collective-permute-start(bf16[384,2048]{1,0:T(8,128)(2,1)} %shard_map.206), channel_id=1, source_target_pairs={{8,0},{16,8},{24,16},{28,24},{20,28},{12,20},{4,12},{0,4},{9,1},{1... | collective-permute-start | bytes 4718600 | tf_op jit(solution)/shard_map/ppermute | solution.py:155
  372.8 4.6 %copy-start.6 = (bf16[2048,3072]{1,0:T(8,128)(2,1)S(1)}, bf16[2048,3072]{1,0:T(8,128)(2,1)}, u32[]{:S(2)}) copy-start(bf16[2048,3072]{1,0:T(8,128)(2,1)} %all-gather.8.cloned.1.call-done.right_ref) | copy-start | bytes 37748740
  382.2 61.6 %collective-permute-start.9 = (bf16[128,2048]{1,0:T(8,128)(2,1)S(1)}, bf16[128,2048]{1,0:T(8,128)(2,1)S(1)}, u32[]{:S(2)}, u32[]{:S(2)}) collective-permute-start(bf16[128,2048]{1,0:T(8,128)(2,1)S(1)} %shard_map.207), channel_id=1, source_target_pairs={{8,0},{16,8},{24,16},{28,24},{20,28},{12,20},{4,12},{0,4},{9,1},{1... | collective-permute-start | bytes 1572872 | tf_op jit(solution)/shard_map/ppermute | solution.py:155
  383.8 4.6 %copy-start.4 = (bf16[2048,3072]{1,0:T(8,128)(2,1)S(1)}, bf16[2048,3072]{1,0:T(8,128)(2,1)}, u32[]{:S(2)}) copy-start(bf16[2048,3072]{1,0:T(8,128)(2,1)} %all-gather.6.cloned.1.call-done.right_ref) | copy-start | bytes 37748740
  388.4 14.9 %slice-start = ((s8[12582912]{0:T(1024)(128)(4,1)}), s8[4194304]{0:T(1024)(128)(4,1)S(1)}, s32[]{:S(2)}) async-start(s8[12582912]{0:T(1024)(128)(4,1)} %bitcast.31), calls=%async_computation.3 | async-start | bytes 8388608
  388.4 14.9 %slice-start.1 = ((s8[12582912]{0:T(1024)(128)(4,1)}), s8[4194304]{0:T(1024)(128)(4,1)S(1)}, s32[]{:S(2)}) async-start(s8[12582912]{0:T(1024)(128)(4,1)} %bitcast.31), calls=%async_computation.4 | async-start | bytes 8388608
  396.7 6.6 %slice-start.2 = ((s8[12582912]{0:T(1024)(128)(4,1)}), s8[4194304]{0:T(1024)(128)(4,1)S(1)}, s32[]{:S(2)}) async-start(s8[12582912]{0:T(1024)(128)(4,1)} %bitcast.31), calls=%async_computation.5 | async-start | bytes 8388608
  396.7 42.6 %collective-permute-start.14 = (bf16[384,2048]{1,0:T(8,128)(2,1)}, bf16[384,2048]{1,0:T(8,128)(2,1)}, u32[]{:S(2)}, u32[]{:S(2)}) collective-permute-start(bf16[384,2048]{1,0:T(8,128)(2,1)} %shard_map.208), channel_id=1, source_target_pairs={{0,8},{8,16},{16,24},{24,28},{28,20},{20,12},{12,4},{4,0},{1,9},{9... | collective-permute-start | bytes 4718600 | tf_op jit(solution)/shard_map/ppermute | solution.py:155
  423.2 21.6 %collective-permute-start.15 = (bf16[128,2048]{1,0:T(8,128)(2,1)S(1)}, bf16[128,2048]{1,0:T(8,128)(2,1)S(1)}, u32[]{:S(2)}, u32[]{:S(2)}) collective-permute-start(bf16[128,2048]{1,0:T(8,128)(2,1)S(1)} %shard_map.209), channel_id=1, source_target_pairs={{0,8},{8,16},{16,24},{24,28},{28,20},{20,12},{12,4},{4,0},{1,9},{9... | collective-permute-start | bytes 1572872 | tf_op jit(solution)/shard_map/ppermute | solution.py:155
Sparse Core Ops, SparseCore 0:
  9.6 84.7 all-gather.3
  95.9 82.0 all-gather.5
  179.7 82.0 all-gather.7

commit v5 on v4

--- a/solution.py
+++ b/solution.py
@@ -22,7 +22,7 @@
     result_ref[...] = (total * scale).astype(result_ref.dtype).reshape(result_ref.shape)
 
 
-def product(left, right, owner=None, out=None, out_shape=None, first_row=0, rows=None):
+def product(left, right, rows=None, row=0, owner=None, out=None, out_shape=None, out_row=0):
     rows, tokens = rows or left.shape[0], left.shape[1]
     columns = right.shape[0]
     tile = min(TILE, columns)
@@ -31,10 +31,10 @@
         out_spec = pl.BlockSpec((rows, tile), lambda j, at: (0, j))
         shape = jax.ShapeDtypeStruct((rows, columns), jnp.bfloat16)
     else:
-        out_spec = pl.BlockSpec((1, 1, rows, tile), lambda j, at: (at[0], 0, 0, j))
+        out_spec = pl.BlockSpec((1, 1, rows, tile), lambda j, at: (at[0], 0, out_row // rows, j))
         shape = jax.ShapeDtypeStruct(out_shape, jnp.float32)
     in_specs = [
-        pl.BlockSpec((rows, tokens), lambda j, at: (first_row // rows, 0)),
+        pl.BlockSpec((rows, tokens), lambda j, at: (row // rows, 0)),
         pl.BlockSpec((tile, tokens), lambda j, at: (j, 0)),
     ]
     operands = [jnp.asarray(owner, jnp.int32).reshape(1), left, right]
@@ -53,7 +53,7 @@
             out_specs=out_spec,
         ),
         input_output_aliases=aliases,
-        compiler_params=pltpu.CompilerParams(vmem_limit_bytes=32 * 1024 * 1024),
+        compiler_params=pltpu.CompilerParams(vmem_limit_bytes=48 * 1024 * 1024),
         cost_estimate=pl.CostEstimate(flops=0, bytes_accessed=0, transcendentals=0),
     )(*operands)
 
@@ -87,8 +87,15 @@
             outs[i] = done[1 + place_of]
         return done[0]
 
-    def put(which, owner, block):
-        outs[which] = product(tie(block), right_own, owner, outs[which], out_shape)
+    def put(which, owner, block, out_row=0):
+        outs[which] = product(
+            tie(block),
+            right_own,
+            owner=owner,
+            out=outs[which],
+            out_shape=out_shape,
+            out_row=out_row,
+        )
 
     def put_arrived(which, owner, block, first_row):
         outs[which] = lax.dynamic_update_slice(
@@ -105,18 +112,33 @@
     far, near = wide_count // 2, (wide_count - 1) // 2
     reach = {(0, 0): far, (0, 1): near, (1, 0): near, (1, 1): far}
     raw = {chain: max(hops - 1, min(hops, 1)) for chain, hops in reach.items()}
-    at = {(which, way): [(q, d)[which]] for which in range(2) for way in range(2)}
+    at = {(which, way): [[(q, d)[which]]] for which in range(2) for way in range(2)}
+    small = owned_rows // QUARTERS
+    big = owned_rows - small
 
     def start(which, step):
         for way in range(2):
             chain = (which, way)
             if step <= raw[chain]:
-                block = at[chain][step - 1]
-                block = block if step == 1 else tie(block)
-                at[chain].append(lax.ppermute(block, "wide", pairs[way]))
+                parts = at[chain][step - 1]
+                if chain == (1, 1) and step == raw[chain] - 1:
+                    parts = [parts[0][:big], parts[0][big:]]
+                if step > 1:
+                    now[:] = at[chain][step - 1][:1]
+                    parts = [tie(part) for part in parts]
+                at[chain].append([lax.ppermute(part, "wide", pairs[way]) for part in parts])
 
     def arrivals(which, step):
-        return [at[which, way][step] for way in range(2) if step <= raw[which, way]]
+        return [at[which, way][step][0] for way in range(2) if step <= raw[which, way]]
+
+    def send(which, way, step, block, rows, row=0, out_row=0):
+        result = product(tie(block), right_next[way], rows=rows, row=row)
+        now.append(result)
+        moved = lax.ppermute(result, "wide", pairs[way])
+        results.append((which, owner_of(way, step + 1), moved, out_row))
+
+    def is_last(which, way, step):
+        return step == raw[which, way] < reach[which, way]
 
     start(0, 1)
     start(1, 1)
@@ -126,42 +148,40 @@
         for which in range(2):
             if not arrivals(which, step):
                 continue
+            start(which, step + 1)
             now[:] = arrivals(which, step)
-            start(which, step + 1)
             if step == 1 and which == 0:
                 for way in range(2):
                     if raw[0, 1 - way] >= 1:
-                        right_next[way] = gather(at[0, 1 - way][1], d)
+                        right_next[way] = gather(at[0, 1 - way][1][0], d)
             together = step in (1, far - 1)
             if which == 0 and together:
                 continue
             if which == 1:
-                for sent, way in ((1, 0), (0, 1), (1, 1), (0, 0)):
-                    if step == raw[sent, way] < reach[sent, way]:
-                        cut = owned_rows - owned_rows // QUARTERS if step == far - 1 else owned_rows
-                        for first_row, rows in ((0, cut), (cut, owned_rows - cut)):
-                            if rows == 0:
-                                continue
-                            result = product(
-                                tie(at[sent, way][step]),
-                                right_next[way],
-                                first_row=first_row,
-                                rows=rows,
-                            )
-                            now.append(result)
-                            results.append((
-                                sent,
-                                owner_of(way, step + 1),
-                                lax.ppermute(result, "wide", pairs[way]),
-                                first_row,
-                            ))
+                for chain in ((1, 0), (0, 1)):
+                    if is_last(*chain, step):
+                        send(*chain, step, at[chain][step][0], owned_rows)
+                for chain in ((0, 0), (1, 1)):
+                    if is_last(*chain, step):
+                        send(*chain, step, at[chain][step][0], big)
             if step == 1:
                 put(0, lax.axis_index("wide"), q)
                 put(1, lax.axis_index("wide"), d)
             for own in range(2) if together else (which,):
                 for way in range(2):
                     if step <= raw[own, way]:
-                        put(own, owner_of(way, step), at[own, way][step])
+                        put(own, owner_of(way, step), at[own, way][step][0])
+            if which == 1:
+                for chain in ((1, 1), (0, 0)):
+                    if is_last(*chain, step):
+                        parts = at[chain][step]
+                        row = 0 if len(parts) == 2 else big
+                        if chain == (0, 0) and len(results) > 4:
+                            put_arrived(*results.pop(0))
+                        send(*chain, step, parts[-1], small, row, big)
+                for way in range(2):
+                    if step <= raw[1, way] and len(at[1, way][step]) == 2:
+                        put(1, owner_of(way, step), at[1, way][step][1], big)
     now[:] = []
     for result in sorted(results, key=lambda result: result[3]):
         put_arrived(*result)

time: 453 us -> 456 us (level)
  Pallas kernels: 170 us -> 216 us
  local copies, waits for them, and re-layouts: 28.8 us -> 4.6 us
  waiting for transfers between devices: 186 us -> 166 us
    pallas_call x18 -> x20, Pallas kernels: 170 us -> 216 us  [product(): pl.pallas_call(functools.partial(product_kernel, 1.0 / tokens), out_shape...]
    unnamed x34 -> x12, local copies, waits for them, and re-layouts: 27.5 us -> 1.69 us
    ppermute x16 -> x18, waiting for transfers between devices: 185 us -> 165 us  [the longest x12 165 us: start(): at[chain].append([lax.ppermute(part, 'wide', pairs[way]) for part in parts])]
    ppermute x16 -> x18, starting transfers between devices: 17.4 us -> 18.8 us  [the longest x12 12.4 us: start(): at[chain].append([lax.ppermute(part, 'wide', pairs[way]) for part in parts])]
  transfers between devices with their start and end apart: 19 -> 21, of which waited for: 8 -> 6; matrix products, arithmetic and copies ran while one was open for 5% -> 5% of each run, Pallas kernels for 38% -> 48%
where the time goes in v5:
time: 456 us; the launch traced here: 454 us
  Pallas kernels  216 us (47%)
  waiting for transfers between devices  166 us (36%)
  between operations  26.6 us (6%)
  other arithmetic  21.6 us (5%)
  starting transfers between devices  18.9 us (4%)
  local copies, waits for them, and re-layouts  4.6 us (1%)
    pallas_call x20, Pallas kernels, product(): pl.pallas_call(functools.partial(product_kernel, 1.0 / tokens), out_shape...  216 us
    ppermute x12, waiting for transfers between devices, start(): at[chain].append([lax.ppermute(part, 'wide', pairs[way]) for part in parts])  165 us
    dynamic_update_slice x6, other arithmetic, put_arrived(): lax.dynamic_update_slice(outs[which], tie(block).astype(jnp.float32)[None...  15.9 us
    ppermute x12, starting transfers between devices, start(): at[chain].append([lax.ppermute(part, 'wide', pairs[way]) for part in parts])  12.4 us
  transfers between devices with their start and end apart: 21, of which 6 were waited for; matrix products, arithmetic and copies ran while one was open for 5% of the time, Pallas kernels for 48%

profile of v5, /device:TPU:0, one launch (start us, length us, event | category | flops | bytes accessed | tf_op | source)
XLA Modules:
  0.0 454.2 jit_solution(6095650169155277461)
XLA Ops:
  7.2 0.0 all-gather.4.cloned.1.call-start
  7.2 0.7 all-gather.4.cloned.1.call-update
  7.9 0.0 all-gather.6.cloned.1.call-start
  7.9 3.1 collective-permute-start.5
  11.0 0.0 collective-permute-start.3
  11.0 5.6 %subtract_convert_fusion.left_ref = bf16[512,3072]{1,0:T(8,128)(2,1)} fusion(bf16[512,3072]{1,0:T(8,128)(2,1)} %left_ref, bf16[512,3072]{1,0:T(8,128)(2,1)} %param.22), kind=kLoop, calls=%fused_computation | loop fusion | flops 6291456 | bytes 9437184 | tf_op jit(solution)/shard_map/convert_element_type | solution.py:109
  16.7 62.7 %collective-permute-done.5.left_ref = bf16[512,3072]{1,0:T(8,128)(2,1)} collective-permute-done((bf16[512,3072]{1,0:T(8,128)(2,1)}, bf16[512,3072]{1,0:T(8,128)(2,1)}, u32[]{:S(2)}, u32[]{:S(2)}) %collective-permute-start.5) | collective-permute-done | bytes 3145760 | tf_op jit(solution)/shard_map/ppermute | solution.py:129
  79.4 1.5 collective-permute-done.3.left_ref
  80.9 0.0 all-gather.6.cloned.1.call-update
  80.9 0.0 all-gather.8.cloned.1.call-start
  81.0 0.7 all-gather.8.cloned.1.call-update
  81.7 1.6 collective-permute-start.7
  83.3 0.4 collective-permute-start
  83.7 1.6 collective-permute-start.6
  85.3 0.4 collective-permute-start.4
  85.8 67.3 %collective-permute-done.7.left_ref = bf16[512,3072]{1,0:T(8,128)(2,1)} collective-permute-done((bf16[512,3072]{1,0:T(8,128)(2,1)}, bf16[512,3072]{1,0:T(8,128)(2,1)}, u32[]{:S(2)}, u32[]{:S(2)}) %collective-permute-start.7) | collective-permute-done | bytes 3145760 | tf_op jit(solution)/shard_map/ppermute | solution.py:129
  153.1 1.6 collective-permute-start.11
  154.6 1.6 slice.9
  156.2 1.7 copy-done.1
  157.9 0.4 collective-permute-start.2
  158.3 0.6 dynamic_slice.57
  164.3 0.7 fusion
  165.0 0.0 copy-start.3
  165.0 10.9 %shard_map.212.refs_0_ = f32[8,1,512,2048]{3,2,1,0:T(8,128)} custom-call(s32[1]{0:T(128)} %bitcast.4.place_ref, bf16[512,3072]{1,0:T(8,128)(2,1)S(1)} %copy-done, bf16[2048,3072]{1,0:T(8,128)(2,1)} %all-gather.4.cloned.1.call-done.right_ref), custom_call_target="tpu_custom_call" | custom-call | tf_op jit(solution)/shard_map/pallas_call | solution.py:46
  175.9 10.9 %shard_map.213.refs_0_ = f32[8,1,512,2048]{3,2,1,0:T(8,128)} custom-call(s32[1]{0:T(128)} %bitcast.4.place_ref, bf16[512,3072]{1,0:T(8,128)(2,1)S(1)} %copy-done.3, bf16[2048,3072]{1,0:T(8,128)(2,1)} %all-gather.4.cloned.1.call-done.right_ref), custom_call_target="tpu_custom_call" | custom-call | tf_op jit(solution)/shard_map/pallas_call | solution.py:46
  186.8 13.6 %shard_map.214.refs_0_ = f32[8,1,512,2048]{3,2,1,0:T(8,128)} custom-call(s32[1]{0:T(128)} %get-tuple-element.174.place_ref, bf16[512,3072]{1,0:T(8,128)(2,1)} %collective-permute-done.5.left_ref, bf16[2048,3072]{1,0:T(8,128)(2,1)} %all-gather.4.cloned.1.call-done.right_ref, f32[8,1,512,2048]{3,2,1,0:T(8,128)} %shard_map.212.refs_0_), custom_call_target="tpu_custom_call", output_to_operand_aliasing={{}: (3, {})} | custom-call | tf_op jit(solution)/shard_map/pallas_call | solution.py:46
  200.4 12.5 %shard_map.215.refs_0_ = f32[8,1,512,2048]{3,2,1,0:T(8,128)} custom-call(s32[1]{0:T(128)} %get-tuple-element.175.place_ref, bf16[512,3072]{1,0:T(8,128)(2,1)} %collective-permute-done.3.left_ref, bf16[2048,3072]{1,0:T(8,128)(2,1)} %all-gather.4.cloned.1.call-done.right_ref, f32[8,1,512,2048]{3,2,1,0:T(8,128)} %shard_map.214.refs_0_), custom_call_target="tpu_custom_call", output_to_operand_aliasing={{}: (3, {})} | custom-call | tf_op jit(solution)/shard_map/pallas_call | solution.py:46
  212.9 12.6 %shard_map.216.refs_0_ = f32[8,1,512,2048]{3,2,1,0:T(8,128)} custom-call(s32[1]{0:T(128)} %get-tuple-element.174.place_ref, bf16[512,3072]{1,0:T(8,128)(2,1)} %collective-permute-done.7.left_ref, bf16[2048,3072]{1,0:T(8,128)(2,1)} %all-gather.4.cloned.1.call-done.right_ref, f32[8,1,512,2048]{3,2,1,0:T(8,128)} %shard_map.213.refs_0_), custom_call_target="tpu_custom_call", output_to_operand_aliasing={{}: (3, {})} | custom-call | tf_op jit(solution)/shard_map/pallas_call | solution.py:46
  225.5 11.6 %shard_map.217.refs_0_ = f32[8,1,512,2048]{3,2,1,0:T(8,128)} custom-call(s32[1]{0:T(128)} %get-tuple-element.175.place_ref, bf16[512,3072]{1,0:T(8,128)(2,1)S(1)} %copy-done.2, bf16[2048,3072]{1,0:T(8,128)(2,1)} %all-gather.4.cloned.1.call-done.right_ref, f32[8,1,512,2048]{3,2,1,0:T(8,128)} %shard_map.216.refs_0_), custom_call_target="tpu_custom_call", output_to_operand_aliasing={{}: (3, {})} | custom-call | tf_op jit(solution)/shard_map/pallas_call | solution.py:46
  237.1 1.6 collective-permute-start.10
  238.7 0.1 slice.8
  238.7 0.7 collective-permute-start.1
  239.4 0.0 collective-permute-done.4.left_ref
  239.4 12.3 %shard_map.218.refs_0_ = f32[8,1,512,2048]{3,2,1,0:T(8,128)} custom-call(s32[1]{0:T(128)} %get-tuple-element.176.place_ref, bf16[512,3072]{1,0:T(8,128)(2,1)} %collective-permute-done.6.left_ref, bf16[2048,3072]{1,0:T(8,128)(2,1)} %all-gather.4.cloned.1.call-done.right_ref, f32[8,1,512,2048]{3,2,1,0:T(8,128)} %shard_map.215.refs_0_), custom_call_target="tpu_custom_call", output_to_operand_aliasing={{}: (3, {})} | custom-call | tf_op jit(solution)/shard_map/pallas_call | solution.py:46
  251.8 12.4 %shard_map.219.refs_0_ = f32[8,1,512,2048]{3,2,1,0:T(8,128)} custom-call(s32[1]{0:T(128)} %get-tuple-element.177.place_ref, bf16[512,3072]{1,0:T(8,128)(2,1)} %collective-permute-done.4.left_ref, bf16[2048,3072]{1,0:T(8,128)(2,1)} %all-gather.4.cloned.1.call-done.right_ref, f32[8,1,512,2048]{3,2,1,0:T(8,128)} %shard_map.218.refs_0_), custom_call_target="tpu_custom_call", output_to_operand_aliasing={{}: (3, {})} | custom-call | tf_op jit(solution)/shard_map/pallas_call | solution.py:46
  264.2 8.4 %collective-permute-done.2.left_ref = bf16[384,3072]{1,0:T(8,128)(2,1)} collective-permute-done((bf16[384,3072]{1,0:T(8,128)(2,1)}, bf16[384,3072]{1,0:T(8,128)(2,1)}, u32[]{:S(2)}, u32[]{:S(2)}) %collective-permute-start.2) | collective-permute-done | bytes 2359328 | tf_op jit(solution)/shard_map/ppermute | solution.py:129
  272.6 0.4 collective-permute-start.9
  273.1 16.4 %collective-permute-done.1.left_ref = bf16[128,3072]{1,0:T(8,128)(2,1)} collective-permute-done((bf16[128,3072]{1,0:T(8,128)(2,1)S(1)}, bf16[128,3072]{1,0:T(8,128)(2,1)}, u32[]{:S(2)}, u32[]{:S(2)}) %collective-permute-start.1) | collective-permute-done | bytes 786464 | tf_op jit(solution)/shard_map/ppermute | solution.py:129
  289.5 11.3 %shard_map.220 = bf16[512,2048]{1,0:T(8,128)(2,1)} custom-call(s32[1]{0:T(128)} %constant.93.clone.1.place_ref, bf16[512,3072]{1,0:T(8,128)(2,1)} %collective-permute-done.11.left_ref, bf16[2048,3072]{1,0:T(8,128)(2,1)} %all-gather.6.cloned.1.call-done.right_ref), custom_call_target="tpu_custom_call" | custom-call | tf_op jit(solution)/shard_map/pallas_call | solution.py:46
  300.8 1.6 collective-permute-start.14
  302.4 11.3 %shard_map.221 = bf16[512,2048]{1,0:T(8,128)(2,1)} custom-call(s32[1]{0:T(128)} %constant.93.clone.1.place_ref, bf16[512,3072]{1,0:T(8,128)(2,1)} %collective-permute-done.4.left_ref, bf16[2048,3072]{1,0:T(8,128)(2,1)} %all-gather.8.cloned.1.call-done.right_ref), custom_call_target="tpu_custom_call" | custom-call | tf_op jit(solution)/shard_map/pallas_call | solution.py:46
  313.7 0.5 collective-permute-start.15
  314.2 0.4 collective-permute-start.8
  314.6 12.3 %shard_map.222.refs_0_ = f32[8,1,512,2048]{3,2,1,0:T(8,128)} custom-call(s32[1]{0:T(128)} %get-tuple-element.176.place_ref, bf16[512,3072]{1,0:T(8,128)(2,1)} %collective-permute-done.11.left_ref, bf16[2048,3072]{1,0:T(8,128)(2,1)} %all-gather.4.cloned.1.call-done.right_ref, f32[8,1,512,2048]{3,2,1,0:T(8,128)} %shard_map.217.refs_0_), custom_call_target="tpu_custom_call", output_to_operand_aliasing={{}: (3, {})} | custom-call | tf_op jit(solution)/shard_map/pallas_call | solution.py:46
  326.9 10.8 %shard_map.223.refs_0_ = f32[8,1,512,2048]{3,2,1,0:T(8,128)} custom-call(s32[1]{0:T(128)} %get-tuple-element.177.place_ref, bf16[384,3072]{1,0:T(8,128)(2,1)} %collective-permute-done.2.left_ref, bf16[2048,3072]{1,0:T(8,128)(2,1)} %all-gather.4.cloned.1.call-done.right_ref, f32[8,1,512,2048]{3,2,1,0:T(8,128)} %shard_map.222.refs_0_), custom_call_target="tpu_custom_call", output_to_operand_aliasing={{}: (3, {})} | custom-call | tf_op jit(solution)/shard_map/pallas_call | solution.py:46
  337.7 9.2 %shard_map.224.refs_0_ = f32[8,1,512,2048]{3,2,1,0:T(8,128)} custom-call(s32[1]{0:T(128)} %get-tuple-element.177.place_ref, bf16[128,3072]{1,0:T(8,128)(2,1)} %collective-permute-done.1.left_ref, bf16[2048,3072]{1,0:T(8,128)(2,1)} %all-gather.4.cloned.1.call-done.right_ref, f32[8,1,512,2048]{3,2,1,0:T(8,128)} %shard_map.223.refs_0_), custom_call_target="tpu_custom_call", output_to_operand_aliasing={{}: (3, {})} | custom-call | tf_op jit(solution)/shard_map/pallas_call | solution.py:46
  346.9 8.3 %collective-permute-done.10.left_ref = bf16[512,3072]{1,0:T(8,128)(2,1)S(1)} collective-permute-done((bf16[512,3072]{1,0:T(8,128)(2,1)}, bf16[512,3072]{1,0:T(8,128)(2,1)S(1)}, u32[]{:S(2)}, u32[]{:S(2)}) %collective-permute-start.10) | collective-permute-done | bytes 3145760 | tf_op jit(solution)/shard_map/ppermute | solution.py:129
  355.2 9.1 %shard_map.225 = bf16[384,2048]{1,0:T(8,128)(2,1)} custom-call(s32[1]{0:T(128)} %constant.93.clone.1.place_ref, bf16[512,3072]{1,0:T(8,128)(2,1)S(1)} %collective-permute-done.10.left_ref, bf16[2048,3072]{1,0:T(8,128)(2,1)} %all-gather.6.cloned.1.call-done.right_ref), custom_call_target="tpu_custom_call" | custom-call | tf_op jit(solution)/shard_map/pallas_call | solution.py:46
  364.3 1.6 collective-permute-start.16
  373.3 9.0 %shard_map.226 = bf16[384,2048]{1,0:T(8,128)(2,1)S(1)} custom-call(s32[1]{0:T(128)} %constant.93.clone.1.place_ref, bf16[384,3072]{1,0:T(8,128)(2,1)} %collective-permute-done.9.left_ref, bf16[2048,3072]{1,0:T(8,128)(2,1)} %all-gather.8.cloned.1.call-done.right_ref), custom_call_target="tpu_custom_call" | custom-call | tf_op jit(solution)/shard_map/pallas_call | solution.py:46
  382.3 0.7 collective-permute-start.13
  383.0 11.4 %shard_map.227 = f32[8,1,512,2048]{3,2,1,0:T(8,128)} custom-call(s32[1]{0:T(128)} %get-tuple-element.179.place_ref, bf16[512,3072]{1,0:T(8,128)(2,1)S(1)} %collective-permute-done.10.left_ref, bf16[2048,3072]{1,0:T(8,128)(2,1)} %all-gather.4.cloned.1.call-done.right_ref, f32[8,1,512,2048]{3,2,1,0:T(8,128)} %shard_map.219.refs_0_), custom_call_target="tpu_custom_call", output_to_operand_aliasing={{}: (3, {})} | custom-call | tf_op jit(solution)/shard_map/pallas_call | solution.py:46
  394.4 10.8 %shard_map.228 = f32[8,1,512,2048]{3,2,1,0:T(8,128)} custom-call(s32[1]{0:T(128)} %get-tuple-element.173.place_ref, bf16[384,3072]{1,0:T(8,128)(2,1)} %collective-permute-done.9.left_ref, bf16[2048,3072]{1,0:T(8,128)(2,1)} %all-gather.4.cloned.1.call-done.right_ref, f32[8,1,512,2048]{3,2,1,0:T(8,128)} %shard_map.224.refs_0_), custom_call_target="tpu_custom_call", output_to_operand_aliasing={{}: (3, {})} | custom-call | tf_op jit(solution)/shard_map/pallas_call | solution.py:46
  405.2 7.7 %shard_map.229 = bf16[128,2048]{1,0:T(8,128)(2,1)S(1)} custom-call(s32[1]{0:T(128)} %constant.93.clone.1.place_ref, bf16[128,3072]{1,0:T(8,128)(2,1)} %collective-permute-done.8.left_ref, bf16[2048,3072]{1,0:T(8,128)(2,1)} %all-gather.8.cloned.1.call-done.right_ref), custom_call_target="tpu_custom_call" | custom-call | tf_op jit(solution)/shard_map/pallas_call | solution.py:46
  412.9 0.4 collective-permute-start.12
  413.3 4.1 convert_dynamic-update-slice_fusion.1.refs_0_
  417.4 7.5 %shard_map.230 = bf16[128,2048]{1,0:T(8,128)(2,1)S(1)} custom-call(s32[1]{0:T(128)} %constant.93.clone.1.place_ref, bf16[512,3072]{1,0:T(8,128)(2,1)S(1)} %collective-permute-done.10.left_ref, bf16[2048,3072]{1,0:T(8,128)(2,1)} %all-gather.6.cloned.1.call-done.right_ref), custom_call_target="tpu_custom_call" | custom-call | tf_op jit(solution)/shard_map/pallas_call | solution.py:46
  425.0 1.8 collective-permute-start.17
  426.7 9.1 %shard_map.231 = f32[8,1,512,2048]{3,2,1,0:T(8,128)} custom-call(s32[1]{0:T(128)} %get-tuple-element.173.place_ref, bf16[128,3072]{1,0:T(8,128)(2,1)} %collective-permute-done.8.left_ref, bf16[2048,3072]{1,0:T(8,128)(2,1)} %all-gather.4.cloned.1.call-done.right_ref, ...), custom_call_target="tpu_custom_call", output_to_operand_aliasing={{}: (3, {})} | custom-call | tf_op jit(solution)/shard_map/pallas_call | solution.py:46
  435.9 4.1 convert_dynamic-update-slice_fusion
  440.0 3.4 convert_dynamic-update-slice_fusion.3
  443.5 2.1 convert_dynamic-update-slice_fusion.2
  445.5 1.1 convert_dynamic-update-slice_fusion.5
  446.6 1.1 convert_dynamic-update-slice_fusion.4
  (24 shorter events, 0.1 us)
Async XLA Ops:
  7.2 157.8 %all-gather.4.cloned.1.call-start = ((), (), s32[]{:S(2)}) async-start(), calls=%async_computation | async-start | bytes 15728640 | tf_op jit(solution)/shard_map/all_gather | solution.py:106
  7.9 281.6 %all-gather.6.cloned.1.call-start = ((), (), s32[]{:S(2)}) async-start(), calls=%async_computation.1 | async-start | bytes 15728640 | tf_op jit(solution)/shard_map/all_gather | solution.py:106
  7.9 71.4 %collective-permute-start.5 = (bf16[512,3072]{1,0:T(8,128)(2,1)}, bf16[512,3072]{1,0:T(8,128)(2,1)}, u32[]{:S(2)}, u32[]{:S(2)}) collective-permute-start(bf16[512,3072]{1,0:T(8,128)(2,1)} %left_ref), channel_id=1, source_target_pairs={{0,8},{8,16},{16,24},{24,28},{28,20},{20,12},{12,4},{4,0},{1,9},{9... | collective-permute-start | bytes 9437192 | tf_op jit(solution)/shard_map/ppermute | solution.py:129
  11.0 69.9 %collective-permute-start.3 = (bf16[512,3072]{1,0:T(8,128)(2,1)}, bf16[512,3072]{1,0:T(8,128)(2,1)}, u32[]{:S(2)}, u32[]{:S(2)}) collective-permute-start(bf16[512,3072]{1,0:T(8,128)(2,1)} %left_ref), channel_id=1, source_target_pairs={{8,0},{16,8},{24,16},{28,24},{20,28},{12,20},{4,12},{0,4},{9,1},{1... | collective-permute-start | bytes 9437192 | tf_op jit(solution)/shard_map/ppermute | solution.py:129
  16.7 141.7 %copy-start.5 = (s32[8]{0:T(128)S(1)}, s32[8]{0:T(128)}, u32[]{:S(2)}) copy-start(s32[8]{0:T(128)} %constant.108.clone) | copy-start | bytes 100
  16.7 147.6 %copy-start.4 = (s32[8]{0:T(128)S(1)}, s32[8]{0:T(128)}, u32[]{:S(2)}) copy-start(s32[8]{0:T(128)} %constant.109.clone) | copy-start | bytes 100
  16.7 148.3 %copy-start = (bf16[512,3072]{1,0:T(8,128)(2,1)S(1)}, bf16[512,3072]{1,0:T(8,128)(2,1)}, u32[]{:S(2)}) copy-start(bf16[512,3072]{1,0:T(8,128)(2,1)} %left_ref) | copy-start | bytes 9437188
  80.9 221.4 %all-gather.8.cloned.1.call-start = ((), (), s32[]{:S(2)}) async-start(), calls=%async_computation.2 | async-start | bytes 15728640 | tf_op jit(solution)/shard_map/all_gather | solution.py:106
  81.7 71.4 %collective-permute-start.7 = (bf16[512,3072]{1,0:T(8,128)(2,1)}, bf16[512,3072]{1,0:T(8,128)(2,1)}, u32[]{:S(2)}, u32[]{:S(2)}) collective-permute-start(bf16[512,3072]{1,0:T(8,128)(2,1)} %subtract_convert_fusion.left_ref), channel_id=1, source_target_pairs={{0,8},{8,16},{16,24},{24,28},{28,20},{20,12},{12,4},{4,0},{1,9},{9... | collective-permute-start | bytes 9437192 | tf_op jit(solution)/shard_map/ppermute | solution.py:129
  83.3 71.4 %collective-permute-start = (bf16[512,3072]{1,0:T(8,128)(2,1)}, bf16[512,3072]{1,0:T(8,128)(2,1)S(1)}, u32[]{:S(2)}, u32[]{:S(2)}) collective-permute-start(bf16[512,3072]{1,0:T(8,128)(2,1)} %subtract_convert_fusion.left_ref), channel_id=1, source_target_pairs={{8,0},{16,8},{24,16},{28,24},{20,28},{12,20},{4,12},{0,4},{9,1},{1... | collective-permute-start | bytes 9437192 | tf_op jit(solution)/shard_map/ppermute | solution.py:129
  83.7 153.4 %collective-permute-start.6 = (bf16[512,3072]{1,0:T(8,128)(2,1)}, bf16[512,3072]{1,0:T(8,128)(2,1)}, u32[]{:S(2)}, u32[]{:S(2)}) collective-permute-start(bf16[512,3072]{1,0:T(8,128)(2,1)} %collective-permute-done.5.left_ref), channel_id=1, source_target_pairs={{0,8},{8,16},{16,24},{24,28},{28,20},{20,12},{12,4},{4,0},{1,9},{9... | collective-permute-start | bytes 9437192 | tf_op jit(solution)/shard_map/ppermute | solution.py:129
  85.3 154.1 %collective-permute-start.4 = (bf16[512,3072]{1,0:T(8,128)(2,1)}, bf16[512,3072]{1,0:T(8,128)(2,1)}, u32[]{:S(2)}, u32[]{:S(2)}) collective-permute-start(bf16[512,3072]{1,0:T(8,128)(2,1)} %collective-permute-done.3.left_ref), channel_id=1, source_target_pairs={{8,0},{16,8},{24,16},{28,24},{20,28},{12,20},{4,12},{0,4},{9,1},{1... | collective-permute-start | bytes 9437192 | tf_op jit(solution)/shard_map/ppermute | solution.py:129
  153.1 136.4 %collective-permute-start.11 = (bf16[512,3072]{1,0:T(8,128)(2,1)}, bf16[512,3072]{1,0:T(8,128)(2,1)}, u32[]{:S(2)}, u32[]{:S(2)}) collective-permute-start(bf16[512,3072]{1,0:T(8,128)(2,1)} %collective-permute-done.7.left_ref), channel_id=1, source_target_pairs={{0,8},{8,16},{16,24},{24,28},{28,20},{20,12},{12,4},{4,0},{1,9},{9... | collective-permute-start | bytes 9437192 | tf_op jit(solution)/shard_map/ppermute | solution.py:129
  156.2 1.7 copy-start.1
  157.9 114.7 %collective-permute-start.2 = (bf16[384,3072]{1,0:T(8,128)(2,1)}, bf16[384,3072]{1,0:T(8,128)(2,1)}, u32[]{:S(2)}, u32[]{:S(2)}) collective-permute-start(bf16[384,3072]{1,0:T(8,128)(2,1)} %slice.9), channel_id=1, source_target_pairs={{8,0},{16,8},{24,16},{28,24},{20,28},{12,20},{4,12},{0,4},{9,1},{1... | collective-permute-start | bytes 7077896 | tf_op jit(solution)/shard_map/ppermute | solution.py:129
  165.0 10.9 %copy-start.3 = (bf16[512,3072]{1,0:T(8,128)(2,1)S(1)}, bf16[512,3072]{1,0:T(8,128)(2,1)}, u32[]{:S(2)}) copy-start(bf16[512,3072]{1,0:T(8,128)(2,1)} %subtract_convert_fusion.left_ref) | copy-start | bytes 9437188
  212.9 12.6 %copy-start.2 = (bf16[512,3072]{1,0:T(8,128)(2,1)S(1)}, bf16[512,3072]{1,0:T(8,128)(2,1)}, u32[]{:S(2)}) copy-start(bf16[512,3072]{1,0:T(8,128)(2,1)} %copy-done.1) | copy-start | bytes 9437188
  237.1 118.1 %collective-permute-start.10 = (bf16[512,3072]{1,0:T(8,128)(2,1)}, bf16[512,3072]{1,0:T(8,128)(2,1)S(1)}, u32[]{:S(2)}, u32[]{:S(2)}) collective-permute-start(bf16[512,3072]{1,0:T(8,128)(2,1)} %collective-permute-done.6.left_ref), channel_id=1, source_target_pairs={{0,8},{8,16},{16,24},{24,28},{28,20},{20,12},{12,4},{4,0},{1,9},{9... | collective-permute-start | bytes 9437192 | tf_op jit(solution)/shard_map/ppermute | solution.py:129
  238.7 50.7 %collective-permute-start.1 = (bf16[128,3072]{1,0:T(8,128)(2,1)S(1)}, bf16[128,3072]{1,0:T(8,128)(2,1)}, u32[]{:S(2)}, u32[]{:S(2)}) collective-permute-start(bf16[128,3072]{1,0:T(8,128)(2,1)S(1)} %slice.8), channel_id=1, source_target_pairs={{8,0},{16,8},{24,16},{28,24},{20,28},{12,20},{4,12},{0,4},{9,1},{1... | collective-permute-start | bytes 2359304 | tf_op jit(solution)/shard_map/ppermute | solution.py:129
  272.6 74.3 %collective-permute-start.9 = (bf16[384,3072]{1,0:T(8,128)(2,1)}, bf16[384,3072]{1,0:T(8,128)(2,1)}, u32[]{:S(2)}, u32[]{:S(2)}) collective-permute-start(bf16[384,3072]{1,0:T(8,128)(2,1)} %collective-permute-done.2.left_ref), channel_id=1, source_target_pairs={{8,0},{16,8},{24,16},{28,24},{20,28},{12,20},{4,12},{0,4},{9,1},{1... | collective-permute-start | bytes 7077896 | tf_op jit(solution)/shard_map/ppermute | solution.py:129
  300.8 112.5 %collective-permute-start.14 = (bf16[512,2048]{1,0:T(8,128)(2,1)}, bf16[512,2048]{1,0:T(8,128)(2,1)}, u32[]{:S(2)}, u32[]{:S(2)}) collective-permute-start(bf16[512,2048]{1,0:T(8,128)(2,1)} %shard_map.220), channel_id=1, source_target_pairs={{0,8},{8,16},{16,24},{24,28},{28,20},{20,12},{12,4},{4,0},{1,9},{9... | collective-permute-start | bytes 6291464 | tf_op jit(solution)/shard_map/ppermute | solution.py:137
  313.7 122.2 %collective-permute-start.15 = (bf16[512,2048]{1,0:T(8,128)(2,1)}, bf16[512,2048]{1,0:T(8,128)(2,1)}, u32[]{:S(2)}, u32[]{:S(2)}) collective-permute-start(bf16[512,2048]{1,0:T(8,128)(2,1)} %shard_map.221), channel_id=1, source_target_pairs={{8,0},{16,8},{24,16},{28,24},{20,28},{12,20},{4,12},{0,4},{9,1},{1... | collective-permute-start | bytes 6291464 | tf_op jit(solution)/shard_map/ppermute | solution.py:137
  314.2 91.0 %collective-permute-start.8 = (bf16[128,3072]{1,0:T(8,128)(2,1)}, bf16[128,3072]{1,0:T(8,128)(2,1)}, u32[]{:S(2)}, u32[]{:S(2)}) collective-permute-start(bf16[128,3072]{1,0:T(8,128)(2,1)} %collective-permute-done.1.left_ref), channel_id=1, source_target_pairs={{8,0},{16,8},{24,16},{28,24},{20,28},{12,20},{4,12},{0,4},{9,1},{1... | collective-permute-start | bytes 2359304 | tf_op jit(solution)/shard_map/ppermute | solution.py:129
  364.3 75.7 %collective-permute-start.16 = (bf16[384,2048]{1,0:T(8,128)(2,1)}, bf16[384,2048]{1,0:T(8,128)(2,1)}, u32[]{:S(2)}, u32[]{:S(2)}) collective-permute-start(bf16[384,2048]{1,0:T(8,128)(2,1)} %shard_map.225), channel_id=1, source_target_pairs={{0,8},{8,16},{16,24},{24,28},{28,20},{20,12},{12,4},{4,0},{1,9},{9... | collective-permute-start | bytes 4718600 | tf_op jit(solution)/shard_map/ppermute | solution.py:137
  382.3 61.2 %collective-permute-start.13 = (bf16[384,2048]{1,0:T(8,128)(2,1)S(1)}, bf16[384,2048]{1,0:T(8,128)(2,1)S(1)}, u32[]{:S(2)}, u32[]{:S(2)}) collective-permute-start(bf16[384,2048]{1,0:T(8,128)(2,1)S(1)} %shard_map.226), channel_id=1, source_target_pairs={{8,0},{16,8},{24,16},{28,24},{20,28},{12,20},{4,12},{0,4},{9,1},{1... | collective-permute-start | bytes 4718600 | tf_op jit(solution)/shard_map/ppermute | solution.py:137
  412.9 32.6 %collective-permute-start.12 = (bf16[128,2048]{1,0:T(8,128)(2,1)S(1)}, bf16[128,2048]{1,0:T(8,128)(2,1)S(1)}, u32[]{:S(2)}, u32[]{:S(2)}) collective-permute-start(bf16[128,2048]{1,0:T(8,128)(2,1)S(1)} %shard_map.229), channel_id=1, source_target_pairs={{8,0},{16,8},{24,16},{28,24},{20,28},{12,20},{4,12},{0,4},{9,1},{1... | collective-permute-start | bytes 1572872 | tf_op jit(solution)/shard_map/ppermute | solution.py:137
  425.0 21.6 %collective-permute-start.17 = (bf16[128,2048]{1,0:T(8,128)(2,1)S(1)}, bf16[128,2048]{1,0:T(8,128)(2,1)S(1)}, u32[]{:S(2)}, u32[]{:S(2)}) collective-permute-start(bf16[128,2048]{1,0:T(8,128)(2,1)S(1)} %shard_map.230), channel_id=1, source_target_pairs={{0,8},{8,16},{16,24},{24,28},{28,20},{20,12},{12,4},{4,0},{1,9},{9... | collective-permute-start | bytes 1572872 | tf_op jit(solution)/shard_map/ppermute | solution.py:137
Sparse Core Ops, SparseCore 0:
  9.6 84.7 all-gather.3
  95.9 82.0 all-gather.5
  179.7 82.0 all-gather.7

commit v6 on v4

--- a/solution.py
+++ b/solution.py
@@ -107,61 +107,57 @@
     raw = {chain: max(hops - 1, min(hops, 1)) for chain, hops in reach.items()}
     at = {(which, way): [(q, d)[which]] for which in range(2) for way in range(2)}
 
-    def start(which, step):
-        for way in range(2):
-            chain = (which, way)
-            if step <= raw[chain]:
-                block = at[chain][step - 1]
-                block = block if step == 1 else tie(block)
-                at[chain].append(lax.ppermute(block, "wide", pairs[way]))
+    def start(chain, step):
+        if step <= raw[chain]:
+            block = at[chain][step - 1]
+            block = block if step == 1 else tie(block)
+            at[chain].append(lax.ppermute(block, "wide", pairs[chain[1]]))
 
-    def arrivals(which, step):
-        return [at[which, way][step] for way in range(2) if step <= raw[which, way]]
+    def send(chain, step, first_row, rows):
+        which, way = chain
+        result = product(tie(at[chain][step]), right_next[way], first_row=first_row, rows=rows)
+        now.append(result)
+        moved = lax.ppermute(result, "wide", pairs[way])
+        results.append((which, owner_of(way, step + 1), moved, first_row))
 
-    start(0, 1)
-    start(1, 1)
+    def is_last(chain, step):
+        return step == raw[chain] < reach[chain]
+
+    far_chains, near_chains = ((0, 0), (1, 1)), ((1, 0), (0, 1))
+    for chain in ((0, 0), (0, 1), (1, 1), (1, 0)):
+        start(chain, 1)
     right_next = [None, None]
     results = []
     for step in range(1, far + 1):
-        for which in range(2):
-            if not arrivals(which, step):
+        for chains in (far_chains, near_chains):
+            here = [chain for chain in chains if step <= raw[chain]]
+            if not here:
                 continue
-            now[:] = arrivals(which, step)
-            start(which, step + 1)
-            if step == 1 and which == 0:
+            now[:] = [at[chain][step] for chain in (raw if step == 1 else here) if step <= raw[chain]]
+            if step == 1 and chains == far_chains and near > 0:
+                moved = lax.optimization_barrier((at[0, 0][1], at[0, 1][1]))
+                moved = lax.optimization_barrier((*moved, at[1, 0][1], at[1, 1][1]))
                 for way in range(2):
-                    if raw[0, 1 - way] >= 1:
-                        right_next[way] = gather(at[0, 1 - way][1], d)
-            together = step in (1, far - 1)
-            if which == 0 and together:
+                    right_next[way] = gather(moved[1 - way])
+            for chain in chains:
+                start(chain, step + 1)
+            cut = owned_rows - owned_rows // QUARTERS if step == far - 1 else owned_rows
+            late = [chain for chain in here if is_last(chain, step) and step < far - 1 and chain[1]]
+            for chain in here:
+                if is_last(chain, step) and chain not in late:
+                    send(chain, step, 0, cut)
+                    if cut < owned_rows:
+                        send(chain, step, cut, owned_rows - cut)
+            if step == 1 and chains == far_chains:
                 continue
-            if which == 1:
-                for sent, way in ((1, 0), (0, 1), (1, 1), (0, 0)):
-                    if step == raw[sent, way] < reach[sent, way]:
-                        cut = owned_rows - owned_rows // QUARTERS if step == far - 1 else owned_rows
-                        for first_row, rows in ((0, cut), (cut, owned_rows - cut)):
-                            if rows == 0:
-                                continue
-                            result = product(
-                                tie(at[sent, way][step]),
-                                right_next[way],
-                                first_row=first_row,
-                                rows=rows,
-                            )
-                            now.append(result)
-                            results.append((
-                                sent,
-                                owner_of(way, step + 1),
-                                lax.ppermute(result, "wide", pairs[way]),
-                                first_row,
-                            ))
             if step == 1:
                 put(0, lax.axis_index("wide"), q)
                 put(1, lax.axis_index("wide"), d)
-            for own in range(2) if together else (which,):
-                for way in range(2):
-                    if step <= raw[own, way]:
-                        put(own, owner_of(way, step), at[own, way][step])
+            for chain in (*far_chains, *near_chains) if step == 1 else here:
+                if step <= raw[chain]:
+                    put(chain[0], owner_of(chain[1], step), at[chain][step])
+            for chain in late:
+                send(chain, step, 0, owned_rows)
     now[:] = []
     for result in sorted(results, key=lambda result: result[3]):
         put_arrived(*result)

time: 453 us -> 453 us (level)
  waiting for transfers between devices: 186 us -> 179 us
  local copies, waits for them, and re-layouts: 28.8 us -> 35.5 us
    unnamed x34 -> x28, local copies, waits for them, and re-layouts: 27.5 us -> 34.2 us
    ppermute x16, waiting for transfers between devices: 185 us -> 178 us  [the longest x10 175 us: start(): at[chain].append(lax.ppermute(block, 'wide', pairs[chain[1]]))]
where the time goes in v6:
time: 453 us; the launch traced here: 452 us
  waiting for transfers between devices  179 us (40%)
  Pallas kernels  171 us (38%)
  local copies, waits for them, and re-layouts  35.5 us (8%)
  between operations  26.8 us (6%)
  other arithmetic  21.5 us (5%)
  starting transfers between devices  17.5 us (4%)
    ppermute x10, waiting for transfers between devices, start(): at[chain].append(lax.ppermute(block, 'wide', pairs[chain[1]]))  175 us
    pallas_call x18, Pallas kernels, product(): pl.pallas_call(functools.partial(product_kernel, 1.0 / tokens), out_shape...  171 us
    unnamed x28, local copies, waits for them, and re-layouts  34.2 us
    dynamic_update_slice x6, other arithmetic, put_arrived(): lax.dynamic_update_slice(outs[which], tie(block).astype(jnp.float32)[None...  15.9 us
    ppermute x10, starting transfers between devices, start(): at[chain].append(lax.ppermute(block, 'wide', pairs[chain[1]]))  11.2 us
  transfers between devices with their start and end apart: 19, of which 8 were waited for; matrix products, arithmetic and copies ran while one was open for 5% of the time, Pallas kernels for 38%

profile of v6, /device:TPU:0, one launch (start us, length us, event | category | flops | bytes accessed | tf_op | source)
XLA Modules:
  0.0 451.8 jit_solution(8888003640364304098)
XLA Ops:
  7.2 0.0 all-gather.4.cloned.1.call-start
  7.2 0.7 all-gather.4.cloned.1.call-update
  7.9 0.0 all-gather.6.cloned.1.call-start
  8.0 3.1 collective-permute-start.1
  11.1 0.0 collective-permute-start.2
  11.1 5.6 %subtract_convert_fusion.left_ref = bf16[512,3072]{1,0:T(8,128)(2,1)} fusion(bf16[512,3072]{1,0:T(8,128)(2,1)} %left_ref, bf16[512,3072]{1,0:T(8,128)(2,1)} %param.20), kind=kLoop, calls=%fused_computation | loop fusion | flops 6291456 | bytes 9437184 | tf_op jit(solution)/shard_map/convert_element_type | solution.py:102
  16.7 2.0 collective-permute-start
  18.6 0.1 collective-permute-start.3
  18.7 61.6 %collective-permute-done.1.left_ref = bf16[512,3072]{1,0:T(8,128)(2,1)} collective-permute-done((bf16[512,3072]{1,0:T(8,128)(2,1)}, bf16[512,3072]{1,0:T(8,128)(2,1)}, u32[]{:S(2)}, u32[]{:S(2)}) %collective-permute-start.1) | collective-permute-done | bytes 3145760 | tf_op jit(solution)/shard_map/ppermute | solution.py:114
  80.2 2.2 collective-permute-done.2.left_ref
  82.4 65.9 %collective-permute-done.left_ref = bf16[512,3072]{1,0:T(8,128)(2,1)} collective-permute-done((bf16[512,3072]{1,0:T(8,128)(2,1)}, bf16[512,3072]{1,0:T(8,128)(2,1)}, u32[]{:S(2)}, u32[]{:S(2)}) %collective-permute-start) | collective-permute-done | bytes 3145760 | tf_op jit(solution)/shard_map/ppermute | solution.py:114
  148.3 0.0 all-gather.6.cloned.1.call-update
  148.4 0.0 all-gather.8.cloned.1.call-start
  148.4 0.7 all-gather.8.cloned.1.call-update
  149.1 0.4 collective-permute-start.4
  149.5 1.7 collective-permute-start.5
  151.2 0.3 collective-permute-start.8
  151.5 1.7 collective-permute-start.9
  153.2 0.6 dynamic_slice.51
  159.2 0.7 fusion
  159.9 6.5 %copy-done = bf16[2048,3072]{1,0:T(8,128)(2,1)S(1)} copy-done((bf16[2048,3072]{1,0:T(8,128)(2,1)S(1)}, bf16[2048,3072]{1,0:T(8,128)(2,1)}, u32[]{:S(2)}) %copy-start) | copy-done | bytes 12582936
  166.5 8.3 %shard_map.194.refs_0_ = f32[8,1,512,2048]{3,2,1,0:T(8,128)} custom-call(s32[1]{0:T(128)} %bitcast.2.place_ref, bf16[512,3072]{1,0:T(8,128)(2,1)S(1)} %copy-done.8, bf16[2048,3072]{1,0:T(8,128)(2,1)S(1)} %copy-done), custom_call_target="tpu_custom_call" | custom-call | tf_op jit(solution)/shard_map/pallas_call | solution.py:46
  174.8 10.2 %shard_map.195.refs_0_ = f32[8,1,512,2048]{3,2,1,0:T(8,128)} custom-call(s32[1]{0:T(128)} %bitcast.2.place_ref, bf16[512,3072]{1,0:T(8,128)(2,1)} %subtract_convert_fusion.left_ref, bf16[2048,3072]{1,0:T(8,128)(2,1)S(1)} %copy-done.1), custom_call_target="tpu_custom_call" | custom-call | tf_op jit(solution)/shard_map/pallas_call | solution.py:46
  185.0 10.9 %shard_map.196.refs_0_ = f32[8,1,512,2048]{3,2,1,0:T(8,128)} custom-call(s32[1]{0:T(128)} %get-tuple-element.164.place_ref, bf16[512,3072]{1,0:T(8,128)(2,1)} %collective-permute-done.1.left_ref, bf16[2048,3072]{1,0:T(8,128)(2,1)S(1)} %copy-done.1, f32[8,1,512,2048]{3,2,1,0:T(8,128)} %shard_map.194.refs_0_), custom_call_target="tpu_custom_call", output_to_operand_aliasing={{}: (3, {})} | custom-call | tf_op jit(solution)/shard_map/pallas_call | solution.py:46
  195.9 10.8 %shard_map.197.refs_0_ = f32[8,1,512,2048]{3,2,1,0:T(8,128)} custom-call(s32[1]{0:T(128)} %get-tuple-element.165.place_ref, bf16[512,3072]{1,0:T(8,128)(2,1)} %collective-permute-done.left_ref, bf16[2048,3072]{1,0:T(8,128)(2,1)S(1)} %copy-done.1, f32[8,1,512,2048]{3,2,1,0:T(8,128)} %shard_map.195.refs_0_), custom_call_target="tpu_custom_call", output_to_operand_aliasing={{}: (3, {})} | custom-call | tf_op jit(solution)/shard_map/pallas_call | solution.py:46
  206.6 10.9 %shard_map.198.refs_0_ = f32[8,1,512,2048]{3,2,1,0:T(8,128)} custom-call(s32[1]{0:T(128)} %get-tuple-element.164.place_ref, bf16[512,3072]{1,0:T(8,128)(2,1)} %collective-permute-done.3.left_ref, bf16[2048,3072]{1,0:T(8,128)(2,1)S(1)} %copy-done.1, f32[8,1,512,2048]{3,2,1,0:T(8,128)} %shard_map.197.refs_0_), custom_call_target="tpu_custom_call", output_to_operand_aliasing={{}: (3, {})} | custom-call | tf_op jit(solution)/shard_map/pallas_call | solution.py:46
  217.5 10.8 %shard_map.199.refs_0_ = f32[8,1,512,2048]{3,2,1,0:T(8,128)} custom-call(s32[1]{0:T(128)} %get-tuple-element.165.place_ref, bf16[512,3072]{1,0:T(8,128)(2,1)} %collective-permute-done.2.left_ref, bf16[2048,3072]{1,0:T(8,128)(2,1)S(1)} %copy-done.1, f32[8,1,512,2048]{3,2,1,0:T(8,128)} %shard_map.196.refs_0_), custom_call_target="tpu_custom_call", output_to_operand_aliasing={{}: (3, {})} | custom-call | tf_op jit(solution)/shard_map/pallas_call | solution.py:46
  228.3 0.9 collective-permute-start.6
  229.2 1.1 collective-permute-start.7
  230.3 10.8 %shard_map.200.refs_0_ = f32[8,1,512,2048]{3,2,1,0:T(8,128)} custom-call(s32[1]{0:T(128)} %get-tuple-element.161.place_ref, bf16[512,3072]{1,0:T(8,128)(2,1)} %collective-permute-done.5.left_ref, bf16[2048,3072]{1,0:T(8,128)(2,1)S(1)} %copy-done.1, f32[8,1,512,2048]{3,2,1,0:T(8,128)} %shard_map.199.refs_0_), custom_call_target="tpu_custom_call", output_to_operand_aliasing={{}: (3, {})} | custom-call | tf_op jit(solution)/shard_map/pallas_call | solution.py:46
  241.2 11.5 %shard_map.201.refs_0_ = f32[8,1,512,2048]{3,2,1,0:T(8,128)} custom-call(s32[1]{0:T(128)} %get-tuple-element.162.place_ref, bf16[512,3072]{1,0:T(8,128)(2,1)} %collective-permute-done.4.left_ref, bf16[2048,3072]{1,0:T(8,128)(2,1)S(1)} %copy-done.1, f32[8,1,512,2048]{3,2,1,0:T(8,128)} %shard_map.198.refs_0_), custom_call_target="tpu_custom_call", output_to_operand_aliasing={{}: (3, {})} | custom-call | tf_op jit(solution)/shard_map/pallas_call | solution.py:46
  252.6 35.3 %collective-permute-done.8.left_ref = bf16[512,3072]{1,0:T(8,128)(2,1)} collective-permute-done((bf16[512,3072]{1,0:T(8,128)(2,1)}, bf16[512,3072]{1,0:T(8,128)(2,1)}, u32[]{:S(2)}, u32[]{:S(2)}) %collective-permute-start.8) | collective-permute-done | bytes 3145760 | tf_op jit(solution)/shard_map/ppermute | solution.py:114
  287.9 0.3 collective-permute-done.9.left_ref
  288.2 4.6 %copy-done.3 = bf16[2048,3072]{1,0:T(8,128)(2,1)S(1)} copy-done((bf16[2048,3072]{1,0:T(8,128)(2,1)S(1)}, bf16[2048,3072]{1,0:T(8,128)(2,1)}, u32[]{:S(2)}) %copy-start.3) | copy-done | bytes 12582936
  292.9 10.0 %shard_map.202 = bf16[512,2048]{1,0:T(8,128)(2,1)} custom-call(s32[1]{0:T(128)} %constant.89.clone.1.place_ref, bf16[512,3072]{1,0:T(8,128)(2,1)} %collective-permute-done.9.left_ref, bf16[2048,3072]{1,0:T(8,128)(2,1)S(1)} %copy-done.3), custom_call_target="tpu_custom_call" | custom-call | tf_op jit(solution)/shard_map/pallas_call | solution.py:46
  302.9 1.7 collective-permute-start.12
  304.6 4.7 %copy-done.2 = bf16[2048,3072]{1,0:T(8,128)(2,1)S(1)} copy-done((bf16[2048,3072]{1,0:T(8,128)(2,1)S(1)}, bf16[2048,3072]{1,0:T(8,128)(2,1)}, u32[]{:S(2)}) %copy-start.2) | copy-done | bytes 12582936
  309.3 10.8 %shard_map.203.refs_0_ = f32[8,1,512,2048]{3,2,1,0:T(8,128)} custom-call(s32[1]{0:T(128)} %get-tuple-element.161.place_ref, bf16[512,3072]{1,0:T(8,128)(2,1)} %collective-permute-done.9.left_ref, bf16[2048,3072]{1,0:T(8,128)(2,1)S(1)} %copy-done.2, f32[8,1,512,2048]{3,2,1,0:T(8,128)} %shard_map.201.refs_0_), custom_call_target="tpu_custom_call", output_to_operand_aliasing={{}: (3, {})} | custom-call | tf_op jit(solution)/shard_map/pallas_call | solution.py:46
  320.1 10.9 %shard_map.204.refs_0_ = f32[8,1,512,2048]{3,2,1,0:T(8,128)} custom-call(s32[1]{0:T(128)} %get-tuple-element.162.place_ref, bf16[512,3072]{1,0:T(8,128)(2,1)} %collective-permute-done.8.left_ref, bf16[2048,3072]{1,0:T(8,128)(2,1)S(1)} %copy-done.2, f32[8,1,512,2048]{3,2,1,0:T(8,128)} %shard_map.200.refs_0_), custom_call_target="tpu_custom_call", output_to_operand_aliasing={{}: (3, {})} | custom-call | tf_op jit(solution)/shard_map/pallas_call | solution.py:46
  331.0 4.6 %copy-done.6 = bf16[2048,3072]{1,0:T(8,128)(2,1)S(1)} copy-done((bf16[2048,3072]{1,0:T(8,128)(2,1)S(1)}, bf16[2048,3072]{1,0:T(8,128)(2,1)}, u32[]{:S(2)}) %copy-start.6) | copy-done | bytes 12582936
  335.6 10.0 %shard_map.211 = bf16[512,2048]{1,0:T(8,128)(2,1)} custom-call(s32[1]{0:T(128)} %constant.89.clone.1.place_ref, bf16[512,3072]{1,0:T(8,128)(2,1)} %collective-permute-done.8.left_ref, bf16[2048,3072]{1,0:T(8,128)(2,1)S(1)} %copy-done.6), custom_call_target="tpu_custom_call" | custom-call | tf_op jit(solution)/shard_map/pallas_call | solution.py:46
  345.6 0.4 collective-permute-start.13
  346.0 9.2 %collective-permute-done.6.left_ref = bf16[512,3072]{1,0:T(8,128)(2,1)S(1)} collective-permute-done((bf16[512,3072]{1,0:T(8,128)(2,1)}, bf16[512,3072]{1,0:T(8,128)(2,1)S(1)}, u32[]{:S(2)}, u32[]{:S(2)}) %collective-permute-start.6) | collective-permute-done | bytes 3145760 | tf_op jit(solution)/shard_map/ppermute | solution.py:114
  355.2 0.4 collective-permute-done.7.left_ref
  355.7 4.6 %copy-done.4 = bf16[2048,3072]{1,0:T(8,128)(2,1)S(1)} copy-done((bf16[2048,3072]{1,0:T(8,128)(2,1)S(1)}, bf16[2048,3072]{1,0:T(8,128)(2,1)}, u32[]{:S(2)}) %copy-start.4) | copy-done | bytes 12582936
  360.2 8.2 %shard_map.205 = bf16[384,2048]{1,0:T(8,128)(2,1)} custom-call(s32[1]{0:T(128)} %constant.89.clone.1.place_ref, bf16[512,3072]{1,0:T(8,128)(2,1)} %collective-permute-done.7.left_ref, bf16[2048,3072]{1,0:T(8,128)(2,1)S(1)} %copy-done.4), custom_call_target="tpu_custom_call" | custom-call | tf_op jit(solution)/shard_map/pallas_call | solution.py:46
  368.4 1.7 collective-permute-start.14
  377.7 4.6 %copy-done.5 = bf16[2048,3072]{1,0:T(8,128)(2,1)S(1)} copy-done((bf16[2048,3072]{1,0:T(8,128)(2,1)S(1)}, bf16[2048,3072]{1,0:T(8,128)(2,1)}, u32[]{:S(2)}) %copy-start.5) | copy-done | bytes 12582936
  382.2 5.9 %shard_map.206 = bf16[128,2048]{1,0:T(8,128)(2,1)S(1)} custom-call(s32[1]{0:T(128)} %constant.89.clone.1.place_ref, bf16[512,3072]{1,0:T(8,128)(2,1)} %collective-permute-done.7.left_ref, bf16[2048,3072]{1,0:T(8,128)(2,1)S(1)} %copy-done.5), custom_call_target="tpu_custom_call" | custom-call | tf_op jit(solution)/shard_map/pallas_call | solution.py:46
  388.2 4.6 %copy-done.7 = bf16[2048,3072]{1,0:T(8,128)(2,1)S(1)} copy-done((bf16[2048,3072]{1,0:T(8,128)(2,1)S(1)}, bf16[2048,3072]{1,0:T(8,128)(2,1)}, u32[]{:S(2)}) %copy-start.7) | copy-done | bytes 12582936
  392.8 6.5 %shard_map.207 = bf16[384,2048]{1,0:T(8,128)(2,1)} custom-call(s32[1]{0:T(128)} %constant.89.clone.1.place_ref, bf16[512,3072]{1,0:T(8,128)(2,1)S(1)} %collective-permute-done.6.left_ref, bf16[2048,3072]{1,0:T(8,128)(2,1)S(1)} %copy-done.7), custom_call_target="tpu_custom_call" | custom-call | tf_op jit(solution)/shard_map/pallas_call | solution.py:46
  399.3 0.3 collective-permute-start.11
  399.6 4.8 %shard_map.208 = bf16[128,2048]{1,0:T(8,128)(2,1)S(1)} custom-call(s32[1]{0:T(128)} %constant.89.clone.1.place_ref, bf16[512,3072]{1,0:T(8,128)(2,1)S(1)} %collective-permute-done.6.left_ref, bf16[2048,3072]{1,0:T(8,128)(2,1)S(1)} %copy-done.7), custom_call_target="tpu_custom_call" | custom-call | tf_op jit(solution)/shard_map/pallas_call | solution.py:46
  404.4 1.7 collective-permute-start.10
  406.1 10.8 %shard_map.209 = f32[8,1,512,2048]{3,2,1,0:T(8,128)} custom-call(s32[1]{0:T(128)} %get-tuple-element.163.place_ref, bf16[512,3072]{1,0:T(8,128)(2,1)} %collective-permute-done.7.left_ref, bf16[2048,3072]{1,0:T(8,128)(2,1)S(1)} %bitcast.32, f32[8,1,512,2048]{3,2,1,0:T(8,128)} %shard_map.204.refs_0_), custom_call_target="tpu_custom_call", output_to_operand_aliasing={{}: (3, {})} | custom-call | tf_op jit(solution)/shard_map/pallas_call | solution.py:46
  416.9 9.0 %shard_map.210 = f32[8,1,512,2048]{3,2,1,0:T(8,128)} custom-call(s32[1]{0:T(128)} %get-tuple-element.166.place_ref, bf16[512,3072]{1,0:T(8,128)(2,1)S(1)} %collective-permute-done.6.left_ref, bf16[2048,3072]{1,0:T(8,128)(2,1)S(1)} %bitcast.32, f32[8,1,512,2048]{3,2,1,0:T(8,128)} %shard_map.203.refs_0_), custom_call_target="tpu_custom_call", output_to_operand_aliasing={{}: (3, {})} | custom-call | tf_op jit(solution)/shard_map/pallas_call | solution.py:46
  425.8 0.4 collective-permute-start.15
  426.2 4.1 convert_dynamic-update-slice_fusion.1
  430.3 4.1 convert_dynamic-update-slice_fusion
  434.5 3.4 convert_dynamic-update-slice_fusion.3
  437.9 2.1 convert_dynamic-update-slice_fusion.2
  440.0 3.1 collective-permute-done.15
  443.1 1.1 convert_dynamic-update-slice_fusion.5
  444.2 1.1 convert_dynamic-update-slice_fusion.4
  (33 shorter events, 0.1 us)
Async XLA Ops:
  7.2 152.7 %all-gather.4.cloned.1.call-start = ((), (), s32[]{:S(2)}) async-start(), calls=%async_computation | async-start | bytes 15728640 | tf_op jit(solution)/shard_map/all_gather | solution.py:99
  7.9 145.3 %copy-start.10 = (s32[8]{0:T(128)S(1)}, s32[8]{0:T(128)}, u32[]{:S(2)}) copy-start(s32[8]{0:T(128)} %constant.104.clone) | copy-start | bytes 100
  7.9 151.3 %copy-start.9 = (s32[8]{0:T(128)S(1)}, s32[8]{0:T(128)}, u32[]{:S(2)}) copy-start(s32[8]{0:T(128)} %constant.105.clone) | copy-start | bytes 100
  7.9 152.0 %copy-start.8 = (bf16[512,3072]{1,0:T(8,128)(2,1)S(1)}, bf16[512,3072]{1,0:T(8,128)(2,1)}, u32[]{:S(2)}) copy-start(bf16[512,3072]{1,0:T(8,128)(2,1)} %left_ref) | copy-start | bytes 9437188
  7.9 280.3 %all-gather.6.cloned.1.call-start = ((), (), s32[]{:S(2)}) async-start(), calls=%async_computation.1 | async-start | bytes 15728640 | tf_op jit(solution)/shard_map/all_gather | solution.py:99
  8.0 72.3 %collective-permute-start.1 = (bf16[512,3072]{1,0:T(8,128)(2,1)}, bf16[512,3072]{1,0:T(8,128)(2,1)}, u32[]{:S(2)}, u32[]{:S(2)}) collective-permute-start(bf16[512,3072]{1,0:T(8,128)(2,1)} %left_ref), channel_id=1, source_target_pairs={{0,8},{8,16},{16,24},{24,28},{28,20},{20,12},{12,4},{4,0},{1,9},{9... | collective-permute-start | bytes 9437192 | tf_op jit(solution)/shard_map/ppermute | solution.py:114
  11.1 71.3 %collective-permute-start.2 = (bf16[512,3072]{1,0:T(8,128)(2,1)}, bf16[512,3072]{1,0:T(8,128)(2,1)}, u32[]{:S(2)}, u32[]{:S(2)}) collective-permute-start(bf16[512,3072]{1,0:T(8,128)(2,1)} %left_ref), channel_id=1, source_target_pairs={{8,0},{16,8},{24,16},{28,24},{20,28},{12,20},{4,12},{0,4},{9,1},{1... | collective-permute-start | bytes 9437192 | tf_op jit(solution)/shard_map/ppermute | solution.py:114
  16.7 131.7 %collective-permute-start = (bf16[512,3072]{1,0:T(8,128)(2,1)}, bf16[512,3072]{1,0:T(8,128)(2,1)}, u32[]{:S(2)}, u32[]{:S(2)}) collective-permute-start(bf16[512,3072]{1,0:T(8,128)(2,1)} %subtract_convert_fusion.left_ref), channel_id=1, source_target_pairs={{8,0},{16,8},{24,16},{28,24},{20,28},{12,20},{4,12},{0,4},{9,1},{1... | collective-permute-start | bytes 9437192 | tf_op jit(solution)/shard_map/ppermute | solution.py:114
  18.6 129.7 %collective-permute-start.3 = (bf16[512,3072]{1,0:T(8,128)(2,1)}, bf16[512,3072]{1,0:T(8,128)(2,1)}, u32[]{:S(2)}, u32[]{:S(2)}) collective-permute-start(bf16[512,3072]{1,0:T(8,128)(2,1)} %subtract_convert_fusion.left_ref), channel_id=1, source_target_pairs={{0,8},{8,16},{16,24},{24,28},{28,20},{20,12},{12,4},{4,0},{1,9},{9... | collective-permute-start | bytes 9437192 | tf_op jit(solution)/shard_map/ppermute | solution.py:114
  148.4 182.7 %all-gather.8.cloned.1.call-start = ((), (), s32[]{:S(2)}) async-start(), calls=%async_computation.2 | async-start | bytes 15728640 | tf_op jit(solution)/shard_map/all_gather | solution.py:99
  149.1 79.2 %collective-permute-start.4 = (bf16[512,3072]{1,0:T(8,128)(2,1)}, bf16[512,3072]{1,0:T(8,128)(2,1)}, u32[]{:S(2)}, u32[]{:S(2)}) collective-permute-start(bf16[512,3072]{1,0:T(8,128)(2,1)} %collective-permute-done.left_ref), channel_id=1, source_target_pairs={{8,0},{16,8},{24,16},{28,24},{20,28},{12,20},{4,12},{0,4},{9,1},{1... | collective-permute-start | bytes 9437192 | tf_op jit(solution)/shard_map/ppermute | solution.py:114
  149.5 78.8 %collective-permute-start.5 = (bf16[512,3072]{1,0:T(8,128)(2,1)}, bf16[512,3072]{1,0:T(8,128)(2,1)}, u32[]{:S(2)}, u32[]{:S(2)}) collective-permute-start(bf16[512,3072]{1,0:T(8,128)(2,1)} %collective-permute-done.1.left_ref), channel_id=1, source_target_pairs={{0,8},{8,16},{16,24},{24,28},{28,20},{20,12},{12,4},{4,0},{1,9},{9... | collective-permute-start | bytes 9437192 | tf_op jit(solution)/shard_map/ppermute | solution.py:114
  151.2 136.7 %collective-permute-start.8 = (bf16[512,3072]{1,0:T(8,128)(2,1)}, bf16[512,3072]{1,0:T(8,128)(2,1)}, u32[]{:S(2)}, u32[]{:S(2)}) collective-permute-start(bf16[512,3072]{1,0:T(8,128)(2,1)} %collective-permute-done.2.left_ref), channel_id=1, source_target_pairs={{8,0},{16,8},{24,16},{28,24},{20,28},{12,20},{4,12},{0,4},{9,1},{1... | collective-permute-start | bytes 9437192 | tf_op jit(solution)/shard_map/ppermute | solution.py:114
  151.5 136.7 %collective-permute-start.9 = (bf16[512,3072]{1,0:T(8,128)(2,1)}, bf16[512,3072]{1,0:T(8,128)(2,1)}, u32[]{:S(2)}, u32[]{:S(2)}) collective-permute-start(bf16[512,3072]{1,0:T(8,128)(2,1)} %collective-permute-done.3.left_ref), channel_id=1, source_target_pairs={{0,8},{8,16},{16,24},{24,28},{28,20},{20,12},{12,4},{4,0},{1,9},{9... | collective-permute-start | bytes 9437192 | tf_op jit(solution)/shard_map/ppermute | solution.py:114
  159.9 6.5 %copy-start = (bf16[2048,3072]{1,0:T(8,128)(2,1)S(1)}, bf16[2048,3072]{1,0:T(8,128)(2,1)}, u32[]{:S(2)}) copy-start(bf16[2048,3072]{1,0:T(8,128)(2,1)} %all-gather.4.cloned.1.call-done.right_ref) | copy-start | bytes 37748740
  166.5 8.3 %copy-start.1 = (bf16[2048,3072]{1,0:T(8,128)(2,1)S(1)}, bf16[2048,3072]{1,0:T(8,128)(2,1)}, u32[]{:S(2)}) copy-start(bf16[2048,3072]{1,0:T(8,128)(2,1)} %all-gather.4.cloned.1.call-done.right_ref) | copy-start | bytes 37748740
  228.3 126.9 %collective-permute-start.6 = (bf16[512,3072]{1,0:T(8,128)(2,1)}, bf16[512,3072]{1,0:T(8,128)(2,1)S(1)}, u32[]{:S(2)}, u32[]{:S(2)}) collective-permute-start(bf16[512,3072]{1,0:T(8,128)(2,1)} %collective-permute-done.4.left_ref), channel_id=1, source_target_pairs={{8,0},{16,8},{24,16},{28,24},{20,28},{12,20},{4,12},{0,4},{9,1},{1... | collective-permute-start | bytes 9437192 | tf_op jit(solution)/shard_map/ppermute | solution.py:114
  229.2 126.5 %collective-permute-start.7 = (bf16[512,3072]{1,0:T(8,128)(2,1)}, bf16[512,3072]{1,0:T(8,128)(2,1)}, u32[]{:S(2)}, u32[]{:S(2)}) collective-permute-start(bf16[512,3072]{1,0:T(8,128)(2,1)} %collective-permute-done.5.left_ref), channel_id=1, source_target_pairs={{0,8},{8,16},{16,24},{24,28},{28,20},{20,12},{12,4},{4,0},{1,9},{9... | collective-permute-start | bytes 9437192 | tf_op jit(solution)/shard_map/ppermute | solution.py:114
  288.2 4.6 %copy-start.3 = (bf16[2048,3072]{1,0:T(8,128)(2,1)S(1)}, bf16[2048,3072]{1,0:T(8,128)(2,1)}, u32[]{:S(2)}) copy-start(bf16[2048,3072]{1,0:T(8,128)(2,1)} %all-gather.6.cloned.1.call-done.right_ref) | copy-start | bytes 37748740
  302.9 122.9 %collective-permute-start.12 = (bf16[512,2048]{1,0:T(8,128)(2,1)}, bf16[512,2048]{1,0:T(8,128)(2,1)}, u32[]{:S(2)}, u32[]{:S(2)}) collective-permute-start(bf16[512,2048]{1,0:T(8,128)(2,1)} %shard_map.202), channel_id=1, source_target_pairs={{0,8},{8,16},{16,24},{24,28},{28,20},{20,12},{12,4},{4,0},{1,9},{9... | collective-permute-start | bytes 6291464 | tf_op jit(solution)/shard_map/ppermute | solution.py:120
  304.6 4.7 %copy-start.2 = (bf16[2048,3072]{1,0:T(8,128)(2,1)S(1)}, bf16[2048,3072]{1,0:T(8,128)(2,1)}, u32[]{:S(2)}) copy-start(bf16[2048,3072]{1,0:T(8,128)(2,1)} %all-gather.4.cloned.1.call-done.right_ref) | copy-start | bytes 37748740
  331.0 4.6 %copy-start.6 = (bf16[2048,3072]{1,0:T(8,128)(2,1)S(1)}, bf16[2048,3072]{1,0:T(8,128)(2,1)}, u32[]{:S(2)}) copy-start(bf16[2048,3072]{1,0:T(8,128)(2,1)} %all-gather.8.cloned.1.call-done.right_ref) | copy-start | bytes 37748740
  345.6 84.7 %collective-permute-start.13 = (bf16[512,2048]{1,0:T(8,128)(2,1)}, bf16[512,2048]{1,0:T(8,128)(2,1)}, u32[]{:S(2)}, u32[]{:S(2)}) collective-permute-start(bf16[512,2048]{1,0:T(8,128)(2,1)} %shard_map.211), channel_id=1, source_target_pairs={{8,0},{16,8},{24,16},{28,24},{20,28},{12,20},{4,12},{0,4},{9,1},{1... | collective-permute-start | bytes 6291464 | tf_op jit(solution)/shard_map/ppermute | solution.py:120
  355.7 4.6 %copy-start.4 = (bf16[2048,3072]{1,0:T(8,128)(2,1)S(1)}, bf16[2048,3072]{1,0:T(8,128)(2,1)}, u32[]{:S(2)}) copy-start(bf16[2048,3072]{1,0:T(8,128)(2,1)} %all-gather.6.cloned.1.call-done.right_ref) | copy-start | bytes 37748740
  368.4 66.1 %collective-permute-start.14 = (bf16[384,2048]{1,0:T(8,128)(2,1)}, bf16[384,2048]{1,0:T(8,128)(2,1)}, u32[]{:S(2)}, u32[]{:S(2)}) collective-permute-start(bf16[384,2048]{1,0:T(8,128)(2,1)} %shard_map.205), channel_id=1, source_target_pairs={{0,8},{8,16},{16,24},{24,28},{28,20},{20,12},{12,4},{4,0},{1,9},{9... | collective-permute-start | bytes 4718600 | tf_op jit(solution)/shard_map/ppermute | solution.py:120
  377.7 4.6 %copy-start.5 = (bf16[2048,3072]{1,0:T(8,128)(2,1)S(1)}, bf16[2048,3072]{1,0:T(8,128)(2,1)}, u32[]{:S(2)}) copy-start(bf16[2048,3072]{1,0:T(8,128)(2,1)} %all-gather.6.cloned.1.call-done.right_ref) | copy-start | bytes 37748740
  388.2 4.6 %copy-start.7 = (bf16[2048,3072]{1,0:T(8,128)(2,1)S(1)}, bf16[2048,3072]{1,0:T(8,128)(2,1)}, u32[]{:S(2)}) copy-start(bf16[2048,3072]{1,0:T(8,128)(2,1)} %all-gather.8.cloned.1.call-done.right_ref) | copy-start | bytes 37748740
  392.7 13.3 %slice-start = ((s8[12582912]{0:T(1024)(128)(4,1)}), s8[4194304]{0:T(1024)(128)(4,1)S(1)}, s32[]{:S(2)}) async-start(s8[12582912]{0:T(1024)(128)(4,1)} %bitcast.31), calls=%async_computation.3 | async-start | bytes 8388608
  392.8 13.3 %slice-start.1 = ((s8[12582912]{0:T(1024)(128)(4,1)}), s8[4194304]{0:T(1024)(128)(4,1)S(1)}, s32[]{:S(2)}) async-start(s8[12582912]{0:T(1024)(128)(4,1)} %bitcast.31), calls=%async_computation.4 | async-start | bytes 8388608
  399.3 6.8 %slice-start.2 = ((s8[12582912]{0:T(1024)(128)(4,1)}), s8[4194304]{0:T(1024)(128)(4,1)S(1)}, s32[]{:S(2)}) async-start(s8[12582912]{0:T(1024)(128)(4,1)} %bitcast.31), calls=%async_computation.5 | async-start | bytes 8388608
  399.3 38.7 %collective-permute-start.11 = (bf16[384,2048]{1,0:T(8,128)(2,1)}, bf16[384,2048]{1,0:T(8,128)(2,1)S(1)}, u32[]{:S(2)}, u32[]{:S(2)}) collective-permute-start(bf16[384,2048]{1,0:T(8,128)(2,1)} %shard_map.207), channel_id=1, source_target_pairs={{8,0},{16,8},{24,16},{28,24},{20,28},{12,20},{4,12},{0,4},{9,1},{1... | collective-permute-start | bytes 4718600 | tf_op jit(solution)/shard_map/ppermute | solution.py:120
  404.4 39.8 %collective-permute-start.10 = (bf16[128,2048]{1,0:T(8,128)(2,1)S(1)}, bf16[128,2048]{1,0:T(8,128)(2,1)S(1)}, u32[]{:S(2)}, u32[]{:S(2)}) collective-permute-start(bf16[128,2048]{1,0:T(8,128)(2,1)S(1)} %shard_map.208), channel_id=1, source_target_pairs={{8,0},{16,8},{24,16},{28,24},{20,28},{12,20},{4,12},{0,4},{9,1},{1... | collective-permute-start | bytes 1572872 | tf_op jit(solution)/shard_map/ppermute | solution.py:120
  425.8 17.3 %collective-permute-start.15 = (bf16[128,2048]{1,0:T(8,128)(2,1)S(1)}, bf16[128,2048]{1,0:T(8,128)(2,1)S(1)}, u32[]{:S(2)}, u32[]{:S(2)}) collective-permute-start(bf16[128,2048]{1,0:T(8,128)(2,1)S(1)} %shard_map.206), channel_id=1, source_target_pairs={{0,8},{8,16},{16,24},{24,28},{28,20},{20,12},{12,4},{4,0},{1,9},{9... | collective-permute-start | bytes 1572872 | tf_op jit(solution)/shard_map/ppermute | solution.py:120
Sparse Core Ops, SparseCore 0:
  9.6 84.7 all-gather.3
  148.5 82.3 all-gather.5
  232.4 82.0 all-gather.7

commit v7 on v6

--- a/solution.py
+++ b/solution.py
@@ -11,28 +11,33 @@
 QUARTERS = 4
 
 
-def product_kernel(scale, place_ref, left_ref, right_ref, *refs):
-    total = lax.dot_general(
+def product_kernel(scale, count, place_ref, left_ref, right_ref, *refs):
+    results = refs[-count:]
+    total = scale * lax.dot_general(
         left_ref[...],
         right_ref[...],
         (((1,), (1,)), ((), ())),
         preferred_element_type=jnp.float32,
     )
-    result_ref = refs[-1]
-    result_ref[...] = (total * scale).astype(result_ref.dtype).reshape(result_ref.shape)
+    row = 0
+    for result_ref in results:
+        rows = result_ref.shape[-2]
+        part = total[row : row + rows].astype(result_ref.dtype)
+        result_ref[...] = part.reshape(result_ref.shape)
+        row += rows
 
 
-def product(left, right, owner=None, out=None, out_shape=None, first_row=0, rows=None):
-    rows, tokens = rows or left.shape[0], left.shape[1]
+def product(left, right, owner=None, out=None, out_shape=None, first_row=0, result_rows=None):
+    rows, tokens = sum(result_rows or left.shape[:1]), left.shape[1]
     columns = right.shape[0]
     tile = min(TILE, columns)
     if owner is None:
         owner = 0
-        out_spec = pl.BlockSpec((rows, tile), lambda j, at: (0, j))
-        shape = jax.ShapeDtypeStruct((rows, columns), jnp.bfloat16)
+        out_specs = [pl.BlockSpec((part, tile), lambda j, at: (0, j)) for part in result_rows]
+        shapes = [jax.ShapeDtypeStruct((part, columns), jnp.bfloat16) for part in result_rows]
     else:
-        out_spec = pl.BlockSpec((1, 1, rows, tile), lambda j, at: (at[0], 0, 0, j))
-        shape = jax.ShapeDtypeStruct(out_shape, jnp.float32)
+        out_specs = [pl.BlockSpec((1, 1, rows, tile), lambda j, at: (at[0], 0, 0, j))]
+        shapes = [jax.ShapeDtypeStruct(out_shape, jnp.float32)]
     in_specs = [
         pl.BlockSpec((rows, tokens), lambda j, at: (first_row // rows, 0)),
         pl.BlockSpec((tile, tokens), lambda j, at: (j, 0)),
@@ -44,16 +49,16 @@
         in_specs.append(pl.BlockSpec(memory_space=pl.ANY))
         operands.append(out)
     return pl.pallas_call(
-        functools.partial(product_kernel, 1.0 / tokens),
-        out_shape=shape,
+        functools.partial(product_kernel, 1.0 / tokens, len(shapes)),
+        out_shape=shapes,
         grid_spec=pltpu.PrefetchScalarGridSpec(
             num_scalar_prefetch=1,
             grid=(columns // tile,),
             in_specs=in_specs,
-            out_specs=out_spec,
+            out_specs=out_specs,
         ),
         input_output_aliases=aliases,
-        compiler_params=pltpu.CompilerParams(vmem_limit_bytes=32 * 1024 * 1024),
+        compiler_params=pltpu.CompilerParams(vmem_limit_bytes=48 * 1024 * 1024),
         cost_estimate=pl.CostEstimate(flops=0, bytes_accessed=0, transcendentals=0),
     )(*operands)
 
@@ -88,7 +93,7 @@
         return done[0]
 
     def put(which, owner, block):
-        outs[which] = product(tie(block), right_own, owner, outs[which], out_shape)
+        (outs[which],) = product(tie(block), right_own, owner, outs[which], out_shape)
 
     def put_arrived(which, owner, block, first_row):
         outs[which] = lax.dynamic_update_slice(
@@ -113,12 +118,16 @@
             block = block if step == 1 else tie(block)
             at[chain].append(lax.ppermute(block, "wide", pairs[chain[1]]))
 
-    def send(chain, step, first_row, rows):
+    def send(chain, step, result_rows, row=0):
         which, way = chain
-        result = product(tie(at[chain][step]), right_next[way], first_row=first_row, rows=rows)
-        now.append(result)
-        moved = lax.ppermute(result, "wide", pairs[way])
-        results.append((which, owner_of(way, step + 1), moved, first_row))
+        parts = product(
+            tie(at[chain][step]), right_next[way], first_row=row, result_rows=result_rows
+        )
+        now.extend(parts)
+        for part in parts:
+            moved = lax.ppermute(part, "wide", pairs[way])
+            results.append((which, owner_of(way, step + 1), moved, row))
+            row += part.shape[0]
 
     def is_last(chain, step):
         return step == raw[chain] < reach[chain]
@@ -141,13 +150,17 @@
                     right_next[way] = gather(moved[1 - way])
             for chain in chains:
                 start(chain, step + 1)
-            cut = owned_rows - owned_rows // QUARTERS if step == far - 1 else owned_rows
             late = [chain for chain in here if is_last(chain, step) and step < far - 1 and chain[1]]
             for chain in here:
                 if is_last(chain, step) and chain not in late:
-                    send(chain, step, 0, cut)
-                    if cut < owned_rows:
-                        send(chain, step, cut, owned_rows - cut)
+                    last = owned_rows // QUARTERS if step == far - 1 else 0
+                    if not last:
+                        send(chain, step, [owned_rows])
+                    elif chain[1] == 0:
+                        send(chain, step, [owned_rows - last, last])
+                    else:
+                        send(chain, step, [owned_rows - last])
+                        send(chain, step, [last], owned_rows - last)
             if step == 1 and chains == far_chains:
                 continue
             if step == 1:
@@ -157,7 +170,7 @@
                 if step <= raw[chain]:
                     put(chain[0], owner_of(chain[1], step), at[chain][step])
             for chain in late:
-                send(chain, step, 0, owned_rows)
+                send(chain, step, [owned_rows])
     now[:] = []
     for result in sorted(results, key=lambda result: result[3]):
         put_arrived(*result)

time: 453 us -> 454 us (level)
  local copies, waits for them, and re-layouts: 35.5 us -> 2.08 us
  Pallas kernels: 171 us -> 196 us
  waiting for transfers between devices: 179 us -> 188 us
    unnamed x28 -> x10, local copies, waits for them, and re-layouts: 34.2 us -> 0.81 us
    pallas_call x18 -> x17, Pallas kernels: 171 us -> 196 us  [product(): pl.pallas_call(functools.partial(product_kernel, 1.0 / tokens, len(shapes...]
    ppermute x6, waiting for transfers between devices: 3.11 us -> 10.3 us  [send(): moved = lax.ppermute(part, 'wide', pairs[way])]
  transfers between devices with their start and end apart: 19 -> 19, of which waited for: 8 -> 9; matrix products, arithmetic and copies ran while one was open for 5% -> 5% of each run, Pallas kernels for 38% -> 43%
where the time goes in v7:
time: 454 us; the launch traced here: 452 us
  Pallas kernels  196 us (43%)
  waiting for transfers between devices  188 us (41%)
  between operations  26.7 us (6%)
  other arithmetic  21.5 us (5%)
  starting transfers between devices  17.9 us (4%)
    pallas_call x17, Pallas kernels, product(): pl.pallas_call(functools.partial(product_kernel, 1.0 / tokens, len(shapes...  196 us
    ppermute x10, waiting for transfers between devices, start(): at[chain].append(lax.ppermute(block, 'wide', pairs[chain[1]]))  176 us
    dynamic_update_slice x6, other arithmetic, put_arrived(): lax.dynamic_update_slice(outs[which], tie(block).astype(jnp.float32)[None...  15.9 us
    ppermute x10, starting transfers between devices, start(): at[chain].append(lax.ppermute(block, 'wide', pairs[chain[1]]))  11.3 us
    ppermute x6, waiting for transfers between devices, send(): moved = lax.ppermute(part, 'wide', pairs[way])  10.3 us
  transfers between devices with their start and end apart: 19, of which 9 were waited for; matrix products, arithmetic and copies ran while one was open for 5% of the time, Pallas kernels for 43%

profile of v7, /device:TPU:0, one launch (start us, length us, event | category | flops | bytes accessed | tf_op | source)
XLA Modules:
  0.0 451.8 jit_solution(18434499345255139476)
XLA Ops:
  7.2 0.0 all-gather.4.cloned.1.call-start
  7.2 0.7 all-gather.4.cloned.1.call-update
  7.9 0.0 copy-start.4
  7.9 0.0 copy-start.3
  7.9 0.0 all-gather.6.cloned.1.call-start
  8.0 3.1 collective-permute-start.1
  11.1 0.0 collective-permute-start.2
  11.1 5.6 %subtract_convert_fusion.left_ref = bf16[512,3072]{1,0:T(8,128)(2,1)} fusion(bf16[512,3072]{1,0:T(8,128)(2,1)} %left_ref, bf16[512,3072]{1,0:T(8,128)(2,1)} %param.20), kind=kLoop, calls=%fused_computation | loop fusion | flops 6291456 | bytes 9437184 | tf_op jit(solution)/shard_map/convert_element_type | solution.py:107
  16.7 2.0 collective-permute-start
  18.6 0.1 collective-permute-start.3
  18.7 61.5 %collective-permute-done.1.left_ref = bf16[512,3072]{1,0:T(8,128)(2,1)} collective-permute-done((bf16[512,3072]{1,0:T(8,128)(2,1)}, bf16[512,3072]{1,0:T(8,128)(2,1)}, u32[]{:S(2)}, u32[]{:S(2)}) %collective-permute-start.1) | collective-permute-done | bytes 3145760 | tf_op jit(solution)/shard_map/ppermute | solution.py:119
  80.2 2.2 collective-permute-done.2.left_ref
  82.4 65.9 %collective-permute-done.left_ref = bf16[512,3072]{1,0:T(8,128)(2,1)} collective-permute-done((bf16[512,3072]{1,0:T(8,128)(2,1)}, bf16[512,3072]{1,0:T(8,128)(2,1)}, u32[]{:S(2)}, u32[]{:S(2)}) %collective-permute-start) | collective-permute-done | bytes 3145760 | tf_op jit(solution)/shard_map/ppermute | solution.py:119
  148.3 0.0 collective-permute-done.3.left_ref
  148.3 0.0 all-gather.6.cloned.1.call-update
  148.4 0.0 all-gather.8.cloned.1.call-start
  148.4 0.7 all-gather.8.cloned.1.call-update
  149.1 0.4 collective-permute-start.4
  149.5 1.7 collective-permute-start.5
  151.2 0.3 collective-permute-start.8
  151.5 1.7 collective-permute-start.9
  153.2 0.6 dynamic_slice.51
  159.2 0.7 fusion
  159.9 11.3 %shard_map.194.refs_0_ = f32[8,1,512,2048]{3,2,1,0:T(8,128)} custom-call(s32[1]{0:T(128)} %bitcast.2.place_ref, bf16[512,3072]{1,0:T(8,128)(2,1)S(1)} %copy-done, bf16[2048,3072]{1,0:T(8,128)(2,1)} %all-gather.4.cloned.1.call-done.right_ref), custom_call_target="tpu_custom_call" | custom-call | tf_op jit(solution)/shard_map/pallas_call | solution.py:51
  171.2 11.7 %shard_map.195.refs_0_ = f32[8,1,512,2048]{3,2,1,0:T(8,128)} custom-call(s32[1]{0:T(128)} %bitcast.2.place_ref, bf16[512,3072]{1,0:T(8,128)(2,1)} %subtract_convert_fusion.left_ref, bf16[2048,3072]{1,0:T(8,128)(2,1)} %all-gather.4.cloned.1.call-done.right_ref), custom_call_target="tpu_custom_call" | custom-call | tf_op jit(solution)/shard_map/pallas_call | solution.py:51
  182.9 12.3 %shard_map.196.refs_0_ = f32[8,1,512,2048]{3,2,1,0:T(8,128)} custom-call(s32[1]{0:T(128)} %get-tuple-element.162.place_ref, bf16[512,3072]{1,0:T(8,128)(2,1)} %collective-permute-done.1.left_ref, bf16[2048,3072]{1,0:T(8,128)(2,1)} %all-gather.4.cloned.1.call-done.right_ref, f32[8,1,512,2048]{3,2,1,0:T(8,128)} %shard_map.194.refs_0_), custom_call_target="tpu_custom_call", output_to_operand_aliasing={{}: (3, {})} | custom-call | tf_op jit(solution)/shard_map/pallas_call | solution.py:51
  195.3 12.4 %shard_map.197.refs_0_ = f32[8,1,512,2048]{3,2,1,0:T(8,128)} custom-call(s32[1]{0:T(128)} %get-tuple-element.163.place_ref, bf16[512,3072]{1,0:T(8,128)(2,1)} %collective-permute-done.left_ref, bf16[2048,3072]{1,0:T(8,128)(2,1)} %all-gather.4.cloned.1.call-done.right_ref, f32[8,1,512,2048]{3,2,1,0:T(8,128)} %shard_map.195.refs_0_), custom_call_target="tpu_custom_call", output_to_operand_aliasing={{}: (3, {})} | custom-call | tf_op jit(solution)/shard_map/pallas_call | solution.py:51
  207.7 12.3 %shard_map.198.refs_0_ = f32[8,1,512,2048]{3,2,1,0:T(8,128)} custom-call(s32[1]{0:T(128)} %get-tuple-element.162.place_ref, bf16[512,3072]{1,0:T(8,128)(2,1)} %collective-permute-done.3.left_ref, bf16[2048,3072]{1,0:T(8,128)(2,1)} %all-gather.4.cloned.1.call-done.right_ref, f32[8,1,512,2048]{3,2,1,0:T(8,128)} %shard_map.197.refs_0_), custom_call_target="tpu_custom_call", output_to_operand_aliasing={{}: (3, {})} | custom-call | tf_op jit(solution)/shard_map/pallas_call | solution.py:51
  220.0 12.4 %shard_map.199.refs_0_ = f32[8,1,512,2048]{3,2,1,0:T(8,128)} custom-call(s32[1]{0:T(128)} %get-tuple-element.163.place_ref, bf16[512,3072]{1,0:T(8,128)(2,1)} %collective-permute-done.2.left_ref, bf16[2048,3072]{1,0:T(8,128)(2,1)} %all-gather.4.cloned.1.call-done.right_ref, f32[8,1,512,2048]{3,2,1,0:T(8,128)} %shard_map.196.refs_0_), custom_call_target="tpu_custom_call", output_to_operand_aliasing={{}: (3, {})} | custom-call | tf_op jit(solution)/shard_map/pallas_call | solution.py:51
  232.4 0.0 collective-permute-done.4.left_ref
  232.4 0.0 collective-permute-done.5.left_ref
  232.4 0.6 collective-permute-start.6
  233.0 1.5 collective-permute-start.7
  234.5 13.0 %shard_map.200.refs_0_ = f32[8,1,512,2048]{3,2,1,0:T(8,128)} custom-call(s32[1]{0:T(128)} %get-tuple-element.159.place_ref, bf16[512,3072]{1,0:T(8,128)(2,1)} %collective-permute-done.5.left_ref, bf16[2048,3072]{1,0:T(8,128)(2,1)} %all-gather.4.cloned.1.call-done.right_ref, f32[8,1,512,2048]{3,2,1,0:T(8,128)} %shard_map.199.refs_0_), custom_call_target="tpu_custom_call", output_to_operand_aliasing={{}: (3, {})} | custom-call | tf_op jit(solution)/shard_map/pallas_call | solution.py:51
  247.5 12.3 %shard_map.201.refs_0_ = f32[8,1,512,2048]{3,2,1,0:T(8,128)} custom-call(s32[1]{0:T(128)} %get-tuple-element.160.place_ref, bf16[512,3072]{1,0:T(8,128)(2,1)} %collective-permute-done.4.left_ref, bf16[2048,3072]{1,0:T(8,128)(2,1)} %all-gather.4.cloned.1.call-done.right_ref, f32[8,1,512,2048]{3,2,1,0:T(8,128)} %shard_map.198.refs_0_), custom_call_target="tpu_custom_call", output_to_operand_aliasing={{}: (3, {})} | custom-call | tf_op jit(solution)/shard_map/pallas_call | solution.py:51
  259.9 28.1 %collective-permute-done.8.left_ref = bf16[512,3072]{1,0:T(8,128)(2,1)} collective-permute-done((bf16[512,3072]{1,0:T(8,128)(2,1)}, bf16[512,3072]{1,0:T(8,128)(2,1)}, u32[]{:S(2)}, u32[]{:S(2)}) %collective-permute-start.8) | collective-permute-done | bytes 3145760 | tf_op jit(solution)/shard_map/ppermute | solution.py:119
  287.9 0.3 collective-permute-done.9.left_ref
  288.2 11.4 %shard_map.202 = bf16[512,2048]{1,0:T(8,128)(2,1)} custom-call(s32[1]{0:T(128)} %constant.89.clone.1.place_ref, bf16[512,3072]{1,0:T(8,128)(2,1)} %collective-permute-done.9.left_ref, bf16[2048,3072]{1,0:T(8,128)(2,1)} %all-gather.6.cloned.1.call-done.right_ref), custom_call_target="tpu_custom_call" | custom-call | tf_op jit(solution)/shard_map/pallas_call | solution.py:51
  299.6 1.7 collective-permute-start.12
  301.3 12.4 %shard_map.203.refs_0_ = f32[8,1,512,2048]{3,2,1,0:T(8,128)} custom-call(s32[1]{0:T(128)} %get-tuple-element.159.place_ref, bf16[512,3072]{1,0:T(8,128)(2,1)} %collective-permute-done.9.left_ref, bf16[2048,3072]{1,0:T(8,128)(2,1)} %all-gather.4.cloned.1.call-done.right_ref, f32[8,1,512,2048]{3,2,1,0:T(8,128)} %shard_map.201.refs_0_), custom_call_target="tpu_custom_call", output_to_operand_aliasing={{}: (3, {})} | custom-call | tf_op jit(solution)/shard_map/pallas_call | solution.py:51
  313.7 12.3 %shard_map.204.refs_0_ = f32[8,1,512,2048]{3,2,1,0:T(8,128)} custom-call(s32[1]{0:T(128)} %get-tuple-element.160.place_ref, bf16[512,3072]{1,0:T(8,128)(2,1)} %collective-permute-done.8.left_ref, bf16[2048,3072]{1,0:T(8,128)(2,1)} %all-gather.4.cloned.1.call-done.right_ref, f32[8,1,512,2048]{3,2,1,0:T(8,128)} %shard_map.200.refs_0_), custom_call_target="tpu_custom_call", output_to_operand_aliasing={{}: (3, {})} | custom-call | tf_op jit(solution)/shard_map/pallas_call | solution.py:51
  326.0 11.3 %shard_map.210 = bf16[512,2048]{1,0:T(8,128)(2,1)} custom-call(s32[1]{0:T(128)} %constant.89.clone.1.place_ref, bf16[512,3072]{1,0:T(8,128)(2,1)} %collective-permute-done.8.left_ref, bf16[2048,3072]{1,0:T(8,128)(2,1)} %all-gather.8.cloned.1.call-done.right_ref), custom_call_target="tpu_custom_call" | custom-call | tf_op jit(solution)/shard_map/pallas_call | solution.py:51
  337.3 0.4 collective-permute-start.13
  337.7 17.5 %collective-permute-done.6.left_ref = bf16[512,3072]{1,0:T(8,128)(2,1)S(1)} collective-permute-done((bf16[512,3072]{1,0:T(8,128)(2,1)}, bf16[512,3072]{1,0:T(8,128)(2,1)S(1)}, u32[]{:S(2)}, u32[]{:S(2)}) %collective-permute-start.6) | collective-permute-done | bytes 3145760 | tf_op jit(solution)/shard_map/ppermute | solution.py:119
  355.2 0.4 collective-permute-done.7.left_ref
  355.7 11.2 %shard_map.205 = (bf16[384,2048]{1,0:T(8,128)(2,1)}, bf16[128,2048]{1,0:T(8,128)(2,1)S(1)}) custom-call(s32[1]{0:T(128)} %constant.89.clone.1.place_ref, bf16[512,3072]{1,0:T(8,128)(2,1)} %collective-permute-done.7.left_ref, bf16[2048,3072]{1,0:T(8,128)(2,1)} %all-gather.6.cloned.1.call-done.right_ref), custom_call_target="tpu_custom_call" | custom-call | tf_op jit(solution)/shard_map/pallas_call | solution.py:51
  366.8 0.8 copy-done.1
  367.6 1.7 collective-permute-start.14
  376.8 8.2 %shard_map.206 = bf16[384,2048]{1,0:T(8,128)(2,1)S(1)} custom-call(s32[1]{0:T(128)} %constant.89.clone.1.place_ref, bf16[512,3072]{1,0:T(8,128)(2,1)S(1)} %collective-permute-done.6.left_ref, bf16[2048,3072]{1,0:T(8,128)(2,1)} %all-gather.8.cloned.1.call-done.right_ref), custom_call_target="tpu_custom_call" | custom-call | tf_op jit(solution)/shard_map/pallas_call | solution.py:51
  385.1 0.4 collective-permute-start.11
  385.4 7.5 %shard_map.207 = bf16[128,2048]{1,0:T(8,128)(2,1)S(1)} custom-call(s32[1]{0:T(128)} %constant.89.clone.1.place_ref, bf16[512,3072]{1,0:T(8,128)(2,1)S(1)} %collective-permute-done.6.left_ref, bf16[2048,3072]{1,0:T(8,128)(2,1)} %all-gather.8.cloned.1.call-done.right_ref), custom_call_target="tpu_custom_call" | custom-call | tf_op jit(solution)/shard_map/pallas_call | solution.py:51
  393.0 1.9 collective-permute-start.10
  394.9 12.3 %shard_map.208 = f32[8,1,512,2048]{3,2,1,0:T(8,128)} custom-call(s32[1]{0:T(128)} %get-tuple-element.161.place_ref, bf16[512,3072]{1,0:T(8,128)(2,1)} %collective-permute-done.7.left_ref, bf16[2048,3072]{1,0:T(8,128)(2,1)} %all-gather.4.cloned.1.call-done.right_ref, f32[8,1,512,2048]{3,2,1,0:T(8,128)} %shard_map.204.refs_0_), custom_call_target="tpu_custom_call", output_to_operand_aliasing={{}: (3, {})} | custom-call | tf_op jit(solution)/shard_map/pallas_call | solution.py:51
  407.3 11.4 %shard_map.209 = f32[8,1,512,2048]{3,2,1,0:T(8,128)} custom-call(s32[1]{0:T(128)} %get-tuple-element.164.place_ref, bf16[512,3072]{1,0:T(8,128)(2,1)S(1)} %collective-permute-done.6.left_ref, bf16[2048,3072]{1,0:T(8,128)(2,1)} %all-gather.4.cloned.1.call-done.right_ref, f32[8,1,512,2048]{3,2,1,0:T(8,128)} %shard_map.203.refs_0_), custom_call_target="tpu_custom_call", output_to_operand_aliasing={{}: (3, {})} | custom-call | tf_op jit(solution)/shard_map/pallas_call | solution.py:51
  418.7 0.4 collective-permute-start.15
  419.1 4.1 convert_dynamic-update-slice_fusion.1
  423.2 4.1 convert_dynamic-update-slice_fusion
  427.3 7.0 %collective-permute-done.14 = bf16[384,2048]{1,0:T(8,128)(2,1)} collective-permute-done((bf16[384,2048]{1,0:T(8,128)(2,1)}, bf16[384,2048]{1,0:T(8,128)(2,1)}, u32[]{:S(2)}, u32[]{:S(2)}) %collective-permute-start.14) | collective-permute-done | bytes 1572896 | tf_op jit(solution)/shard_map/ppermute | solution.py:128
  434.3 3.4 convert_dynamic-update-slice_fusion.3
  437.8 0.0 collective-permute-done.11
  437.8 2.1 convert_dynamic-update-slice_fusion.2
  439.8 3.3 collective-permute-done.15
  443.1 1.1 convert_dynamic-update-slice_fusion.5
  444.2 1.1 convert_dynamic-update-slice_fusion.4
  (13 shorter events, 0.0 us)
Async XLA Ops:
  7.2 152.7 %all-gather.4.cloned.1.call-start = ((), (), s32[]{:S(2)}) async-start(), calls=%async_computation | async-start | bytes 15728640 | tf_op jit(solution)/shard_map/all_gather | solution.py:104
  7.9 145.3 %copy-start.4 = (s32[8]{0:T(128)S(1)}, s32[8]{0:T(128)}, u32[]{:S(2)}) copy-start(s32[8]{0:T(128)} %constant.104.clone) | copy-start | bytes 100
  7.9 151.3 %copy-start.3 = (s32[8]{0:T(128)S(1)}, s32[8]{0:T(128)}, u32[]{:S(2)}) copy-start(s32[8]{0:T(128)} %constant.105.clone) | copy-start | bytes 100
  7.9 152.0 %copy-start = (bf16[512,3072]{1,0:T(8,128)(2,1)S(1)}, bf16[512,3072]{1,0:T(8,128)(2,1)}, u32[]{:S(2)}) copy-start(bf16[512,3072]{1,0:T(8,128)(2,1)} %left_ref) | copy-start | bytes 9437188
  7.9 280.3 %all-gather.6.cloned.1.call-start = ((), (), s32[]{:S(2)}) async-start(), calls=%async_computation.1 | async-start | bytes 15728640 | tf_op jit(solution)/shard_map/all_gather | solution.py:104
  8.0 72.3 %collective-permute-start.1 = (bf16[512,3072]{1,0:T(8,128)(2,1)}, bf16[512,3072]{1,0:T(8,128)(2,1)}, u32[]{:S(2)}, u32[]{:S(2)}) collective-permute-start(bf16[512,3072]{1,0:T(8,128)(2,1)} %left_ref), channel_id=1, source_target_pairs={{0,8},{8,16},{16,24},{24,28},{28,20},{20,12},{12,4},{4,0},{1,9},{9... | collective-permute-start | bytes 9437192 | tf_op jit(solution)/shard_map/ppermute | solution.py:119
  11.1 71.3 %collective-permute-start.2 = (bf16[512,3072]{1,0:T(8,128)(2,1)}, bf16[512,3072]{1,0:T(8,128)(2,1)}, u32[]{:S(2)}, u32[]{:S(2)}) collective-permute-start(bf16[512,3072]{1,0:T(8,128)(2,1)} %left_ref), channel_id=1, source_target_pairs={{8,0},{16,8},{24,16},{28,24},{20,28},{12,20},{4,12},{0,4},{9,1},{1... | collective-permute-start | bytes 9437192 | tf_op jit(solution)/shard_map/ppermute | solution.py:119
  16.7 131.7 %collective-permute-start = (bf16[512,3072]{1,0:T(8,128)(2,1)}, bf16[512,3072]{1,0:T(8,128)(2,1)}, u32[]{:S(2)}, u32[]{:S(2)}) collective-permute-start(bf16[512,3072]{1,0:T(8,128)(2,1)} %subtract_convert_fusion.left_ref), channel_id=1, source_target_pairs={{8,0},{16,8},{24,16},{28,24},{20,28},{12,20},{4,12},{0,4},{9,1},{1... | collective-permute-start | bytes 9437192 | tf_op jit(solution)/shard_map/ppermute | solution.py:119
  18.6 129.7 %collective-permute-start.3 = (bf16[512,3072]{1,0:T(8,128)(2,1)}, bf16[512,3072]{1,0:T(8,128)(2,1)}, u32[]{:S(2)}, u32[]{:S(2)}) collective-permute-start(bf16[512,3072]{1,0:T(8,128)(2,1)} %subtract_convert_fusion.left_ref), channel_id=1, source_target_pairs={{0,8},{8,16},{16,24},{24,28},{28,20},{20,12},{12,4},{4,0},{1,9},{9... | collective-permute-start | bytes 9437192 | tf_op jit(solution)/shard_map/ppermute | solution.py:119
  148.4 177.6 %all-gather.8.cloned.1.call-start = ((), (), s32[]{:S(2)}) async-start(), calls=%async_computation.2 | async-start | bytes 15728640 | tf_op jit(solution)/shard_map/all_gather | solution.py:104
  149.1 83.3 %collective-permute-start.4 = (bf16[512,3072]{1,0:T(8,128)(2,1)}, bf16[512,3072]{1,0:T(8,128)(2,1)}, u32[]{:S(2)}, u32[]{:S(2)}) collective-permute-start(bf16[512,3072]{1,0:T(8,128)(2,1)} %collective-permute-done.left_ref), channel_id=1, source_target_pairs={{8,0},{16,8},{24,16},{28,24},{20,28},{12,20},{4,12},{0,4},{9,1},{1... | collective-permute-start | bytes 9437192 | tf_op jit(solution)/shard_map/ppermute | solution.py:119
  149.5 82.9 %collective-permute-start.5 = (bf16[512,3072]{1,0:T(8,128)(2,1)}, bf16[512,3072]{1,0:T(8,128)(2,1)}, u32[]{:S(2)}, u32[]{:S(2)}) collective-permute-start(bf16[512,3072]{1,0:T(8,128)(2,1)} %collective-permute-done.1.left_ref), channel_id=1, source_target_pairs={{0,8},{8,16},{16,24},{24,28},{28,20},{20,12},{12,4},{4,0},{1,9},{9... | collective-permute-start | bytes 9437192 | tf_op jit(solution)/shard_map/ppermute | solution.py:119
  151.2 136.7 %collective-permute-start.8 = (bf16[512,3072]{1,0:T(8,128)(2,1)}, bf16[512,3072]{1,0:T(8,128)(2,1)}, u32[]{:S(2)}, u32[]{:S(2)}) collective-permute-start(bf16[512,3072]{1,0:T(8,128)(2,1)} %collective-permute-done.2.left_ref), channel_id=1, source_target_pairs={{8,0},{16,8},{24,16},{28,24},{20,28},{12,20},{4,12},{0,4},{9,1},{1... | collective-permute-start | bytes 9437192 | tf_op jit(solution)/shard_map/ppermute | solution.py:119
  151.5 136.7 %collective-permute-start.9 = (bf16[512,3072]{1,0:T(8,128)(2,1)}, bf16[512,3072]{1,0:T(8,128)(2,1)}, u32[]{:S(2)}, u32[]{:S(2)}) collective-permute-start(bf16[512,3072]{1,0:T(8,128)(2,1)} %collective-permute-done.3.left_ref), channel_id=1, source_target_pairs={{0,8},{8,16},{16,24},{24,28},{28,20},{20,12},{12,4},{4,0},{1,9},{9... | collective-permute-start | bytes 9437192 | tf_op jit(solution)/shard_map/ppermute | solution.py:119
  232.4 122.8 %collective-permute-start.6 = (bf16[512,3072]{1,0:T(8,128)(2,1)}, bf16[512,3072]{1,0:T(8,128)(2,1)S(1)}, u32[]{:S(2)}, u32[]{:S(2)}) collective-permute-start(bf16[512,3072]{1,0:T(8,128)(2,1)} %collective-permute-done.4.left_ref), channel_id=1, source_target_pairs={{8,0},{16,8},{24,16},{28,24},{20,28},{12,20},{4,12},{0,4},{9,1},{1... | collective-permute-start | bytes 9437192 | tf_op jit(solution)/shard_map/ppermute | solution.py:119
  233.0 122.6 %collective-permute-start.7 = (bf16[512,3072]{1,0:T(8,128)(2,1)}, bf16[512,3072]{1,0:T(8,128)(2,1)}, u32[]{:S(2)}, u32[]{:S(2)}) collective-permute-start(bf16[512,3072]{1,0:T(8,128)(2,1)} %collective-permute-done.5.left_ref), channel_id=1, source_target_pairs={{0,8},{8,16},{16,24},{24,28},{28,20},{20,12},{12,4},{4,0},{1,9},{9... | collective-permute-start | bytes 9437192 | tf_op jit(solution)/shard_map/ppermute | solution.py:119
  299.6 119.1 %collective-permute-start.12 = (bf16[512,2048]{1,0:T(8,128)(2,1)}, bf16[512,2048]{1,0:T(8,128)(2,1)}, u32[]{:S(2)}, u32[]{:S(2)}) collective-permute-start(bf16[512,2048]{1,0:T(8,128)(2,1)} %shard_map.202), channel_id=1, source_target_pairs={{0,8},{8,16},{16,24},{24,28},{28,20},{20,12},{12,4},{4,0},{1,9},{9... | collective-permute-start | bytes 6291464 | tf_op jit(solution)/shard_map/ppermute | solution.py:128
  337.3 85.9 %collective-permute-start.13 = (bf16[512,2048]{1,0:T(8,128)(2,1)}, bf16[512,2048]{1,0:T(8,128)(2,1)}, u32[]{:S(2)}, u32[]{:S(2)}) collective-permute-start(bf16[512,2048]{1,0:T(8,128)(2,1)} %shard_map.210), channel_id=1, source_target_pairs={{8,0},{16,8},{24,16},{28,24},{20,28},{12,20},{4,12},{0,4},{9,1},{1... | collective-permute-start | bytes 6291464 | tf_op jit(solution)/shard_map/ppermute | solution.py:128
  366.8 0.8 copy-start.1
  367.6 66.7 %collective-permute-start.14 = (bf16[384,2048]{1,0:T(8,128)(2,1)}, bf16[384,2048]{1,0:T(8,128)(2,1)}, u32[]{:S(2)}, u32[]{:S(2)}) collective-permute-start(bf16[384,2048]{1,0:T(8,128)(2,1)} %get-tuple-element.129), channel_id=1, source_target_pairs={{0,8},{8,16},{16,24},{24,28},{28,20},{20,12},{12,4},{4,0},{1,9},{9... | collective-permute-start | bytes 4718600 | tf_op jit(solution)/shard_map/ppermute | solution.py:128
  385.1 52.7 %collective-permute-start.11 = (bf16[384,2048]{1,0:T(8,128)(2,1)S(1)}, bf16[384,2048]{1,0:T(8,128)(2,1)S(1)}, u32[]{:S(2)}, u32[]{:S(2)}) collective-permute-start(bf16[384,2048]{1,0:T(8,128)(2,1)S(1)} %shard_map.206), channel_id=1, source_target_pairs={{8,0},{16,8},{24,16},{28,24},{20,28},{12,20},{4,12},{0,4},{9,1},{1... | collective-permute-start | bytes 4718600 | tf_op jit(solution)/shard_map/ppermute | solution.py:128
  393.0 51.2 %collective-permute-start.10 = (bf16[128,2048]{1,0:T(8,128)(2,1)S(1)}, bf16[128,2048]{1,0:T(8,128)(2,1)S(1)}, u32[]{:S(2)}, u32[]{:S(2)}) collective-permute-start(bf16[128,2048]{1,0:T(8,128)(2,1)S(1)} %shard_map.207), channel_id=1, source_target_pairs={{8,0},{16,8},{24,16},{28,24},{20,28},{12,20},{4,12},{0,4},{9,1},{1... | collective-permute-start | bytes 1572872 | tf_op jit(solution)/shard_map/ppermute | solution.py:128
  407.3 11.4 %copy-start.2 = (bf16[128,2048]{1,0:T(8,128)(2,1)S(1)}, bf16[128,2048]{1,0:T(8,128)(2,1)}, u32[]{:S(2)}) copy-start(bf16[128,2048]{1,0:T(8,128)(2,1)} %copy-done.1) | copy-start | bytes 1572868
  418.7 24.4 %collective-permute-start.15 = (bf16[128,2048]{1,0:T(8,128)(2,1)S(1)}, bf16[128,2048]{1,0:T(8,128)(2,1)S(1)}, u32[]{:S(2)}, u32[]{:S(2)}) collective-permute-start(bf16[128,2048]{1,0:T(8,128)(2,1)S(1)} %copy-done.2), channel_id=1, source_target_pairs={{0,8},{8,16},{16,24},{24,28},{28,20},{20,12},{12,4},{4,0},{1,9},{9... | collective-permute-start | bytes 1572872 | tf_op jit(solution)/shard_map/ppermute | solution.py:128
Sparse Core Ops, SparseCore 0:
  9.6 84.7 all-gather.3
  148.5 82.3 all-gather.5
  232.4 82.0 all-gather.7

commit v8 on v7

--- a/solution.py
+++ b/solution.py
@@ -58,8 +58,12 @@
             out_specs=out_specs,
         ),
         input_output_aliases=aliases,
-        compiler_params=pltpu.CompilerParams(vmem_limit_bytes=48 * 1024 * 1024),
-        cost_estimate=pl.CostEstimate(flops=0, bytes_accessed=0, transcendentals=0),
+        compiler_params=pltpu.CompilerParams(vmem_limit_bytes=32 * 1024 * 1024),
+        cost_estimate=pl.CostEstimate(
+            flops=4 * rows * columns * tokens if result_rows is None else 0,
+            bytes_accessed=0,
+            transcendentals=0,
+        ),
     )(*operands)
 
 
@@ -136,13 +140,14 @@
     for chain in ((0, 0), (0, 1), (1, 1), (1, 0)):
         start(chain, 1)
     right_next = [None, None]
-    results = []
+    results, earlier = [], []
     for step in range(1, far + 1):
         for chains in (far_chains, near_chains):
             here = [chain for chain in chains if step <= raw[chain]]
             if not here:
                 continue
             now[:] = [at[chain][step] for chain in (raw if step == 1 else here) if step <= raw[chain]]
+            now += earlier
             if step == 1 and chains == far_chains and near > 0:
                 moved = lax.optimization_barrier((at[0, 0][1], at[0, 1][1]))
                 moved = lax.optimization_barrier((*moved, at[1, 0][1], at[1, 1][1]))
@@ -171,6 +176,7 @@
                     put(chain[0], owner_of(chain[1], step), at[chain][step])
             for chain in late:
                 send(chain, step, [owned_rows])
+                earlier.append(now[-1])
     now[:] = []
     for result in sorted(results, key=lambda result: result[3]):
         put_arrived(*result)

time: 454 us -> 467 us (1.029)
  Pallas kernels: 196 us -> 167 us
  local copies, waits for them, and re-layouts: 2.08 us -> 29 us
  waiting for transfers between devices: 188 us -> 206 us
    pallas_call x17, Pallas kernels: 196 us -> 167 us  [product(): pl.pallas_call(functools.partial(product_kernel, 1.0 / tokens, len(shapes...]
    unnamed x10 -> x26, local copies, waits for them, and re-layouts: 0.81 us -> 27.8 us
    ppermute x6, waiting for transfers between devices: 10.3 us -> 20.7 us  [send(): moved = lax.ppermute(part, 'wide', pairs[way])]
    ppermute x10, waiting for transfers between devices: 176 us -> 183 us  [start(): at[chain].append(lax.ppermute(block, 'wide', pairs[chain[1]]))]
  transfers between devices with their start and end apart: 19 -> 19, of which waited for: 9 -> 11; matrix products, arithmetic and copies ran while one was open for 5% -> 4% of each run, Pallas kernels for 43% -> 36%
where the time goes in v8:
time: 467 us; the launch traced here: 466 us
  waiting for transfers between devices  206 us (44%)
  Pallas kernels  167 us (36%)
  local copies, waits for them, and re-layouts  29 us (6%)
  between operations  26.7 us (6%)
  other arithmetic  20 us (4%)
  starting transfers between devices  17.7 us (4%)
    ppermute x10, waiting for transfers between devices, start(): at[chain].append(lax.ppermute(block, 'wide', pairs[chain[1]]))  183 us
    pallas_call x17, Pallas kernels, product(): pl.pallas_call(functools.partial(product_kernel, 1.0 / tokens, len(shapes...  167 us
    unnamed x26, local copies, waits for them, and re-layouts  27.8 us
    ppermute x6, waiting for transfers between devices, send(): moved = lax.ppermute(part, 'wide', pairs[way])  20.7 us
    dynamic_update_slice x6, other arithmetic, put_arrived(): lax.dynamic_update_slice(outs[which], tie(block).astype(jnp.float32)[None...  14.4 us
    ppermute x10, starting transfers between devices, start(): at[chain].append(lax.ppermute(block, 'wide', pairs[chain[1]]))  11.2 us
  transfers between devices with their start and end apart: 19, of which 11 were waited for; matrix products, arithmetic and copies ran while one was open for 4% of the time, Pallas kernels for 36%

profile of v8, /device:TPU:0, one launch (start us, length us, event | category | flops | bytes accessed | tf_op | source)
XLA Modules:
  0.0 466.0 jit_solution(15604263761862468217)
XLA Ops:
  7.2 0.0 all-gather.4.cloned.1.call-start
  7.2 0.7 all-gather.4.cloned.1.call-update
  7.9 0.0 all-gather.6.cloned.1.call-start
  8.0 3.1 collective-permute-start.1
  11.1 5.7 %subtract_convert_fusion.left_ref = bf16[512,3072]{1,0:T(8,128)(2,1)} fusion(bf16[512,3072]{1,0:T(8,128)(2,1)} %left_ref, bf16[512,3072]{1,0:T(8,128)(2,1)} %param.20), kind=kLoop, calls=%fused_computation | loop fusion | flops 6291456 | bytes 9437184 | tf_op jit(solution)/shard_map/convert_element_type | solution.py:111
  16.7 2.0 collective-permute-start
  18.7 0.1 collective-permute-start.3
  18.7 61.5 %collective-permute-done.1.left_ref = bf16[512,3072]{1,0:T(8,128)(2,1)} collective-permute-done((bf16[512,3072]{1,0:T(8,128)(2,1)}, bf16[512,3072]{1,0:T(8,128)(2,1)}, u32[]{:S(2)}, u32[]{:S(2)}) %collective-permute-start.1) | collective-permute-done | bytes 3145760 | tf_op jit(solution)/shard_map/ppermute | solution.py:123
  80.2 2.2 collective-permute-done.2.left_ref
  82.4 65.9 %collective-permute-done.left_ref = bf16[512,3072]{1,0:T(8,128)(2,1)} collective-permute-done((bf16[512,3072]{1,0:T(8,128)(2,1)}, bf16[512,3072]{1,0:T(8,128)(2,1)}, u32[]{:S(2)}, u32[]{:S(2)}) %collective-permute-start) | collective-permute-done | bytes 3145760 | tf_op jit(solution)/shard_map/ppermute | solution.py:123
  148.3 0.0 all-gather.6.cloned.1.call-update
  148.4 0.0 all-gather.8.cloned.1.call-start
  148.4 0.7 all-gather.8.cloned.1.call-update
  149.1 0.6 dynamic_slice.51
  155.1 0.7 fusion
  163.3 0.3 collective-permute-start.4
  163.7 1.7 collective-permute-start.5
  165.4 0.3 collective-permute-start.8
  165.7 1.7 collective-permute-start.9
  167.4 4.7 %copy-done = bf16[2048,3072]{1,0:T(8,128)(2,1)S(1)} copy-done((bf16[2048,3072]{1,0:T(8,128)(2,1)S(1)}, bf16[2048,3072]{1,0:T(8,128)(2,1)}, u32[]{:S(2)}) %copy-start) | copy-done | bytes 12582936
  172.2 8.3 %shard_map.194.refs_0_ = f32[8,1,512,2048]{3,2,1,0:T(8,128)} custom-call(s32[1]{0:T(128)} %bitcast.2.place_ref, bf16[512,3072]{1,0:T(8,128)(2,1)S(1)} %copy-done.7, bf16[2048,3072]{1,0:T(8,128)(2,1)S(1)} %copy-done), custom_call_target="tpu_custom_call" | custom-call | flops 12884901888 | tf_op jit(solution)/shard_map/pallas_call | solution.py:51
  180.5 10.2 %shard_map.195.refs_0_ = f32[8,1,512,2048]{3,2,1,0:T(8,128)} custom-call(s32[1]{0:T(128)} %bitcast.2.place_ref, bf16[512,3072]{1,0:T(8,128)(2,1)} %subtract_convert_fusion.left_ref, bf16[2048,3072]{1,0:T(8,128)(2,1)S(1)} %copy-done.1), custom_call_target="tpu_custom_call" | custom-call | flops 12884901888 | tf_op jit(solution)/shard_map/pallas_call | solution.py:51
  190.7 10.9 %shard_map.196.refs_0_ = f32[8,1,512,2048]{3,2,1,0:T(8,128)} custom-call(s32[1]{0:T(128)} %get-tuple-element.162.place_ref, bf16[512,3072]{1,0:T(8,128)(2,1)} %collective-permute-done.1.left_ref, bf16[2048,3072]{1,0:T(8,128)(2,1)S(1)} %copy-done.1, f32[8,1,512,2048]{3,2,1,0:T(8,128)} %shard_map.194.refs_0_), custom_call_target="tpu_custom_call", output_to_operand_aliasing={{}: (3, {})} | custom-call | flops 12884901888 | tf_op jit(solution)/shard_map/pallas_call | solution.py:51
  201.6 10.8 %shard_map.197.refs_0_ = f32[8,1,512,2048]{3,2,1,0:T(8,128)} custom-call(s32[1]{0:T(128)} %get-tuple-element.163.place_ref, bf16[512,3072]{1,0:T(8,128)(2,1)} %collective-permute-done.left_ref, bf16[2048,3072]{1,0:T(8,128)(2,1)S(1)} %copy-done.1, f32[8,1,512,2048]{3,2,1,0:T(8,128)} %shard_map.195.refs_0_), custom_call_target="tpu_custom_call", output_to_operand_aliasing={{}: (3, {})} | custom-call | flops 12884901888 | tf_op jit(solution)/shard_map/pallas_call | solution.py:51
  212.3 10.9 %shard_map.198.refs_0_ = f32[8,1,512,2048]{3,2,1,0:T(8,128)} custom-call(s32[1]{0:T(128)} %get-tuple-element.162.place_ref, bf16[512,3072]{1,0:T(8,128)(2,1)} %collective-permute-done.3.left_ref, bf16[2048,3072]{1,0:T(8,128)(2,1)S(1)} %copy-done.1, f32[8,1,512,2048]{3,2,1,0:T(8,128)} %shard_map.197.refs_0_), custom_call_target="tpu_custom_call", output_to_operand_aliasing={{}: (3, {})} | custom-call | flops 12884901888 | tf_op jit(solution)/shard_map/pallas_call | solution.py:51
  223.3 10.8 %shard_map.199.refs_0_ = f32[8,1,512,2048]{3,2,1,0:T(8,128)} custom-call(s32[1]{0:T(128)} %get-tuple-element.163.place_ref, bf16[512,3072]{1,0:T(8,128)(2,1)} %collective-permute-done.2.left_ref, bf16[2048,3072]{1,0:T(8,128)(2,1)S(1)} %copy-done.1, f32[8,1,512,2048]{3,2,1,0:T(8,128)} %shard_map.196.refs_0_), custom_call_target="tpu_custom_call", output_to_operand_aliasing={{}: (3, {})} | custom-call | flops 12884901888 | tf_op jit(solution)/shard_map/pallas_call | solution.py:51
  234.0 0.7 collective-permute-done.4.left_ref
  234.7 0.3 collective-permute-done.5.left_ref
  235.0 1.7 collective-permute-start.6
  236.7 0.3 collective-permute-start.7
  237.1 11.3 %shard_map.200.refs_0_ = f32[8,1,512,2048]{3,2,1,0:T(8,128)} custom-call(s32[1]{0:T(128)} %get-tuple-element.159.place_ref, bf16[512,3072]{1,0:T(8,128)(2,1)} %collective-permute-done.5.left_ref, bf16[2048,3072]{1,0:T(8,128)(2,1)S(1)} %copy-done.1, f32[8,1,512,2048]{3,2,1,0:T(8,128)} %shard_map.199.refs_0_), custom_call_target="tpu_custom_call", output_to_operand_aliasing={{}: (3, {})} | custom-call | flops 12884901888 | tf_op jit(solution)/shard_map/pallas_call | solution.py:51
  248.4 10.9 %shard_map.201.refs_0_ = f32[8,1,512,2048]{3,2,1,0:T(8,128)} custom-call(s32[1]{0:T(128)} %get-tuple-element.160.place_ref, bf16[512,3072]{1,0:T(8,128)(2,1)} %collective-permute-done.4.left_ref, bf16[2048,3072]{1,0:T(8,128)(2,1)S(1)} %copy-done.1, f32[8,1,512,2048]{3,2,1,0:T(8,128)} %shard_map.198.refs_0_), custom_call_target="tpu_custom_call", output_to_operand_aliasing={{}: (3, {})} | custom-call | flops 12884901888 | tf_op jit(solution)/shard_map/pallas_call | solution.py:51
  259.3 42.9 %collective-permute-done.8.left_ref = bf16[512,3072]{1,0:T(8,128)(2,1)} collective-permute-done((bf16[512,3072]{1,0:T(8,128)(2,1)}, bf16[512,3072]{1,0:T(8,128)(2,1)}, u32[]{:S(2)}, u32[]{:S(2)}) %collective-permute-start.8) | collective-permute-done | bytes 3145760 | tf_op jit(solution)/shard_map/ppermute | solution.py:123
  302.2 0.3 collective-permute-done.9.left_ref
  302.4 4.7 %copy-done.5 = bf16[2048,3072]{1,0:T(8,128)(2,1)S(1)} copy-done((bf16[2048,3072]{1,0:T(8,128)(2,1)S(1)}, bf16[2048,3072]{1,0:T(8,128)(2,1)}, u32[]{:S(2)}) %copy-start.5) | copy-done | bytes 12582936
  307.2 10.1 %shard_map.202 = bf16[512,2048]{1,0:T(8,128)(2,1)} custom-call(s32[1]{0:T(128)} %constant.89.clone.1.place_ref, bf16[512,3072]{1,0:T(8,128)(2,1)} %collective-permute-done.9.left_ref, bf16[2048,3072]{1,0:T(8,128)(2,1)S(1)} %copy-done.5), custom_call_target="tpu_custom_call" | custom-call | tf_op jit(solution)/shard_map/pallas_call | solution.py:51
  317.2 1.7 collective-permute-start.12
  319.0 4.6 copy-done.2
  323.6 10.8 %shard_map.203.refs_0_ = f32[8,1,512,2048]{3,2,1,0:T(8,128)} custom-call(s32[1]{0:T(128)} %get-tuple-element.159.place_ref, bf16[512,3072]{1,0:T(8,128)(2,1)} %collective-permute-done.9.left_ref, bf16[2048,3072]{1,0:T(8,128)(2,1)S(1)} %copy-done.2, f32[8,1,512,2048]{3,2,1,0:T(8,128)} %shard_map.201.refs_0_), custom_call_target="tpu_custom_call", output_to_operand_aliasing={{}: (3, {})} | custom-call | flops 12884901888 | tf_op jit(solution)/shard_map/pallas_call | solution.py:51
  334.4 10.9 %shard_map.204.refs_0_ = f32[8,1,512,2048]{3,2,1,0:T(8,128)} custom-call(s32[1]{0:T(128)} %get-tuple-element.160.place_ref, bf16[512,3072]{1,0:T(8,128)(2,1)} %collective-permute-done.8.left_ref, bf16[2048,3072]{1,0:T(8,128)(2,1)S(1)} %copy-done.2, f32[8,1,512,2048]{3,2,1,0:T(8,128)} %shard_map.200.refs_0_), custom_call_target="tpu_custom_call", output_to_operand_aliasing={{}: (3, {})} | custom-call | flops 12884901888 | tf_op jit(solution)/shard_map/pallas_call | solution.py:51
  345.3 4.6 copy-done.3
  349.9 10.0 %shard_map.205 = bf16[512,2048]{1,0:T(8,128)(2,1)} custom-call(s32[1]{0:T(128)} %constant.89.clone.1.place_ref, bf16[512,3072]{1,0:T(8,128)(2,1)} %collective-permute-done.8.left_ref, bf16[2048,3072]{1,0:T(8,128)(2,1)S(1)} %copy-done.3), custom_call_target="tpu_custom_call" | custom-call | tf_op jit(solution)/shard_map/pallas_call | solution.py:51
  359.9 0.3 collective-permute-start.13
  360.2 9.3 %collective-permute-done.6.left_ref = bf16[512,3072]{1,0:T(8,128)(2,1)S(1)} collective-permute-done((bf16[512,3072]{1,0:T(8,128)(2,1)}, bf16[512,3072]{1,0:T(8,128)(2,1)S(1)}, u32[]{:S(2)}, u32[]{:S(2)}) %collective-permute-start.6) | collective-permute-done | bytes 3145760 | tf_op jit(solution)/shard_map/ppermute | solution.py:123
  369.5 0.4 collective-permute-done.7.left_ref
  369.9 4.6 copy-done.6
  374.4 10.0 %shard_map.206 = (bf16[384,2048]{1,0:T(8,128)(2,1)}, bf16[128,2048]{1,0:T(8,128)(2,1)S(1)}) custom-call(s32[1]{0:T(128)} %constant.89.clone.1.place_ref, bf16[512,3072]{1,0:T(8,128)(2,1)} %collective-permute-done.7.left_ref, bf16[2048,3072]{1,0:T(8,128)(2,1)S(1)} %copy-done.6), custom_call_target="tpu_custom_call" | custom-call | tf_op jit(solution)/shard_map/pallas_call | solution.py:51
  384.4 1.7 collective-permute-start.14
  386.2 4.6 copy-done.4
  390.8 6.5 %shard_map.207 = bf16[384,2048]{1,0:T(8,128)(2,1)} custom-call(s32[1]{0:T(128)} %constant.89.clone.1.place_ref, bf16[512,3072]{1,0:T(8,128)(2,1)S(1)} %collective-permute-done.6.left_ref, bf16[2048,3072]{1,0:T(8,128)(2,1)S(1)} %copy-done.4), custom_call_target="tpu_custom_call" | custom-call | tf_op jit(solution)/shard_map/pallas_call | solution.py:51
  397.3 0.3 collective-permute-start.11
  397.6 4.8 %shard_map.208 = bf16[128,2048]{1,0:T(8,128)(2,1)S(1)} custom-call(s32[1]{0:T(128)} %constant.89.clone.1.place_ref, bf16[512,3072]{1,0:T(8,128)(2,1)S(1)} %collective-permute-done.6.left_ref, bf16[2048,3072]{1,0:T(8,128)(2,1)S(1)} %copy-done.4), custom_call_target="tpu_custom_call" | custom-call | tf_op jit(solution)/shard_map/pallas_call | solution.py:51
  402.3 2.0 collective-permute-start.10
  404.3 10.8 %shard_map.209 = f32[8,1,512,2048]{3,2,1,0:T(8,128)} custom-call(s32[1]{0:T(128)} %get-tuple-element.161.place_ref, bf16[512,3072]{1,0:T(8,128)(2,1)} %collective-permute-done.7.left_ref, bf16[2048,3072]{1,0:T(8,128)(2,1)S(1)} %bitcast.32, f32[8,1,512,2048]{3,2,1,0:T(8,128)} %shard_map.204.refs_0_), custom_call_target="tpu_custom_call", output_to_operand_aliasing={{}: (3, {})} | custom-call | flops 12884901888 | tf_op jit(solution)/shard_map/pallas_call | solution.py:51
  415.1 9.0 %shard_map.210 = f32[8,1,512,2048]{3,2,1,0:T(8,128)} custom-call(s32[1]{0:T(128)} %get-tuple-element.164.place_ref, bf16[512,3072]{1,0:T(8,128)(2,1)S(1)} %collective-permute-done.6.left_ref, bf16[2048,3072]{1,0:T(8,128)(2,1)S(1)} %bitcast.32, f32[8,1,512,2048]{3,2,1,0:T(8,128)} %shard_map.203.refs_0_), custom_call_target="tpu_custom_call", output_to_operand_aliasing={{}: (3, {})} | custom-call | flops 12884901888 | tf_op jit(solution)/shard_map/pallas_call | solution.py:51
  424.1 0.3 collective-permute-start.15
  424.4 4.1 convert_dynamic-update-slice_fusion.1
  428.5 2.6 convert_dynamic-update-slice_fusion
  431.1 17.4 %collective-permute-done.14 = bf16[384,2048]{1,0:T(8,128)(2,1)} collective-permute-done((bf16[384,2048]{1,0:T(8,128)(2,1)}, bf16[384,2048]{1,0:T(8,128)(2,1)}, u32[]{:S(2)}, u32[]{:S(2)}) %collective-permute-start.14) | collective-permute-done | bytes 1572896 | tf_op jit(solution)/shard_map/ppermute | solution.py:132
  448.5 3.4 convert_dynamic-update-slice_fusion.3
  451.9 2.1 convert_dynamic-update-slice_fusion.2
  454.0 3.3 collective-permute-done.15
  457.3 1.1 convert_dynamic-update-slice_fusion.5
  458.4 1.1 convert_dynamic-update-slice_fusion.4
  (30 shorter events, 0.1 us)
Async XLA Ops:
  7.2 160.3 %all-gather.4.cloned.1.call-start = ((), (), s32[]{:S(2)}) async-start(), calls=%async_computation | async-start | bytes 15728640 | tf_op jit(solution)/shard_map/all_gather | solution.py:108
  7.9 141.2 %copy-start.9 = (s32[8]{0:T(128)S(1)}, s32[8]{0:T(128)}, u32[]{:S(2)}) copy-start(s32[8]{0:T(128)} %constant.104.clone) | copy-start | bytes 100
  7.9 147.2 %copy-start.8 = (s32[8]{0:T(128)S(1)}, s32[8]{0:T(128)}, u32[]{:S(2)}) copy-start(s32[8]{0:T(128)} %constant.105.clone) | copy-start | bytes 100
  7.9 159.5 %copy-start.7 = (bf16[512,3072]{1,0:T(8,128)(2,1)S(1)}, bf16[512,3072]{1,0:T(8,128)(2,1)}, u32[]{:S(2)}) copy-start(bf16[512,3072]{1,0:T(8,128)(2,1)} %left_ref) | copy-start | bytes 9437188
  7.9 294.5 %all-gather.6.cloned.1.call-start = ((), (), s32[]{:S(2)}) async-start(), calls=%async_computation.1 | async-start | bytes 15728640 | tf_op jit(solution)/shard_map/all_gather | solution.py:108
  8.0 72.3 %collective-permute-start.1 = (bf16[512,3072]{1,0:T(8,128)(2,1)}, bf16[512,3072]{1,0:T(8,128)(2,1)}, u32[]{:S(2)}, u32[]{:S(2)}) collective-permute-start(bf16[512,3072]{1,0:T(8,128)(2,1)} %left_ref), channel_id=1, source_target_pairs={{0,8},{8,16},{16,24},{24,28},{28,20},{20,12},{12,4},{4,0},{1,9},{9... | collective-permute-start | bytes 9437192 | tf_op jit(solution)/shard_map/ppermute | solution.py:123
  11.1 71.3 %collective-permute-start.2 = (bf16[512,3072]{1,0:T(8,128)(2,1)}, bf16[512,3072]{1,0:T(8,128)(2,1)}, u32[]{:S(2)}, u32[]{:S(2)}) collective-permute-start(bf16[512,3072]{1,0:T(8,128)(2,1)} %left_ref), channel_id=1, source_target_pairs={{8,0},{16,8},{24,16},{28,24},{20,28},{12,20},{4,12},{0,4},{9,1},{1... | collective-permute-start | bytes 9437192 | tf_op jit(solution)/shard_map/ppermute | solution.py:123
  16.7 131.6 %collective-permute-start = (bf16[512,3072]{1,0:T(8,128)(2,1)}, bf16[512,3072]{1,0:T(8,128)(2,1)}, u32[]{:S(2)}, u32[]{:S(2)}) collective-permute-start(bf16[512,3072]{1,0:T(8,128)(2,1)} %subtract_convert_fusion.left_ref), channel_id=1, source_target_pairs={{8,0},{16,8},{24,16},{28,24},{20,28},{12,20},{4,12},{0,4},{9,1},{1... | collective-permute-start | bytes 9437192 | tf_op jit(solution)/shard_map/ppermute | solution.py:123
  18.7 129.7 %collective-permute-start.3 = (bf16[512,3072]{1,0:T(8,128)(2,1)}, bf16[512,3072]{1,0:T(8,128)(2,1)}, u32[]{:S(2)}, u32[]{:S(2)}) collective-permute-start(bf16[512,3072]{1,0:T(8,128)(2,1)} %subtract_convert_fusion.left_ref), channel_id=1, source_target_pairs={{0,8},{8,16},{16,24},{24,28},{28,20},{20,12},{12,4},{4,0},{1,9},{9... | collective-permute-start | bytes 9437192 | tf_op jit(solution)/shard_map/ppermute | solution.py:123
  148.4 196.9 %all-gather.8.cloned.1.call-start = ((), (), s32[]{:S(2)}) async-start(), calls=%async_computation.2 | async-start | bytes 15728640 | tf_op jit(solution)/shard_map/all_gather | solution.py:108
  163.3 71.4 %collective-permute-start.4 = (bf16[512,3072]{1,0:T(8,128)(2,1)}, bf16[512,3072]{1,0:T(8,128)(2,1)}, u32[]{:S(2)}, u32[]{:S(2)}) collective-permute-start(bf16[512,3072]{1,0:T(8,128)(2,1)} %collective-permute-done.left_ref), channel_id=1, source_target_pairs={{8,0},{16,8},{24,16},{28,24},{20,28},{12,20},{4,12},{0,4},{9,1},{1... | collective-permute-start | bytes 9437192 | tf_op jit(solution)/shard_map/ppermute | solution.py:123
  163.7 71.4 %collective-permute-start.5 = (bf16[512,3072]{1,0:T(8,128)(2,1)}, bf16[512,3072]{1,0:T(8,128)(2,1)}, u32[]{:S(2)}, u32[]{:S(2)}) collective-permute-start(bf16[512,3072]{1,0:T(8,128)(2,1)} %collective-permute-done.1.left_ref), channel_id=1, source_target_pairs={{0,8},{8,16},{16,24},{24,28},{28,20},{20,12},{12,4},{4,0},{1,9},{9... | collective-permute-start | bytes 9437192 | tf_op jit(solution)/shard_map/ppermute | solution.py:123
  165.4 136.7 %collective-permute-start.8 = (bf16[512,3072]{1,0:T(8,128)(2,1)}, bf16[512,3072]{1,0:T(8,128)(2,1)}, u32[]{:S(2)}, u32[]{:S(2)}) collective-permute-start(bf16[512,3072]{1,0:T(8,128)(2,1)} %collective-permute-done.2.left_ref), channel_id=1, source_target_pairs={{8,0},{16,8},{24,16},{28,24},{20,28},{12,20},{4,12},{0,4},{9,1},{1... | collective-permute-start | bytes 9437192 | tf_op jit(solution)/shard_map/ppermute | solution.py:123
  165.7 136.7 %collective-permute-start.9 = (bf16[512,3072]{1,0:T(8,128)(2,1)}, bf16[512,3072]{1,0:T(8,128)(2,1)}, u32[]{:S(2)}, u32[]{:S(2)}) collective-permute-start(bf16[512,3072]{1,0:T(8,128)(2,1)} %collective-permute-done.3.left_ref), channel_id=1, source_target_pairs={{0,8},{8,16},{16,24},{24,28},{28,20},{20,12},{12,4},{4,0},{1,9},{9... | collective-permute-start | bytes 9437192 | tf_op jit(solution)/shard_map/ppermute | solution.py:123
  167.4 4.7 %copy-start = (bf16[2048,3072]{1,0:T(8,128)(2,1)S(1)}, bf16[2048,3072]{1,0:T(8,128)(2,1)}, u32[]{:S(2)}) copy-start(bf16[2048,3072]{1,0:T(8,128)(2,1)} %all-gather.4.cloned.1.call-done.right_ref) | copy-start | bytes 37748740
  172.2 8.3 %copy-start.1 = (bf16[2048,3072]{1,0:T(8,128)(2,1)S(1)}, bf16[2048,3072]{1,0:T(8,128)(2,1)}, u32[]{:S(2)}) copy-start(bf16[2048,3072]{1,0:T(8,128)(2,1)} %all-gather.4.cloned.1.call-done.right_ref) | copy-start | bytes 37748740
  235.0 134.4 %collective-permute-start.6 = (bf16[512,3072]{1,0:T(8,128)(2,1)}, bf16[512,3072]{1,0:T(8,128)(2,1)S(1)}, u32[]{:S(2)}, u32[]{:S(2)}) collective-permute-start(bf16[512,3072]{1,0:T(8,128)(2,1)} %collective-permute-done.4.left_ref), channel_id=1, source_target_pairs={{8,0},{16,8},{24,16},{28,24},{20,28},{12,20},{4,12},{0,4},{9,1},{1... | collective-permute-start | bytes 9437192 | tf_op jit(solution)/shard_map/ppermute | solution.py:123
  236.7 133.1 %collective-permute-start.7 = (bf16[512,3072]{1,0:T(8,128)(2,1)}, bf16[512,3072]{1,0:T(8,128)(2,1)}, u32[]{:S(2)}, u32[]{:S(2)}) collective-permute-start(bf16[512,3072]{1,0:T(8,128)(2,1)} %collective-permute-done.5.left_ref), channel_id=1, source_target_pairs={{0,8},{8,16},{16,24},{24,28},{28,20},{20,12},{12,4},{4,0},{1,9},{9... | collective-permute-start | bytes 9437192 | tf_op jit(solution)/shard_map/ppermute | solution.py:123
  302.4 4.7 %copy-start.5 = (bf16[2048,3072]{1,0:T(8,128)(2,1)S(1)}, bf16[2048,3072]{1,0:T(8,128)(2,1)}, u32[]{:S(2)}) copy-start(bf16[2048,3072]{1,0:T(8,128)(2,1)} %all-gather.6.cloned.1.call-done.right_ref) | copy-start | bytes 37748740
  317.2 106.8 %collective-permute-start.12 = (bf16[512,2048]{1,0:T(8,128)(2,1)}, bf16[512,2048]{1,0:T(8,128)(2,1)}, u32[]{:S(2)}, u32[]{:S(2)}) collective-permute-start(bf16[512,2048]{1,0:T(8,128)(2,1)} %shard_map.202), channel_id=1, source_target_pairs={{0,8},{8,16},{16,24},{24,28},{28,20},{20,12},{12,4},{4,0},{1,9},{9... | collective-permute-start | bytes 6291464 | tf_op jit(solution)/shard_map/ppermute | solution.py:132
  319.0 4.6 copy-start.2
  345.3 4.6 copy-start.3
  359.9 68.6 %collective-permute-start.13 = (bf16[512,2048]{1,0:T(8,128)(2,1)}, bf16[512,2048]{1,0:T(8,128)(2,1)S(1)}, u32[]{:S(2)}, u32[]{:S(2)}) collective-permute-start(bf16[512,2048]{1,0:T(8,128)(2,1)} %shard_map.205), channel_id=1, source_target_pairs={{8,0},{16,8},{24,16},{28,24},{20,28},{12,20},{4,12},{0,4},{9,1},{1... | collective-permute-start | bytes 6291464 | tf_op jit(solution)/shard_map/ppermute | solution.py:132
  369.8 4.6 copy-start.6
  384.4 64.1 %collective-permute-start.14 = (bf16[384,2048]{1,0:T(8,128)(2,1)}, bf16[384,2048]{1,0:T(8,128)(2,1)}, u32[]{:S(2)}, u32[]{:S(2)}) collective-permute-start(bf16[384,2048]{1,0:T(8,128)(2,1)} %get-tuple-element.132), channel_id=1, source_target_pairs={{0,8},{8,16},{16,24},{24,28},{28,20},{20,12},{12,4},{4,0},{1,9},{9... | collective-permute-start | bytes 4718600 | tf_op jit(solution)/shard_map/ppermute | solution.py:132
  386.2 4.6 copy-start.4
  390.7 13.6 %slice-start = ((s8[12582912]{0:T(1024)(128)(4,1)}), s8[4194304]{0:T(1024)(128)(4,1)S(1)}, s32[]{:S(2)}) async-start(s8[12582912]{0:T(1024)(128)(4,1)} %bitcast.31), calls=%async_computation.3 | async-start | bytes 8388608
  390.7 13.6 %slice-start.1 = ((s8[12582912]{0:T(1024)(128)(4,1)}), s8[4194304]{0:T(1024)(128)(4,1)S(1)}, s32[]{:S(2)}) async-start(s8[12582912]{0:T(1024)(128)(4,1)} %bitcast.31), calls=%async_computation.4 | async-start | bytes 8388608
  397.3 7.0 %slice-start.2 = ((s8[12582912]{0:T(1024)(128)(4,1)}), s8[4194304]{0:T(1024)(128)(4,1)S(1)}, s32[]{:S(2)}) async-start(s8[12582912]{0:T(1024)(128)(4,1)} %bitcast.31), calls=%async_computation.5 | async-start | bytes 8388608
  397.3 54.7 %collective-permute-start.11 = (bf16[384,2048]{1,0:T(8,128)(2,1)}, bf16[384,2048]{1,0:T(8,128)(2,1)S(1)}, u32[]{:S(2)}, u32[]{:S(2)}) collective-permute-start(bf16[384,2048]{1,0:T(8,128)(2,1)} %shard_map.207), channel_id=1, source_target_pairs={{8,0},{16,8},{24,16},{28,24},{20,28},{12,20},{4,12},{0,4},{9,1},{1... | collective-permute-start | bytes 4718600 | tf_op jit(solution)/shard_map/ppermute | solution.py:132
  402.3 56.0 %collective-permute-start.10 = (bf16[128,2048]{1,0:T(8,128)(2,1)S(1)}, bf16[128,2048]{1,0:T(8,128)(2,1)S(1)}, u32[]{:S(2)}, u32[]{:S(2)}) collective-permute-start(bf16[128,2048]{1,0:T(8,128)(2,1)S(1)} %shard_map.208), channel_id=1, source_target_pairs={{8,0},{16,8},{24,16},{28,24},{20,28},{12,20},{4,12},{0,4},{9,1},{1... | collective-permute-start | bytes 1572872 | tf_op jit(solution)/shard_map/ppermute | solution.py:132
  424.1 33.2 %collective-permute-start.15 = (bf16[128,2048]{1,0:T(8,128)(2,1)S(1)}, bf16[128,2048]{1,0:T(8,128)(2,1)S(1)}, u32[]{:S(2)}, u32[]{:S(2)}) collective-permute-start(bf16[128,2048]{1,0:T(8,128)(2,1)S(1)} %get-tuple-element.133), channel_id=1, source_target_pairs={{0,8},{8,16},{16,24},{24,28},{28,20},{20,12},{12,4},{4,0},{1,9},{9... | collective-permute-start | bytes 1572872 | tf_op jit(solution)/shard_map/ppermute | solution.py:132
Sparse Core Ops, SparseCore 0:
  9.6 84.7 all-gather.3
  148.5 82.3 all-gather.5
  232.4 82.1 all-gather.7

commit v9 on v7

--- a/solution.py
+++ b/solution.py
@@ -58,7 +58,7 @@
             out_specs=out_specs,
         ),
         input_output_aliases=aliases,
-        compiler_params=pltpu.CompilerParams(vmem_limit_bytes=48 * 1024 * 1024),
+        compiler_params=pltpu.CompilerParams(vmem_limit_bytes=32 * 1024 * 1024),
         cost_estimate=pl.CostEstimate(flops=0, bytes_accessed=0, transcendentals=0),
     )(*operands)
 

time: 454 us -> 453 us (level)
  local copies, waits for them, and re-layouts: 2.08 us -> 31.8 us
  Pallas kernels: 196 us -> 167 us
    unnamed x10 -> x30, local copies, waits for them, and re-layouts: 0.81 us -> 30.5 us
    pallas_call x17, Pallas kernels: 196 us -> 167 us  [product(): pl.pallas_call(functools.partial(product_kernel, 1.0 / tokens, len(shapes...]
  transfers between devices with their start and end apart: 19 -> 19, of which waited for: 9 -> 9; matrix products, arithmetic and copies ran while one was open for 5% -> 5% of each run, Pallas kernels for 43% -> 37%
where the time goes in v9:
time: 453 us; the launch traced here: 452 us
  waiting for transfers between devices  187 us (41%)
  Pallas kernels  167 us (37%)
  local copies, waits for them, and re-layouts  31.8 us (7%)
  between operations  27.1 us (6%)
  other arithmetic  21.5 us (5%)
  starting transfers between devices  17.7 us (4%)
    ppermute x10, waiting for transfers between devices, start(): at[chain].append(lax.ppermute(block, 'wide', pairs[chain[1]]))  175 us
    pallas_call x17, Pallas kernels, product(): pl.pallas_call(functools.partial(product_kernel, 1.0 / tokens, len(shapes...  167 us
    unnamed x30, local copies, waits for them, and re-layouts  30.5 us
    dynamic_update_slice x6, other arithmetic, put_arrived(): lax.dynamic_update_slice(outs[which], tie(block).astype(jnp.float32)[None...  15.9 us
    ppermute x10, starting transfers between devices, start(): at[chain].append(lax.ppermute(block, 'wide', pairs[chain[1]]))  11.2 us
    ppermute x6, waiting for transfers between devices, send(): moved = lax.ppermute(part, 'wide', pairs[way])  10.2 us
  transfers between devices with their start and end apart: 19, of which 9 were waited for; matrix products, arithmetic and copies ran while one was open for 5% of the time, Pallas kernels for 37%

profile of v9, /device:TPU:0, one launch (start us, length us, event | category | flops | bytes accessed | tf_op | source)
XLA Modules:
  0.0 451.8 jit_solution(1986489382735469978)
XLA Ops:
  7.2 0.0 all-gather.4.cloned.1.call-start
  7.2 0.7 all-gather.4.cloned.1.call-update
  7.9 0.0 all-gather.6.cloned.1.call-start
  8.0 3.1 collective-permute-start.1
  11.1 0.0 collective-permute-start.2
  11.1 5.6 %subtract_convert_fusion.left_ref = bf16[512,3072]{1,0:T(8,128)(2,1)} fusion(bf16[512,3072]{1,0:T(8,128)(2,1)} %left_ref, bf16[512,3072]{1,0:T(8,128)(2,1)} %param.20), kind=kLoop, calls=%fused_computation | loop fusion | flops 6291456 | bytes 9437184 | tf_op jit(solution)/shard_map/convert_element_type | solution.py:107
  16.7 2.0 collective-permute-start
  18.6 0.1 collective-permute-start.3
  18.7 61.5 %collective-permute-done.1.left_ref = bf16[512,3072]{1,0:T(8,128)(2,1)} collective-permute-done((bf16[512,3072]{1,0:T(8,128)(2,1)}, bf16[512,3072]{1,0:T(8,128)(2,1)}, u32[]{:S(2)}, u32[]{:S(2)}) %collective-permute-start.1) | collective-permute-done | bytes 3145760 | tf_op jit(solution)/shard_map/ppermute | solution.py:119
  80.2 2.2 collective-permute-done.2.left_ref
  82.4 65.9 %collective-permute-done.left_ref = bf16[512,3072]{1,0:T(8,128)(2,1)} collective-permute-done((bf16[512,3072]{1,0:T(8,128)(2,1)}, bf16[512,3072]{1,0:T(8,128)(2,1)}, u32[]{:S(2)}, u32[]{:S(2)}) %collective-permute-start) | collective-permute-done | bytes 3145760 | tf_op jit(solution)/shard_map/ppermute | solution.py:119
  148.3 0.0 all-gather.6.cloned.1.call-update
  148.4 0.0 all-gather.8.cloned.1.call-start
  148.4 0.7 all-gather.8.cloned.1.call-update
  149.1 0.4 collective-permute-start.4
  149.5 1.7 collective-permute-start.5
  151.2 0.3 collective-permute-start.8
  151.5 1.7 collective-permute-start.9
  153.2 0.6 dynamic_slice.51
  159.2 0.7 fusion
  159.9 6.5 %copy-done = bf16[2048,3072]{1,0:T(8,128)(2,1)S(1)} copy-done((bf16[2048,3072]{1,0:T(8,128)(2,1)S(1)}, bf16[2048,3072]{1,0:T(8,128)(2,1)}, u32[]{:S(2)}) %copy-start) | copy-done | bytes 12582936
  166.5 8.3 %shard_map.194.refs_0_ = f32[8,1,512,2048]{3,2,1,0:T(8,128)} custom-call(s32[1]{0:T(128)} %bitcast.2.place_ref, bf16[512,3072]{1,0:T(8,128)(2,1)S(1)} %copy-done.7, bf16[2048,3072]{1,0:T(8,128)(2,1)S(1)} %copy-done), custom_call_target="tpu_custom_call" | custom-call | tf_op jit(solution)/shard_map/pallas_call | solution.py:51
  174.8 10.2 %shard_map.195.refs_0_ = f32[8,1,512,2048]{3,2,1,0:T(8,128)} custom-call(s32[1]{0:T(128)} %bitcast.2.place_ref, bf16[512,3072]{1,0:T(8,128)(2,1)} %subtract_convert_fusion.left_ref, bf16[2048,3072]{1,0:T(8,128)(2,1)S(1)} %copy-done.1), custom_call_target="tpu_custom_call" | custom-call | tf_op jit(solution)/shard_map/pallas_call | solution.py:51
  185.0 10.9 %shard_map.196.refs_0_ = f32[8,1,512,2048]{3,2,1,0:T(8,128)} custom-call(s32[1]{0:T(128)} %get-tuple-element.162.place_ref, bf16[512,3072]{1,0:T(8,128)(2,1)} %collective-permute-done.1.left_ref, bf16[2048,3072]{1,0:T(8,128)(2,1)S(1)} %copy-done.1, f32[8,1,512,2048]{3,2,1,0:T(8,128)} %shard_map.194.refs_0_), custom_call_target="tpu_custom_call", output_to_operand_aliasing={{}: (3, {})} | custom-call | tf_op jit(solution)/shard_map/pallas_call | solution.py:51
  195.9 10.8 %shard_map.197.refs_0_ = f32[8,1,512,2048]{3,2,1,0:T(8,128)} custom-call(s32[1]{0:T(128)} %get-tuple-element.163.place_ref, bf16[512,3072]{1,0:T(8,128)(2,1)} %collective-permute-done.left_ref, bf16[2048,3072]{1,0:T(8,128)(2,1)S(1)} %copy-done.1, f32[8,1,512,2048]{3,2,1,0:T(8,128)} %shard_map.195.refs_0_), custom_call_target="tpu_custom_call", output_to_operand_aliasing={{}: (3, {})} | custom-call | tf_op jit(solution)/shard_map/pallas_call | solution.py:51
  206.7 10.9 %shard_map.198.refs_0_ = f32[8,1,512,2048]{3,2,1,0:T(8,128)} custom-call(s32[1]{0:T(128)} %get-tuple-element.162.place_ref, bf16[512,3072]{1,0:T(8,128)(2,1)} %collective-permute-done.3.left_ref, bf16[2048,3072]{1,0:T(8,128)(2,1)S(1)} %copy-done.1, f32[8,1,512,2048]{3,2,1,0:T(8,128)} %shard_map.197.refs_0_), custom_call_target="tpu_custom_call", output_to_operand_aliasing={{}: (3, {})} | custom-call | tf_op jit(solution)/shard_map/pallas_call | solution.py:51
  217.6 10.8 %shard_map.199.refs_0_ = f32[8,1,512,2048]{3,2,1,0:T(8,128)} custom-call(s32[1]{0:T(128)} %get-tuple-element.163.place_ref, bf16[512,3072]{1,0:T(8,128)(2,1)} %collective-permute-done.2.left_ref, bf16[2048,3072]{1,0:T(8,128)(2,1)S(1)} %copy-done.1, f32[8,1,512,2048]{3,2,1,0:T(8,128)} %shard_map.196.refs_0_), custom_call_target="tpu_custom_call", output_to_operand_aliasing={{}: (3, {})} | custom-call | tf_op jit(solution)/shard_map/pallas_call | solution.py:51
  228.5 0.9 collective-permute-start.6
  229.4 1.1 collective-permute-start.7
  230.5 10.8 %shard_map.200.refs_0_ = f32[8,1,512,2048]{3,2,1,0:T(8,128)} custom-call(s32[1]{0:T(128)} %get-tuple-element.159.place_ref, bf16[512,3072]{1,0:T(8,128)(2,1)} %collective-permute-done.5.left_ref, bf16[2048,3072]{1,0:T(8,128)(2,1)S(1)} %copy-done.1, f32[8,1,512,2048]{3,2,1,0:T(8,128)} %shard_map.199.refs_0_), custom_call_target="tpu_custom_call", output_to_operand_aliasing={{}: (3, {})} | custom-call | tf_op jit(solution)/shard_map/pallas_call | solution.py:51
  241.3 11.4 %shard_map.201.refs_0_ = f32[8,1,512,2048]{3,2,1,0:T(8,128)} custom-call(s32[1]{0:T(128)} %get-tuple-element.160.place_ref, bf16[512,3072]{1,0:T(8,128)(2,1)} %collective-permute-done.4.left_ref, bf16[2048,3072]{1,0:T(8,128)(2,1)S(1)} %copy-done.1, f32[8,1,512,2048]{3,2,1,0:T(8,128)} %shard_map.198.refs_0_), custom_call_target="tpu_custom_call", output_to_operand_aliasing={{}: (3, {})} | custom-call | tf_op jit(solution)/shard_map/pallas_call | solution.py:51
  252.7 35.2 %collective-permute-done.8.left_ref = bf16[512,3072]{1,0:T(8,128)(2,1)} collective-permute-done((bf16[512,3072]{1,0:T(8,128)(2,1)}, bf16[512,3072]{1,0:T(8,128)(2,1)}, u32[]{:S(2)}, u32[]{:S(2)}) %collective-permute-start.8) | collective-permute-done | bytes 3145760 | tf_op jit(solution)/shard_map/ppermute | solution.py:119
  287.9 0.3 collective-permute-done.9.left_ref
  288.2 4.6 %copy-done.5 = bf16[2048,3072]{1,0:T(8,128)(2,1)S(1)} copy-done((bf16[2048,3072]{1,0:T(8,128)(2,1)S(1)}, bf16[2048,3072]{1,0:T(8,128)(2,1)}, u32[]{:S(2)}) %copy-start.5) | copy-done | bytes 12582936
  292.9 10.0 %shard_map.202 = bf16[512,2048]{1,0:T(8,128)(2,1)} custom-call(s32[1]{0:T(128)} %constant.89.clone.1.place_ref, bf16[512,3072]{1,0:T(8,128)(2,1)} %collective-permute-done.9.left_ref, bf16[2048,3072]{1,0:T(8,128)(2,1)S(1)} %copy-done.5), custom_call_target="tpu_custom_call" | custom-call | tf_op jit(solution)/shard_map/pallas_call | solution.py:51
  302.9 1.7 collective-permute-start.12
  304.6 4.7 %copy-done.2 = bf16[2048,3072]{1,0:T(8,128)(2,1)S(1)} copy-done((bf16[2048,3072]{1,0:T(8,128)(2,1)S(1)}, bf16[2048,3072]{1,0:T(8,128)(2,1)}, u32[]{:S(2)}) %copy-start.2) | copy-done | bytes 12582936
  309.3 10.8 %shard_map.203.refs_0_ = f32[8,1,512,2048]{3,2,1,0:T(8,128)} custom-call(s32[1]{0:T(128)} %get-tuple-element.159.place_ref, bf16[512,3072]{1,0:T(8,128)(2,1)} %collective-permute-done.9.left_ref, bf16[2048,3072]{1,0:T(8,128)(2,1)S(1)} %copy-done.2, f32[8,1,512,2048]{3,2,1,0:T(8,128)} %shard_map.201.refs_0_), custom_call_target="tpu_custom_call", output_to_operand_aliasing={{}: (3, {})} | custom-call | tf_op jit(solution)/shard_map/pallas_call | solution.py:51
  320.1 10.9 %shard_map.204.refs_0_ = f32[8,1,512,2048]{3,2,1,0:T(8,128)} custom-call(s32[1]{0:T(128)} %get-tuple-element.160.place_ref, bf16[512,3072]{1,0:T(8,128)(2,1)} %collective-permute-done.8.left_ref, bf16[2048,3072]{1,0:T(8,128)(2,1)S(1)} %copy-done.2, f32[8,1,512,2048]{3,2,1,0:T(8,128)} %shard_map.200.refs_0_), custom_call_target="tpu_custom_call", output_to_operand_aliasing={{}: (3, {})} | custom-call | tf_op jit(solution)/shard_map/pallas_call | solution.py:51
  331.0 4.6 %copy-done.3 = bf16[2048,3072]{1,0:T(8,128)(2,1)S(1)} copy-done((bf16[2048,3072]{1,0:T(8,128)(2,1)S(1)}, bf16[2048,3072]{1,0:T(8,128)(2,1)}, u32[]{:S(2)}) %copy-start.3) | copy-done | bytes 12582936
  335.5 10.0 %shard_map.210 = bf16[512,2048]{1,0:T(8,128)(2,1)} custom-call(s32[1]{0:T(128)} %constant.89.clone.1.place_ref, bf16[512,3072]{1,0:T(8,128)(2,1)} %collective-permute-done.8.left_ref, bf16[2048,3072]{1,0:T(8,128)(2,1)S(1)} %copy-done.3), custom_call_target="tpu_custom_call" | custom-call | tf_op jit(solution)/shard_map/pallas_call | solution.py:51
  345.6 0.4 collective-permute-start.13
  345.9 9.3 %collective-permute-done.6.left_ref = bf16[512,3072]{1,0:T(8,128)(2,1)S(1)} collective-permute-done((bf16[512,3072]{1,0:T(8,128)(2,1)}, bf16[512,3072]{1,0:T(8,128)(2,1)S(1)}, u32[]{:S(2)}, u32[]{:S(2)}) %collective-permute-start.6) | collective-permute-done | bytes 3145760 | tf_op jit(solution)/shard_map/ppermute | solution.py:119
  355.2 0.4 collective-permute-done.7.left_ref
  355.7 4.6 %copy-done.6 = bf16[2048,3072]{1,0:T(8,128)(2,1)S(1)} copy-done((bf16[2048,3072]{1,0:T(8,128)(2,1)S(1)}, bf16[2048,3072]{1,0:T(8,128)(2,1)}, u32[]{:S(2)}) %copy-start.6) | copy-done | bytes 12582936
  360.2 10.0 %shard_map.205 = (bf16[384,2048]{1,0:T(8,128)(2,1)}, bf16[128,2048]{1,0:T(8,128)(2,1)S(1)}) custom-call(s32[1]{0:T(128)} %constant.89.clone.1.place_ref, bf16[512,3072]{1,0:T(8,128)(2,1)} %collective-permute-done.7.left_ref, bf16[2048,3072]{1,0:T(8,128)(2,1)S(1)} %copy-done.6), custom_call_target="tpu_custom_call" | custom-call | tf_op jit(solution)/shard_map/pallas_call | solution.py:51
  370.3 0.8 copy-done.8
  371.1 1.7 collective-permute-start.14
  380.7 4.6 %copy-done.4 = bf16[2048,3072]{1,0:T(8,128)(2,1)S(1)} copy-done((bf16[2048,3072]{1,0:T(8,128)(2,1)S(1)}, bf16[2048,3072]{1,0:T(8,128)(2,1)}, u32[]{:S(2)}) %copy-start.4) | copy-done | bytes 12582936
  385.2 6.5 %shard_map.206 = bf16[384,2048]{1,0:T(8,128)(2,1)} custom-call(s32[1]{0:T(128)} %constant.89.clone.1.place_ref, bf16[512,3072]{1,0:T(8,128)(2,1)S(1)} %collective-permute-done.6.left_ref, bf16[2048,3072]{1,0:T(8,128)(2,1)S(1)} %copy-done.4), custom_call_target="tpu_custom_call" | custom-call | tf_op jit(solution)/shard_map/pallas_call | solution.py:51
  391.8 0.3 collective-permute-start.11
  392.1 4.8 %shard_map.207 = bf16[128,2048]{1,0:T(8,128)(2,1)S(1)} custom-call(s32[1]{0:T(128)} %constant.89.clone.1.place_ref, bf16[512,3072]{1,0:T(8,128)(2,1)S(1)} %collective-permute-done.6.left_ref, bf16[2048,3072]{1,0:T(8,128)(2,1)S(1)} %copy-done.4), custom_call_target="tpu_custom_call" | custom-call | tf_op jit(solution)/shard_map/pallas_call | solution.py:51
  396.9 1.9 collective-permute-start.10
  398.8 10.9 %shard_map.208 = f32[8,1,512,2048]{3,2,1,0:T(8,128)} custom-call(s32[1]{0:T(128)} %get-tuple-element.161.place_ref, bf16[512,3072]{1,0:T(8,128)(2,1)} %collective-permute-done.7.left_ref, bf16[2048,3072]{1,0:T(8,128)(2,1)S(1)} %bitcast.32, f32[8,1,512,2048]{3,2,1,0:T(8,128)} %shard_map.204.refs_0_), custom_call_target="tpu_custom_call", output_to_operand_aliasing={{}: (3, {})} | custom-call | tf_op jit(solution)/shard_map/pallas_call | solution.py:51
  409.7 9.1 %shard_map.209 = f32[8,1,512,2048]{3,2,1,0:T(8,128)} custom-call(s32[1]{0:T(128)} %get-tuple-element.164.place_ref, bf16[512,3072]{1,0:T(8,128)(2,1)S(1)} %collective-permute-done.6.left_ref, bf16[2048,3072]{1,0:T(8,128)(2,1)S(1)} %bitcast.32, f32[8,1,512,2048]{3,2,1,0:T(8,128)} %shard_map.203.refs_0_), custom_call_target="tpu_custom_call", output_to_operand_aliasing={{}: (3, {})} | custom-call | tf_op jit(solution)/shard_map/pallas_call | solution.py:51
  418.7 0.4 collective-permute-start.15
  419.1 4.1 convert_dynamic-update-slice_fusion.1
  423.2 4.1 convert_dynamic-update-slice_fusion
  427.4 6.9 %collective-permute-done.14 = bf16[384,2048]{1,0:T(8,128)(2,1)} collective-permute-done((bf16[384,2048]{1,0:T(8,128)(2,1)}, bf16[384,2048]{1,0:T(8,128)(2,1)}, u32[]{:S(2)}, u32[]{:S(2)}) %collective-permute-start.14) | collective-permute-done | bytes 1572896 | tf_op jit(solution)/shard_map/ppermute | solution.py:128
  434.3 3.4 convert_dynamic-update-slice_fusion.3
  437.8 2.0 convert_dynamic-update-slice_fusion.2
  439.8 3.3 collective-permute-done.15
  443.1 1.1 convert_dynamic-update-slice_fusion.5
  444.2 1.1 convert_dynamic-update-slice_fusion.4
  (34 shorter events, 0.1 us)
Async XLA Ops:
  7.2 152.7 %all-gather.4.cloned.1.call-start = ((), (), s32[]{:S(2)}) async-start(), calls=%async_computation | async-start | bytes 15728640 | tf_op jit(solution)/shard_map/all_gather | solution.py:104
  7.9 145.3 %copy-start.11 = (s32[8]{0:T(128)S(1)}, s32[8]{0:T(128)}, u32[]{:S(2)}) copy-start(s32[8]{0:T(128)} %constant.104.clone) | copy-start | bytes 100
  7.9 151.3 %copy-start.10 = (s32[8]{0:T(128)S(1)}, s32[8]{0:T(128)}, u32[]{:S(2)}) copy-start(s32[8]{0:T(128)} %constant.105.clone) | copy-start | bytes 100
  7.9 152.0 %copy-start.7 = (bf16[512,3072]{1,0:T(8,128)(2,1)S(1)}, bf16[512,3072]{1,0:T(8,128)(2,1)}, u32[]{:S(2)}) copy-start(bf16[512,3072]{1,0:T(8,128)(2,1)} %left_ref) | copy-start | bytes 9437188
  7.9 280.3 %all-gather.6.cloned.1.call-start = ((), (), s32[]{:S(2)}) async-start(), calls=%async_computation.1 | async-start | bytes 15728640 | tf_op jit(solution)/shard_map/all_gather | solution.py:104
  8.0 72.3 %collective-permute-start.1 = (bf16[512,3072]{1,0:T(8,128)(2,1)}, bf16[512,3072]{1,0:T(8,128)(2,1)}, u32[]{:S(2)}, u32[]{:S(2)}) collective-permute-start(bf16[512,3072]{1,0:T(8,128)(2,1)} %left_ref), channel_id=1, source_target_pairs={{0,8},{8,16},{16,24},{24,28},{28,20},{20,12},{12,4},{4,0},{1,9},{9... | collective-permute-start | bytes 9437192 | tf_op jit(solution)/shard_map/ppermute | solution.py:119
  11.1 71.3 %collective-permute-start.2 = (bf16[512,3072]{1,0:T(8,128)(2,1)}, bf16[512,3072]{1,0:T(8,128)(2,1)}, u32[]{:S(2)}, u32[]{:S(2)}) collective-permute-start(bf16[512,3072]{1,0:T(8,128)(2,1)} %left_ref), channel_id=1, source_target_pairs={{8,0},{16,8},{24,16},{28,24},{20,28},{12,20},{4,12},{0,4},{9,1},{1... | collective-permute-start | bytes 9437192 | tf_op jit(solution)/shard_map/ppermute | solution.py:119
  16.7 131.7 %collective-permute-start = (bf16[512,3072]{1,0:T(8,128)(2,1)}, bf16[512,3072]{1,0:T(8,128)(2,1)}, u32[]{:S(2)}, u32[]{:S(2)}) collective-permute-start(bf16[512,3072]{1,0:T(8,128)(2,1)} %subtract_convert_fusion.left_ref), channel_id=1, source_target_pairs={{8,0},{16,8},{24,16},{28,24},{20,28},{12,20},{4,12},{0,4},{9,1},{1... | collective-permute-start | bytes 9437192 | tf_op jit(solution)/shard_map/ppermute | solution.py:119
  18.6 129.7 %collective-permute-start.3 = (bf16[512,3072]{1,0:T(8,128)(2,1)}, bf16[512,3072]{1,0:T(8,128)(2,1)}, u32[]{:S(2)}, u32[]{:S(2)}) collective-permute-start(bf16[512,3072]{1,0:T(8,128)(2,1)} %subtract_convert_fusion.left_ref), channel_id=1, source_target_pairs={{0,8},{8,16},{16,24},{24,28},{28,20},{20,12},{12,4},{4,0},{1,9},{9... | collective-permute-start | bytes 9437192 | tf_op jit(solution)/shard_map/ppermute | solution.py:119
  148.4 182.6 %all-gather.8.cloned.1.call-start = ((), (), s32[]{:S(2)}) async-start(), calls=%async_computation.2 | async-start | bytes 15728640 | tf_op jit(solution)/shard_map/all_gather | solution.py:104
  149.1 79.4 %collective-permute-start.4 = (bf16[512,3072]{1,0:T(8,128)(2,1)}, bf16[512,3072]{1,0:T(8,128)(2,1)}, u32[]{:S(2)}, u32[]{:S(2)}) collective-permute-start(bf16[512,3072]{1,0:T(8,128)(2,1)} %collective-permute-done.left_ref), channel_id=1, source_target_pairs={{8,0},{16,8},{24,16},{28,24},{20,28},{12,20},{4,12},{0,4},{9,1},{1... | collective-permute-start | bytes 9437192 | tf_op jit(solution)/shard_map/ppermute | solution.py:119
  149.5 79.0 %collective-permute-start.5 = (bf16[512,3072]{1,0:T(8,128)(2,1)}, bf16[512,3072]{1,0:T(8,128)(2,1)}, u32[]{:S(2)}, u32[]{:S(2)}) collective-permute-start(bf16[512,3072]{1,0:T(8,128)(2,1)} %collective-permute-done.1.left_ref), channel_id=1, source_target_pairs={{0,8},{8,16},{16,24},{24,28},{28,20},{20,12},{12,4},{4,0},{1,9},{9... | collective-permute-start | bytes 9437192 | tf_op jit(solution)/shard_map/ppermute | solution.py:119
  151.2 136.7 %collective-permute-start.8 = (bf16[512,3072]{1,0:T(8,128)(2,1)}, bf16[512,3072]{1,0:T(8,128)(2,1)}, u32[]{:S(2)}, u32[]{:S(2)}) collective-permute-start(bf16[512,3072]{1,0:T(8,128)(2,1)} %collective-permute-done.2.left_ref), channel_id=1, source_target_pairs={{8,0},{16,8},{24,16},{28,24},{20,28},{12,20},{4,12},{0,4},{9,1},{1... | collective-permute-start | bytes 9437192 | tf_op jit(solution)/shard_map/ppermute | solution.py:119
  151.5 136.7 %collective-permute-start.9 = (bf16[512,3072]{1,0:T(8,128)(2,1)}, bf16[512,3072]{1,0:T(8,128)(2,1)}, u32[]{:S(2)}, u32[]{:S(2)}) collective-permute-start(bf16[512,3072]{1,0:T(8,128)(2,1)} %collective-permute-done.3.left_ref), channel_id=1, source_target_pairs={{0,8},{8,16},{16,24},{24,28},{28,20},{20,12},{12,4},{4,0},{1,9},{9... | collective-permute-start | bytes 9437192 | tf_op jit(solution)/shard_map/ppermute | solution.py:119
  159.9 6.5 %copy-start = (bf16[2048,3072]{1,0:T(8,128)(2,1)S(1)}, bf16[2048,3072]{1,0:T(8,128)(2,1)}, u32[]{:S(2)}) copy-start(bf16[2048,3072]{1,0:T(8,128)(2,1)} %all-gather.4.cloned.1.call-done.right_ref) | copy-start | bytes 37748740
  166.5 8.3 %copy-start.1 = (bf16[2048,3072]{1,0:T(8,128)(2,1)S(1)}, bf16[2048,3072]{1,0:T(8,128)(2,1)}, u32[]{:S(2)}) copy-start(bf16[2048,3072]{1,0:T(8,128)(2,1)} %all-gather.4.cloned.1.call-done.right_ref) | copy-start | bytes 37748740
  228.5 126.8 %collective-permute-start.6 = (bf16[512,3072]{1,0:T(8,128)(2,1)}, bf16[512,3072]{1,0:T(8,128)(2,1)S(1)}, u32[]{:S(2)}, u32[]{:S(2)}) collective-permute-start(bf16[512,3072]{1,0:T(8,128)(2,1)} %collective-permute-done.4.left_ref), channel_id=1, source_target_pairs={{8,0},{16,8},{24,16},{28,24},{20,28},{12,20},{4,12},{0,4},{9,1},{1... | collective-permute-start | bytes 9437192 | tf_op jit(solution)/shard_map/ppermute | solution.py:119
  229.4 126.3 %collective-permute-start.7 = (bf16[512,3072]{1,0:T(8,128)(2,1)}, bf16[512,3072]{1,0:T(8,128)(2,1)}, u32[]{:S(2)}, u32[]{:S(2)}) collective-permute-start(bf16[512,3072]{1,0:T(8,128)(2,1)} %collective-permute-done.5.left_ref), channel_id=1, source_target_pairs={{0,8},{8,16},{16,24},{24,28},{28,20},{20,12},{12,4},{4,0},{1,9},{9... | collective-permute-start | bytes 9437192 | tf_op jit(solution)/shard_map/ppermute | solution.py:119
  288.2 4.6 %copy-start.5 = (bf16[2048,3072]{1,0:T(8,128)(2,1)S(1)}, bf16[2048,3072]{1,0:T(8,128)(2,1)}, u32[]{:S(2)}) copy-start(bf16[2048,3072]{1,0:T(8,128)(2,1)} %all-gather.6.cloned.1.call-done.right_ref) | copy-start | bytes 37748740
  302.9 115.8 %collective-permute-start.12 = (bf16[512,2048]{1,0:T(8,128)(2,1)}, bf16[512,2048]{1,0:T(8,128)(2,1)}, u32[]{:S(2)}, u32[]{:S(2)}) collective-permute-start(bf16[512,2048]{1,0:T(8,128)(2,1)} %shard_map.202), channel_id=1, source_target_pairs={{0,8},{8,16},{16,24},{24,28},{28,20},{20,12},{12,4},{4,0},{1,9},{9... | collective-permute-start | bytes 6291464 | tf_op jit(solution)/shard_map/ppermute | solution.py:128
  304.6 4.7 %copy-start.2 = (bf16[2048,3072]{1,0:T(8,128)(2,1)S(1)}, bf16[2048,3072]{1,0:T(8,128)(2,1)}, u32[]{:S(2)}) copy-start(bf16[2048,3072]{1,0:T(8,128)(2,1)} %all-gather.4.cloned.1.call-done.right_ref) | copy-start | bytes 37748740
  331.0 4.6 %copy-start.3 = (bf16[2048,3072]{1,0:T(8,128)(2,1)S(1)}, bf16[2048,3072]{1,0:T(8,128)(2,1)}, u32[]{:S(2)}) copy-start(bf16[2048,3072]{1,0:T(8,128)(2,1)} %all-gather.8.cloned.1.call-done.right_ref) | copy-start | bytes 37748740
  345.6 77.7 %collective-permute-start.13 = (bf16[512,2048]{1,0:T(8,128)(2,1)}, bf16[512,2048]{1,0:T(8,128)(2,1)}, u32[]{:S(2)}, u32[]{:S(2)}) collective-permute-start(bf16[512,2048]{1,0:T(8,128)(2,1)} %shard_map.210), channel_id=1, source_target_pairs={{8,0},{16,8},{24,16},{28,24},{20,28},{12,20},{4,12},{0,4},{9,1},{1... | collective-permute-start | bytes 6291464 | tf_op jit(solution)/shard_map/ppermute | solution.py:128
  355.7 4.6 %copy-start.6 = (bf16[2048,3072]{1,0:T(8,128)(2,1)S(1)}, bf16[2048,3072]{1,0:T(8,128)(2,1)}, u32[]{:S(2)}) copy-start(bf16[2048,3072]{1,0:T(8,128)(2,1)} %all-gather.6.cloned.1.call-done.right_ref) | copy-start | bytes 37748740
  370.3 0.8 copy-start.8
  371.1 63.2 %collective-permute-start.14 = (bf16[384,2048]{1,0:T(8,128)(2,1)}, bf16[384,2048]{1,0:T(8,128)(2,1)}, u32[]{:S(2)}, u32[]{:S(2)}) collective-permute-start(bf16[384,2048]{1,0:T(8,128)(2,1)} %get-tuple-element.129), channel_id=1, source_target_pairs={{0,8},{8,16},{16,24},{24,28},{28,20},{20,12},{12,4},{4,0},{1,9},{9... | collective-permute-start | bytes 4718600 | tf_op jit(solution)/shard_map/ppermute | solution.py:128
  380.7 4.6 %copy-start.4 = (bf16[2048,3072]{1,0:T(8,128)(2,1)S(1)}, bf16[2048,3072]{1,0:T(8,128)(2,1)}, u32[]{:S(2)}) copy-start(bf16[2048,3072]{1,0:T(8,128)(2,1)} %all-gather.8.cloned.1.call-done.right_ref) | copy-start | bytes 37748740
  385.2 13.6 %slice-start = ((s8[12582912]{0:T(1024)(128)(4,1)}), s8[4194304]{0:T(1024)(128)(4,1)S(1)}, s32[]{:S(2)}) async-start(s8[12582912]{0:T(1024)(128)(4,1)} %bitcast.31), calls=%async_computation.3 | async-start | bytes 8388608
  385.2 13.6 %slice-start.1 = ((s8[12582912]{0:T(1024)(128)(4,1)}), s8[4194304]{0:T(1024)(128)(4,1)S(1)}, s32[]{:S(2)}) async-start(s8[12582912]{0:T(1024)(128)(4,1)} %bitcast.31), calls=%async_computation.4 | async-start | bytes 8388608
  391.8 7.0 %slice-start.2 = ((s8[12582912]{0:T(1024)(128)(4,1)}), s8[4194304]{0:T(1024)(128)(4,1)S(1)}, s32[]{:S(2)}) async-start(s8[12582912]{0:T(1024)(128)(4,1)} %bitcast.31), calls=%async_computation.5 | async-start | bytes 8388608
  391.8 46.0 %collective-permute-start.11 = (bf16[384,2048]{1,0:T(8,128)(2,1)}, bf16[384,2048]{1,0:T(8,128)(2,1)S(1)}, u32[]{:S(2)}, u32[]{:S(2)}) collective-permute-start(bf16[384,2048]{1,0:T(8,128)(2,1)} %shard_map.206), channel_id=1, source_target_pairs={{8,0},{16,8},{24,16},{28,24},{20,28},{12,20},{4,12},{0,4},{9,1},{1... | collective-permute-start | bytes 4718600 | tf_op jit(solution)/shard_map/ppermute | solution.py:128
  396.9 47.3 %collective-permute-start.10 = (bf16[128,2048]{1,0:T(8,128)(2,1)S(1)}, bf16[128,2048]{1,0:T(8,128)(2,1)S(1)}, u32[]{:S(2)}, u32[]{:S(2)}) collective-permute-start(bf16[128,2048]{1,0:T(8,128)(2,1)S(1)} %shard_map.207), channel_id=1, source_target_pairs={{8,0},{16,8},{24,16},{28,24},{20,28},{12,20},{4,12},{0,4},{9,1},{1... | collective-permute-start | bytes 1572872 | tf_op jit(solution)/shard_map/ppermute | solution.py:128
  409.7 9.1 %copy-start.9 = (bf16[128,2048]{1,0:T(8,128)(2,1)S(1)}, bf16[128,2048]{1,0:T(8,128)(2,1)}, u32[]{:S(2)}) copy-start(bf16[128,2048]{1,0:T(8,128)(2,1)} %copy-done.8) | copy-start | bytes 1572868
  418.7 24.4 %collective-permute-start.15 = (bf16[128,2048]{1,0:T(8,128)(2,1)S(1)}, bf16[128,2048]{1,0:T(8,128)(2,1)S(1)}, u32[]{:S(2)}, u32[]{:S(2)}) collective-permute-start(bf16[128,2048]{1,0:T(8,128)(2,1)S(1)} %copy-done.9), channel_id=1, source_target_pairs={{0,8},{8,16},{16,24},{24,28},{28,20},{20,12},{12,4},{4,0},{1,9},{9... | collective-permute-start | bytes 1572872 | tf_op jit(solution)/shard_map/ppermute | solution.py:128
Sparse Core Ops, SparseCore 0:
  9.6 84.7 all-gather.3
  148.5 82.3 all-gather.5
  232.4 82.0 all-gather.7
